TPU v7x, 512 devices: a whole 4x4x16 slice. The times are simulated.
512 devices in a mesh: seq: 64 (over z, x), head: 8 (over y, core).
Axes of the slice: x: 4, y: 4, z: 16, core: 2. Of those that a mesh axis runs over, the one named last changes fastest.
Arguments:
- queries: bfloat16 [8192, 4096], P('seq', 'head'), may hold values from -110 to 110
- keys: bfloat16 [8192, 1024], P('seq', 'head'), may hold values from -5 to 5
- values: bfloat16 [8192, 1024], P('seq', 'head'), may hold values from -24 to 24
- cache_keys: bfloat16 [8192, 1024], P('seq', 'head'), may hold values from -5 to 5
- cache_values: bfloat16 [8192, 1024], P('seq', 'head'), may hold values from -24 to 24
- spans: int32 [32], P('head'), may hold values from 128 to 16384, as said below
- out_weight: bfloat16 [4096, 4096], P('head'), may hold values from -0.09375 to 0.09375
Outputs:
- mixed_t: bfloat16 [4096, 8192], P('head', 'seq')
Inputs may be any that keep to these rules, and one draw needn't show every extreme that they name: In every group of 4 consecutive heads exactly 2 spans exceed 4 * 128; those lie between (16384) // 2 and 16384, the others between 128 and 512. All four ends are reached.
All inputs are finite; a program needn't handle non-finite values.
Results may differ from a plain program's by a relative error of at most 0.019.
Values may be sent and summed in bfloat16 or wider, within the bound.
No kernel may reach another device: no remote copies, remote signals or barrier semaphores. Data moves between devices by JAX's collectives and lax.ppermute only.
A program may use at most 128 MiB of HBM per device.

v0:
```python
import math

import jax
import jax.numpy as jnp
from jax import lax
from jax.sharding import PartitionSpec as P

REACH = 4


masked_score = -1e30


def shifted(block, axis, distance):
    devices = range(lax.axis_size(axis))
    route = [((i - distance) % len(devices), i) for i in devices]
    return lax.ppermute(block, axis, route)


def online_update(carry, query_rows, query_pos, span_rows, key_rows, value_rows, key_pos, scale):
    largest, weight_sum, accum = carry
    scores = jnp.dot(query_rows, key_rows.T, preferred_element_type=jnp.float32) * scale
    allowed = (key_pos[None, :] <= query_pos[:, None]) & (
        key_pos[None, :] > (query_pos - span_rows)[:, None]
    )
    masked = jnp.where(allowed, scores, masked_score)
    fresh = jnp.maximum(largest, jnp.max(masked, axis=1))
    weights = jnp.where(allowed, jnp.exp(masked - fresh[:, None]), 0.0)
    weight_sum = jnp.sum(weights, axis=1)
    accum = jnp.dot(weights.astype(jnp.bfloat16), value_rows, preferred_element_type=jnp.float32)
    return (fresh, weight_sum, accum)


def per_device(queries, keys, values, cache_keys, cache_values, spans, out_weight):
    rows_local = queries.shape[0]
    head_size = keys.shape[1]
    group_size = queries.shape[1] // head_size
    scale = 1.0 / math.sqrt(head_size)
    seq_index = lax.axis_index("seq")
    seq_count = lax.axis_size("seq")
    cache_len = rows_local * seq_count
    local_offsets = jnp.arange(rows_local, dtype=jnp.int32)
    query_pos = cache_len + seq_index * rows_local + local_offsets
    long_flag = (spans > REACH * rows_local).astype(jnp.int32)
    order = jnp.argsort(1 - long_flag, stable=True)
    head_queries = queries.reshape(rows_local, group_size, head_size).transpose(1, 0, 2)
    chosen_queries = jnp.take(head_queries, order, axis=0)
    chosen_spans = jnp.take(spans, order, axis=0)
    far_count = group_size // 2
    far_rows = chosen_queries[:far_count].reshape(far_count * rows_local, head_size)
    far_pos = jnp.tile(query_pos, far_count)
    far_spans = jnp.repeat(chosen_spans[:far_count], rows_local)
    far_init = (
        jnp.full((far_count * rows_local,), masked_score, jnp.float32),
        jnp.zeros((far_count * rows_local,), jnp.float32),
        jnp.zeros((far_count * rows_local, head_size), jnp.float32),
    )
    block_keys = lax.all_gather(cache_keys, "seq", axis=0, tiled=True)
    block_values = lax.all_gather(cache_values, "seq", axis=0, tiled=True)
    window_keys = lax.all_gather(keys, "seq", axis=0, tiled=True)
    window_values = lax.all_gather(values, "seq", axis=0, tiled=True)
    offsets = jnp.arange(block_keys.shape[0], dtype=jnp.int32)
    joined_keys = jnp.concatenate([block_keys, window_keys], axis=0)
    joined_values = jnp.concatenate([block_values, window_values], axis=0)
    joined_pos = jnp.concatenate([offsets, cache_len + offsets], axis=0)
    far_state = online_update(
        far_init, far_rows, far_pos, far_spans, joined_keys, joined_values, joined_pos, scale
    )
    far_out = (far_state[2] / far_state[1][:, None]).reshape(far_count, rows_local, head_size)
    near_count = group_size - far_count
    key_parts = []
    value_parts = []
    for back in range(REACH, 0, -1):
        wraps = seq_index >= seq_count - back
        send_keys = jnp.where(wraps, cache_keys, keys)
        send_values = jnp.where(wraps, cache_values, values)
        prior_keys, prior_values = shifted((send_keys, send_values), "seq", back)
        key_parts.append(prior_keys)
        value_parts.append(prior_values)
    near_keys = jnp.concatenate(key_parts + [keys], axis=0)
    near_values = jnp.concatenate(value_parts + [values], axis=0)
    near_key_pos = (
        cache_len
        + (seq_index - REACH) * rows_local
        + jnp.arange((REACH + 1) * rows_local, dtype=jnp.int32)
    )
    near_rows = chosen_queries[far_count:].reshape(near_count * rows_local, head_size)
    near_pos = jnp.tile(query_pos, near_count)
    near_spans = jnp.repeat(chosen_spans[far_count:], rows_local)
    near_init = (
        jnp.full((near_count * rows_local,), masked_score, jnp.float32),
        jnp.zeros((near_count * rows_local,), jnp.float32),
        jnp.zeros((near_count * rows_local, head_size), jnp.float32),
    )
    near_state = online_update(
        near_init, near_rows, near_pos, near_spans, near_keys, near_values, near_key_pos, scale
    )
    near_out = (near_state[2] / near_state[1][:, None]).reshape(near_count, rows_local, head_size)
    chosen_out = jnp.concatenate([far_out, near_out], axis=0)
    inverse = jnp.argsort(order, stable=True)
    heads_out = jnp.take(chosen_out, inverse, axis=0)
    attn = (
        heads_out.transpose(1, 0, 2)
        .reshape(rows_local, group_size * head_size)
        .astype(jnp.bfloat16)
    )
    return lax.psum_scatter(
        jnp.dot(attn, out_weight, preferred_element_type=jnp.float32).T.astype(jnp.bfloat16),
        "head",
        scatter_dimension=0,
        tiled=True,
    )


def solution(mesh):
    placed = (
        P("seq", "head"),
        P("seq", "head"),
        P("seq", "head"),
        P("seq", "head"),
        P("seq", "head"),
        P("head"),
        P("head", None),
    )
    return jax.shard_map(
        per_device, mesh=mesh, in_specs=placed, out_specs=P("head", "seq"), check_vma=False
    )
```

profile of v0, /device:TPU:1, one launch (start us, length us, event | category | flops | bytes accessed | tf_op | source)
XLA Modules:
  0.0 632.6 jit_solution(1732479795805882089)
XLA Ops:
  6.5 0.0 all-gather.5.cloned.1.call-start
  6.5 0.7 all-gather.5.cloned.1.call-update
  7.3 0.0 all-gather.7.cloned.1.call-start
  7.3 0.7 all-gather.7.cloned.1.call-update
  8.0 0.0 all-gather.11.cloned.1.call-start
  8.1 0.7 all-gather.11.cloned.1.call-update
  8.7 0.0 all-gather.9.cloned.1.call-start
  8.8 0.8 broadcast_select_fusion.2
  9.6 4.4 collective-permute-start
  14.0 4.4 collective-permute-start.1
  18.4 3.8 collective-permute-start.2
  22.2 2.5 collective-permute-start.3
  24.7 0.0 all-gather.9.cloned.1.call-update
  24.7 0.0 reduce-scatter.2.cloned.1.call-start
  24.8 0.8 broadcast_select_fusion.1
  25.6 3.5 collective-permute-start.4
  29.1 0.7 fusion.27
  29.8 0.7 sort.31
  30.5 0.7 sort.32
  31.3 1.3 gather_fusion
  32.6 0.1 fusion.33
  32.7 1.0 copy.10
  33.7 0.1 copy.11
  33.9 0.6 gather_fusion.1
  34.4 0.1 broadcast_select_fusion
  34.6 0.1 bitcast_subtract_fusion.1
  34.7 0.0 collective-permute-done
  34.7 6.5 %collective-permute-start.5 = (bf16[128,128]{1,0:T(8,128)(2,1)S(1)}, bf16[128,128]{1,0:T(8,128)(2,1)S(1)}, u32[]{:S(2)}, u32[]{:S(2)}) collective-permute-start(bf16[128,128]{1,0:T(8,128)(2,1)S(1)} %get-tuple-element.18), channel_id=1, source_target_pairs={{488,0},{496,8},{504,16},{0,24},{8,32},{16,40},{24,48},{32,56},{40... | collective-permute-start | bytes 98312 | tf_op jit(solution)/shard_map/ppermute | solution.py:17
  41.2 0.0 collective-permute-done.1
  41.3 3.1 collective-permute-start.6
  44.4 0.0 collective-permute-done.2
  44.4 2.2 collective-permute-start.7
  46.7 0.0 collective-permute-done.3
  46.7 0.8 constant_dynamic-update-slice_fusion
  47.5 0.0 collective-permute-done.4
  47.5 0.0 collective-permute-done.5
  47.5 2.0 collective-permute-done.6
  49.6 3.2 collective-permute-done.7
  52.7 0.8 constant_dynamic-update-slice_fusion.5
  53.5 0.4 fusion.34
  53.9 0.3 fusion.18
  54.2 0.3 convolution_divide_fusion
  54.6 93.3 %all-gather.5.cloned.1.call-done = bf16[8192,128]{1,0:T(8,128)(2,1)} async-done(((bf16[128,128]{1,0:T(8,128)(2,1)}), bf16[8192,128]{1,0:T(8,128)(2,1)}) %all-gather.5.cloned.1.call-update) | async-done | bytes 2097168 | tf_op jit(solution)/shard_map/all_gather | solution.py:58
  147.9 139.9 %all-gather.7.cloned.1.call-done = bf16[8192,128]{1,0:T(8,128)(2,1)} async-done(((bf16[128,128]{1,0:T(8,128)(2,1)}), bf16[8192,128]{1,0:T(8,128)(2,1)}) %all-gather.7.cloned.1.call-update) | async-done | bytes 2097168 | tf_op jit(solution)/shard_map/all_gather | solution.py:60
  287.8 7.1 %fusion.35 = (f32[256]{0:T(256)S(1)}, f32[256,16384]{1,0:T(8,128)S(1)}) fusion(bf16[256,128]{1,0:T(8,128)(2,1)S(1)} %bitcast.28, bf16[8192,128]{1,0:T(8,128)(2,1)} %all-gather.7.cloned.1.call-done, bf16[8192,128]{1,0:T(8,128)(2,1)} %all-gather.5.cloned.1.call-done, s32[256]{0:T(256)S(1)} %get-tuple-element.21, s32[256]{0:T(256)S(1)} %broadcast_bitcast_fusion, ...), kind=kOutput, calls=%fused_computation.78 | convolution fusion | flops 1107296000 | bytes 21105664 | tf_op jit(solution)/shard_map/dot_general | solution.py:22
  294.9 0.0 copy-start
  294.9 5.7 copy-done
  300.7 5.0 fusion.1
  305.6 122.1 %all-gather.11.cloned.1.call-done = bf16[8192,128]{1,0:T(8,128)(2,1)} async-done(((bf16[128,128]{1,0:T(8,128)(2,1)}), bf16[8192,128]{1,0:T(8,128)(2,1)}) %all-gather.11.cloned.1.call-update) | async-done | bytes 2097168 | tf_op jit(solution)/shard_map/all_gather | solution.py:61
  427.8 139.8 %all-gather.9.cloned.1.call-done = bf16[8192,128]{1,0:T(8,128)(2,1)} async-done(((bf16[128,128]{1,0:T(8,128)(2,1)}), bf16[8192,128]{1,0:T(8,128)(2,1)}) %all-gather.9.cloned.1.call-update) | async-done | bytes 2097168 | tf_op jit(solution)/shard_map/all_gather | solution.py:59
  567.5 9.2 %fusion.13 = bf16[256,128]{1,0:T(8,128)(2,1)S(1)} fusion(bf16[8192,128]{1,0:T(8,128)(2,1)} %all-gather.11.cloned.1.call-done, bf16[8192,128]{1,0:T(8,128)(2,1)} %all-gather.9.cloned.1.call-done, f32[256,16384]{1,0:T(8,128)} %copy-done, f32[256]{0:T(256)S(1)} %broadcast_maximum_fusion.1, s32[16384]{0:T(1024)S(1)} %pad_add_fusion, ...), kind=kOutput, calls=%fused_computation.21 | convolution fusion | flops 1107361792 | bytes 21106688 | tf_op jit(solution)/shard_map/dot_general | solution.py:30
  576.8 0.6 gather_fusion.2
  577.4 0.1 fusion.26
  577.5 0.1 copy.12
  577.6 3.9 fusion.5
  581.5 0.0 reduce-scatter.2.cloned.1.call-update
  581.5 42.9 %reduce-scatter.2.cloned.1.call-done = bf16[512,128]{0,1:T(8,128)(2,1)} async-done(((bf16[4096,128]{0,1:T(8,128)(2,1)}), bf16[512,128]{0,1:T(8,128)(2,1)}) %reduce-scatter.2.cloned.1.call-update) | async-done | bytes 131088 | tf_op jit(solution)/shard_map/reduce_scatter | solution.py:107
  624.4 1.7 copy.13
  (25 shorter events, 0.2 us)
Async XLA Ops:
  6.5 141.4 %all-gather.5.cloned.1.call-start = ((), (), s32[]{:S(2)}) async-start(), calls=%async_computation.1 | async-start | bytes 2129920 | tf_op jit(solution)/shard_map/all_gather | solution.py:58
  7.3 280.6 %all-gather.7.cloned.1.call-start = ((), (), s32[]{:S(2)}) async-start(), calls=%async_computation.2 | async-start | bytes 2129920 | tf_op jit(solution)/shard_map/all_gather | solution.py:60
  8.0 419.7 %all-gather.11.cloned.1.call-start = ((), (), s32[]{:S(2)}) async-start(), calls=%async_computation.4 | async-start | bytes 2129920 | tf_op jit(solution)/shard_map/all_gather | solution.py:61
  8.7 558.8 %all-gather.9.cloned.1.call-start = ((), (), s32[]{:S(2)}) async-start(), calls=%async_computation.3 | async-start | bytes 2129920 | tf_op jit(solution)/shard_map/all_gather | solution.py:59
  9.6 25.1 %collective-permute-start = (bf16[128,128]{1,0:T(8,128)(2,1)S(1)}, bf16[128,128]{1,0:T(8,128)(2,1)S(1)}, u32[]{:S(2)}, u32[]{:S(2)}) collective-permute-start(bf16[128,128]{1,0:T(8,128)(2,1)S(1)} %get-tuple-element.15), channel_id=1, source_target_pairs={{480,0},{488,8},{496,16},{504,24},{0,32},{8,40},{16,48},{24,56},{3... | collective-permute-start | bytes 98312 | tf_op jit(solution)/shard_map/ppermute | solution.py:17
  14.0 27.3 %collective-permute-start.1 = (bf16[128,128]{1,0:T(8,128)(2,1)S(1)}, bf16[128,128]{1,0:T(8,128)(2,1)S(1)}, u32[]{:S(2)}, u32[]{:S(2)}) collective-permute-start(bf16[128,128]{1,0:T(8,128)(2,1)S(1)} %get-tuple-element.14), channel_id=1, source_target_pairs={{488,0},{496,8},{504,16},{0,24},{8,32},{16,40},{24,48},{32,56},{40... | collective-permute-start | bytes 98312 | tf_op jit(solution)/shard_map/ppermute | solution.py:17
  18.4 26.1 %collective-permute-start.2 = (bf16[128,128]{1,0:T(8,128)(2,1)S(1)}, bf16[128,128]{1,0:T(8,128)(2,1)S(1)}, u32[]{:S(2)}, u32[]{:S(2)}) collective-permute-start(bf16[128,128]{1,0:T(8,128)(2,1)S(1)} %get-tuple-element.16), channel_id=1, source_target_pairs={{496,0},{504,8},{0,16},{8,24},{16,32},{24,40},{32,48},{40,56},{48,... | collective-permute-start | bytes 98312 | tf_op jit(solution)/shard_map/ppermute | solution.py:17
  22.2 24.5 %collective-permute-start.3 = (bf16[128,128]{1,0:T(8,128)(2,1)S(1)}, bf16[128,128]{1,0:T(8,128)(2,1)S(1)}, u32[]{:S(2)}, u32[]{:S(2)}) collective-permute-start(bf16[128,128]{1,0:T(8,128)(2,1)S(1)} %get-tuple-element.13), channel_id=1, source_target_pairs={{504,0},{0,8},{8,16},{16,24},{24,32},{32,40},{40,48},{48,56},{56,6... | collective-permute-start | bytes 98312 | tf_op jit(solution)/shard_map/ppermute | solution.py:17
  24.7 599.7 %reduce-scatter.2.cloned.1.call-start = ((), (), s32[]{:S(2)}) async-start(), calls=%async_computation.5 | async-start | bytes 1179648 | tf_op jit(solution)/shard_map/reduce_scatter | solution.py:107
  25.6 22.0 %collective-permute-start.4 = (bf16[128,128]{1,0:T(8,128)(2,1)S(1)}, bf16[128,128]{1,0:T(8,128)(2,1)S(1)}, u32[]{:S(2)}, u32[]{:S(2)}) collective-permute-start(bf16[128,128]{1,0:T(8,128)(2,1)S(1)} %get-tuple-element.19), channel_id=1, source_target_pairs={{480,0},{488,8},{496,16},{504,24},{0,32},{8,40},{16,48},{24,56},{3... | collective-permute-start | bytes 98312 | tf_op jit(solution)/shard_map/ppermute | solution.py:17
  34.7 12.8 %collective-permute-start.5 = (bf16[128,128]{1,0:T(8,128)(2,1)S(1)}, bf16[128,128]{1,0:T(8,128)(2,1)S(1)}, u32[]{:S(2)}, u32[]{:S(2)}) collective-permute-start(bf16[128,128]{1,0:T(8,128)(2,1)S(1)} %get-tuple-element.18), channel_id=1, source_target_pairs={{488,0},{496,8},{504,16},{0,24},{8,32},{16,40},{24,48},{32,56},{40... | collective-permute-start | bytes 98312 | tf_op jit(solution)/shard_map/ppermute | solution.py:17
  41.3 8.3 %collective-permute-start.6 = (bf16[128,128]{1,0:T(8,128)(2,1)S(1)}, bf16[128,128]{1,0:T(8,128)(2,1)S(1)}, u32[]{:S(2)}, u32[]{:S(2)}) collective-permute-start(bf16[128,128]{1,0:T(8,128)(2,1)S(1)} %get-tuple-element.20), channel_id=1, source_target_pairs={{496,0},{504,8},{0,16},{8,24},{16,32},{24,40},{32,48},{40,56},{48,... | collective-permute-start | bytes 98312 | tf_op jit(solution)/shard_map/ppermute | solution.py:17
  44.4 8.3 %collective-permute-start.7 = (bf16[128,128]{1,0:T(8,128)(2,1)S(1)}, bf16[128,128]{1,0:T(8,128)(2,1)S(1)}, u32[]{:S(2)}, u32[]{:S(2)}) collective-permute-start(bf16[128,128]{1,0:T(8,128)(2,1)S(1)} %get-tuple-element.17), channel_id=1, source_target_pairs={{504,0},{0,8},{8,16},{16,24},{24,32},{32,40},{40,48},{48,56},{56,6... | collective-permute-start | bytes 98312 | tf_op jit(solution)/shard_map/ppermute | solution.py:17
  294.9 5.7 copy-start
Sparse Core Ops, SparseCore 0:
  10.3 137.5 all-gather.4
  150.8 136.9 all-gather.6
  290.8 136.9 all-gather.10
  430.5 136.9 all-gather.8
  581.7 42.7 reduce-scatter.1
where the time goes:
time: 634 us; the launch traced here: 633 us
  waiting for transfers between devices  545 us (86%)
  starting transfers between devices  30.7 us (5%)
  matrix products  21 us (3%)
  between operations  13.4 us (2%)
  local copies, waits for them, and re-layouts  12.8 us (2%)
  other arithmetic  9.34 us (1%)
    all_gather x1, waiting for transfers between devices, per_device(): window_keys = lax.all_gather(keys, 'seq', axis=0, tiled=True)  140 us
    all_gather x1, waiting for transfers between devices, per_device(): block_values = lax.all_gather(cache_values, 'seq', axis=0, tiled=True)  140 us
    all_gather x1, waiting for transfers between devices, per_device(): window_values = lax.all_gather(values, 'seq', axis=0, tiled=True)  122 us
    all_gather x1, waiting for transfers between devices, per_device(): block_keys = lax.all_gather(cache_keys, 'seq', axis=0, tiled=True)  93.3 us
    reduce_scatter x1, waiting for transfers between devices, per_device(): lax.psum_scatter(jnp.dot(attn, out_weight, preferred_element_type=jnp.flo...  42.9 us
    ppermute x8, starting transfers between devices, shifted(): return lax.ppermute(block, axis, route)  30.5 us
  transfers between devices with their start and end apart: 13, of which 7 were waited for; matrix products, arithmetic and copies ran while one was open for 3% of the time, Pallas kernels for 0%

commit v1 on v0

v1 whole, which is shorter than its diff:
```python
import functools
import math

import jax
import jax.numpy as jnp
from jax import lax
from jax.experimental import pallas as pl
from jax.experimental.pallas import tpu as pltpu
from jax.sharding import Mesh
from jax.sharding import PartitionSpec as P

HD = 128
GROUP = 4
BLOCKS = 8
RING = 8
STATS = 16
PIECE = GROUP * HD + STATS
MASKED = -1e30
FLOOR = -1e29
FACTOR = math.log2(math.e) / math.sqrt(HD)
TILE = 256


def _scores(keys, rows):
    return lax.dot_general(
        keys, rows, (((1,), (1,)), ((), ())), preferred_element_type=jnp.float32
    )


def _weighted(values, weights):
    return lax.dot_general(
        values, weights, (((0,), (0,)), ((), ())), preferred_element_type=jnp.float32
    )


def _write_stats(stats, block, slot, top, total):
    level = jnp.where(total > 0.0, top * FACTOR + jnp.log2(total), MASKED)
    for i in range(3):
        term = level.astype(jnp.bfloat16).astype(jnp.float32)
        stats[block, pl.ds(slot * 4 + i, 1), :] = term
        level = level - term


def attention_kernel(info, queries, *refs):
    kv, (out, scores, stats) = refs[:-3], refs[-3:]
    blocks = []
    for i in range(RING - 1):
        blocks.append((kv[i], 0, True, i))
        blocks.append((kv[i], 2 * HD, False, i))
    blocks.append((kv[RING - 1], 0, True, RING - 1))
    blocks.append((kv[RING], 0, False, RING - 1))
    window = info[8 + RING]
    base = lax.broadcasted_iota(jnp.int32, (HD, TILE), 1) - lax.broadcasted_iota(
        jnp.int32, (HD, TILE), 0
    )
    stats[...] = jnp.zeros_like(stats)
    per = TILE // HD

    def far(step, _):
        slot = step // (BLOCKS // per)
        first = (step % (BLOCKS // per)) * per
        span = info[slot]
        position = info[4] + first * HD
        rows = queries[pl.ds(first, per), slot].reshape(TILE, HD)
        top = jnp.full((8, TILE), FLOOR, jnp.float32)
        for n, (ref, at, cached, i) in enumerate(blocks):
            found = _scores(ref[at : at + HD, :], rows)
            start = info[8 + i]
            if cached:
                allowed = base < span - position + start
            else:
                allowed = base >= start + window - position
            found = jnp.where(allowed, found, MASKED)
            scores[n * HD : (n + 1) * HD, :] = found
            top = jnp.maximum(top, jnp.max(found.reshape(HD // 8, 8, TILE), axis=0))
        top = jnp.max(top, axis=0, keepdims=True)
        total = jnp.zeros((8, TILE), jnp.float32)
        summed = jnp.zeros((HD, TILE), jnp.float32)
        for n, (ref, at, cached, i) in enumerate(blocks):
            weights = jnp.exp2((scores[n * HD : (n + 1) * HD, :] - top) * FACTOR)
            total = total + jnp.sum(weights.reshape(HD // 8, 8, TILE), axis=0)
            summed = summed + _weighted(
                ref[at + HD : at + 2 * HD, :], weights.astype(jnp.bfloat16)
            )
        total = jnp.sum(total, axis=0, keepdims=True)
        normal = summed * (1.0 / jnp.maximum(total, 1e-30))
        for j in range(per):
            cut = slice(j * HD, (j + 1) * HD)
            out[first + j, pl.ds(pl.multiple_of(slot * HD, HD), HD), :] = normal[:, cut].astype(
                jnp.bfloat16
            )
            _write_stats(stats, first + j, slot, top[:, cut], total[:, cut])
        return 0

    lax.fori_loop(0, 2 * BLOCKS // per, far, 0)

    own = info[6]
    near_base = base[:, :HD]

    def near(step, _):
        slot = 2 + step // BLOCKS
        block = step % BLOCKS
        span = info[slot]
        position = info[4] + block * HD
        rows = queries[block, slot]
        earlier = block < own
        wraps = info[5] == 1
        before = info[8 + 1] + jnp.where(wraps, 0, window)
        start = jnp.where(earlier, before, info[8] + window)
        at = pl.multiple_of(jnp.where(wraps, 0, 2 * HD), HD)
        key_rows = jnp.where(earlier, kv[1][pl.ds(at, HD), :], kv[0][2 * HD : 3 * HD, :])
        value_rows = jnp.where(earlier, kv[1][pl.ds(at + HD, HD), :], kv[0][3 * HD :, :])
        found = _scores(key_rows, rows)
        behind = near_base + (position - start)
        allowed = (behind >= 0) & (behind < span)
        found = jnp.where(allowed, found, MASKED)
        top = jnp.maximum(jnp.max(found, axis=0, keepdims=True), FLOOR)
        weights = jnp.exp2((found - top) * FACTOR)
        total = jnp.sum(weights, axis=0, keepdims=True)
        summed = _weighted(value_rows, weights.astype(jnp.bfloat16))
        normal = summed * (1.0 / jnp.maximum(total, 1e-30))
        out[block, pl.ds(pl.multiple_of(slot * HD, HD), HD), :] = normal.astype(jnp.bfloat16)
        _write_stats(stats, block, slot, top, total)
        return 0

    lax.fori_loop(0, 2 * BLOCKS, near, 0)
    out[:, GROUP * HD :, :] = stats[...].astype(jnp.bfloat16)


def attention(info, queries, kv):
    vmem = pl.BlockSpec(memory_space=pltpu.VMEM)
    return pl.pallas_call(
        attention_kernel,
        out_shape=jax.ShapeDtypeStruct((BLOCKS, PIECE, HD), jnp.bfloat16),
        in_specs=[pl.BlockSpec(memory_space=pltpu.SMEM), vmem] + [vmem] * len(kv),
        out_specs=vmem,
        scratch_shapes=[
            pltpu.VMEM((2 * RING * HD, TILE), jnp.float32),
            pltpu.VMEM((BLOCKS, STATS, HD), jnp.float32),
        ],
        compiler_params=pltpu.CompilerParams(vmem_limit_bytes=32 * 2**20),
        cost_estimate=pl.CostEstimate(
            flops=4 * 2048 * 2048 * 128, bytes_accessed=4 * 2**20, transcendentals=2048 * 2048
        ),
    )(info, queries, *kv)


def per_device(queries, keys, values, cache_keys, cache_values, spans, out_weight):
    rows = queries.shape[0]
    k, e, x = lax.axis_index("k"), lax.axis_index("e"), lax.axis_index("x")
    cache_len = rows * RING * BLOCKS
    far = (spans > 4 * rows).astype(jnp.int32)
    before = jnp.cumsum(far) - far
    rank = jnp.where(far == 1, before, 2 + jnp.arange(GROUP, dtype=jnp.int32) - before)
    slots = jnp.arange(GROUP, dtype=jnp.int32)
    order = jnp.sum(jnp.where(rank[None, :] == slots[:, None], slots[None, :], 0), axis=1)
    slot_spans = jnp.sum(jnp.where(rank[None, :] == slots[:, None], spans[None, :], 0), axis=1)

    heads = jnp.take(queries.reshape(rows, GROUP, HD).transpose(1, 0, 2), order, axis=0)
    sent = jnp.broadcast_to(heads[None], (BLOCKS,) + heads.shape)
    grouped = lax.all_to_all(sent, ("e", "x"), 0, 0, tiled=True)

    own = jnp.concatenate([cache_keys, cache_values, keys, values], axis=0)
    up_route = [(i, (i + 1) % RING) for i in range(RING)]
    down_route = [(i, (i - 1) % RING) for i in range(RING)]
    kv, up, down = [own], own, own
    for _ in range(RING // 2 - 1):
        up = lax.ppermute(up, "k", up_route)
        down = lax.ppermute(down, "k", down_route)
        kv += [up, down]
    kv.append(lax.ppermute(up[: 2 * rows], "k", up_route))
    kv.append(lax.ppermute(down[2 * rows :], "k", down_route))
    distances = [0, -1, 1, -2, 2, -3, 3, 4]
    starts = [(((k + d + RING) % RING * 2 + e) * 4 + x) * rows for d in distances]
    info = jnp.concatenate(
        [
            slot_spans,
            jnp.stack(
                [cache_len + k * (BLOCKS * rows), (k == 0).astype(jnp.int32), e * 4 + x, k * 0]
                + starts
                + [k * 0 + cache_len]
            ).astype(jnp.int32),
        ]
    )
    partial = attention(info, grouped, kv)
    parts = lax.all_to_all(partial, ("e", "x"), 0, 0, tiled=True)

    terms = parts[:, GROUP * HD :].reshape(BLOCKS, GROUP, 4, rows).astype(jnp.float32)
    level = terms[:, :, 0] + terms[:, :, 1] + terms[:, :, 2]
    share = jnp.exp2(level - jnp.max(level, axis=0, keepdims=True))
    share = share / jnp.sum(share, axis=0, keepdims=True)
    found = parts[:, : GROUP * HD].reshape(BLOCKS, GROUP, HD, rows).astype(jnp.float32)
    attn = jnp.sum(found * share[:, :, None, :], axis=0).astype(jnp.bfloat16)
    attn = jnp.take(attn, rank, axis=0).reshape(GROUP * HD, rows)
    product = lax.dot_general(
        out_weight, attn, (((0,), (0,)), ((), ())), preferred_element_type=jnp.float32
    ).astype(jnp.bfloat16)
    shares = lax.all_to_all(
        product.reshape(8, -1, rows), ("y", "c"), 0, 0, tiled=True
    )
    return jnp.sum(shares.astype(jnp.float32), axis=0).astype(jnp.bfloat16)


def solution(mesh):
    fine = Mesh(mesh.devices.reshape(RING, 2, 4, 4, 2), ("k", "e", "x", "y", "c"))
    seq, head = ("k", "e", "x"), ("y", "c")
    placed = (P(seq, head),) * 5 + (P(head), P(head, None))
    return jax.shard_map(
        per_device, mesh=fine, in_specs=placed, out_specs=P(head, seq), check_vma=False
    )
```

time: 634 us -> 132 us (0.21)
  waiting for transfers between devices: 545 us -> 28.3 us
  blocking collectives: 0 us -> 26.2 us
  Pallas kernels: 0 us -> 20.1 us
  matrix products: 21 us -> 2.93 us
  starting transfers between devices: 30.7 us -> 46.2 us
  between operations: 13.4 us -> 0.43 us
  local copies, waits for them, and re-layouts: 12.8 us -> 4.55 us
  other arithmetic: 9.34 us -> 2.97 us
    all_gather x4 -> x0, waiting for transfers between devices: 495 us -> none  [the longest x1 140 us: per_device(): window_keys = lax.all_gather(keys, 'seq', axis=0, tiled=True)]
    reduce_scatter x1 -> x0, waiting for transfers between devices: 42.9 us -> none  [per_device(): lax.psum_scatter(jnp.dot(attn, out_weight, preferred_element_type=jnp.flo...]
    all_to_all x0 -> x1, blocking collectives: none -> 26.2 us  [per_device(): lax.all_to_all(product.reshape(8, -1, rows), ('y', 'c'), 0, 0, tiled=True)]
    pallas_call x0 -> x1, Pallas kernels: none -> 20.1 us  [attention(): pl.pallas_call(attention_kernel, out_shape=jax.ShapeDtypeStruct((BLOCKS,...]
    dot_general x5 -> x1, matrix products: 21 us -> 2.93 us  [per_device(): lax.dot_general(out_weight, attn, (((0,), (0,)), ((), ())), preferred_ele...]
    ppermute x8, waiting for transfers between devices: 5.19 us -> 18.8 us  [the longest x3 17.5 us: per_device(): up = lax.ppermute(up, 'k', up_route)]
    all_to_all x0 -> x2, starting transfers between devices: none -> 9.76 us  [the longest x1 6.2 us: per_device(): grouped = lax.all_to_all(sent, ('e', 'x'), 0, 0, tiled=True)]
    all_to_all x0 -> x2, waiting for transfers between devices: none -> 9.51 us  [the longest x1 9.51 us: per_device(): parts = lax.all_to_all(partial, ('e', 'x'), 0, 0, tiled=True)]
  transfers between devices with their start and end apart: 13 -> 10, of which waited for: 7 -> 5; matrix products, arithmetic and copies ran while one was open for 3% -> 0% of each run, Pallas kernels for 0% -> 0%
where the time goes in v1:
time: 132 us
  starting transfers between devices  46.2 us (35%)
  waiting for transfers between devices  28.3 us (21%)
  blocking collectives  26.2 us (20%)
  Pallas kernels  20.1 us (15%)
  local copies, waits for them, and re-layouts  4.55 us (3%)
  other arithmetic  2.97 us (2%)
  matrix products  2.93 us (2%)
    all_to_all x1, blocking collectives, per_device(): lax.all_to_all(product.reshape(8, -1, rows), ('y', 'c'), 0, 0, tiled=True)  26.2 us
    pallas_call x1, Pallas kernels, attention(): pl.pallas_call(attention_kernel, out_shape=jax.ShapeDtypeStruct((BLOCKS,...  20.1 us
    ppermute x3, starting transfers between devices, per_device(): down = lax.ppermute(down, 'k', down_route)  19.9 us
    ppermute x3, waiting for transfers between devices, per_device(): up = lax.ppermute(up, 'k', up_route)  17.5 us
    all_to_all x1, waiting for transfers between devices, per_device(): parts = lax.all_to_all(partial, ('e', 'x'), 0, 0, tiled=True)  9.51 us
    ppermute x3, starting transfers between devices, per_device(): up = lax.ppermute(up, 'k', up_route)  8.72 us
    all_to_all x1, starting transfers between devices, per_device(): grouped = lax.all_to_all(sent, ('e', 'x'), 0, 0, tiled=True)  6.2 us
    ppermute x1, starting transfers between devices, per_device(): kv.append(lax.ppermute(down[2 * rows:], 'k', down_route))  5.87 us
  transfers between devices with their start and end apart: 10, of which 5 were waited for; matrix products, arithmetic and copies ran while one was open for 0% of the time, Pallas kernels for 0%

profile of v1, /device:TPU:1, one launch (start us, length us, event | category | flops | bytes accessed | tf_op | source)
XLA Modules:
  0.0 131.7 jit_solution(12004114220301650519)
XLA Ops:
  0.0 0.7 fusion.1
  0.7 0.2 reduce-window.9
  0.8 0.7 compare_and_fusion
  1.5 0.8 select_reduce_fusion
  2.3 1.0 copy.15
  3.4 0.0 copy-start
  3.4 0.0 copy-start.1
  3.4 0.0 copy-start.2
  3.4 0.0 copy-start.3
  3.4 0.1 copy.16
  3.6 0.6 gather_fusion
  4.1 0.1 broadcast_select_fusion.1
  4.2 1.2 broadcast_in_dim.45
  5.5 6.2 %all-to-all-start = ((bf16[8,4,128,128]{3,2,1,0:T(8,128)(2,1)}), bf16[8,4,128,128]{3,2,1,0:T(8,128)(2,1)S(1)}, u32[]{:S(2)}, u32[]{:S(2)}) async-start(bf16[8,4,128,128]{3,2,1,0:T(8,128)(2,1)} %broadcast_in_dim.45), calls=%async_computation | async-start | bytes 2097152 | tf_op jit(solution)/shard_map/all_to_all | solution.py:161
  11.7 0.0 copy-done
  11.7 0.0 copy-done.1
  11.7 0.0 copy-done.2
  11.7 0.0 copy-done.3
  11.7 4.9 %collective-permute-start = (bf16[512,128]{1,0:T(8,128)(2,1)S(1)}, bf16[512,128]{1,0:T(8,128)(2,1)S(1)}, u32[]{:S(2)}, u32[]{:S(2)}) collective-permute-start(bf16[512,128]{1,0:T(8,128)(2,1)S(1)} %constant_dynamic-update-slice_fusion.refs_0_), channel_id=1, source_target_pairs={{0,64},{64,128},{128,192},{192,256},{256,320},{320,384},{384,448},... | collective-permute-start | bytes 393224 | tf_op jit(solution)/shard_map/ppermute | solution.py:168
  16.7 7.7 %collective-permute-start.1 = (bf16[512,128]{1,0:T(8,128)(2,1)S(1)}, bf16[512,128]{1,0:T(8,128)(2,1)S(1)}, u32[]{:S(2)}, u32[]{:S(2)}) collective-permute-start(bf16[512,128]{1,0:T(8,128)(2,1)S(1)} %constant_dynamic-update-slice_fusion.refs_0_), channel_id=1, source_target_pairs={{0,448},{64,0},{128,64},{192,128},{256,192},{320,256},{384,320},{4... | collective-permute-start | bytes 393224 | tf_op jit(solution)/shard_map/ppermute | solution.py:169
  24.4 16.1 %collective-permute-done.refs_1_ = bf16[512,128]{1,0:T(8,128)(2,1)S(1)} collective-permute-done((bf16[512,128]{1,0:T(8,128)(2,1)S(1)}, bf16[512,128]{1,0:T(8,128)(2,1)S(1)}, u32[]{:S(2)}, u32[]{:S(2)}) %collective-permute-start) | collective-permute-done | bytes 131104 | tf_op jit(solution)/shard_map/ppermute | solution.py:168
  40.4 1.9 %collective-permute-start.2 = (bf16[512,128]{1,0:T(8,128)(2,1)S(1)}, bf16[512,128]{1,0:T(8,128)(2,1)S(1)}, u32[]{:S(2)}, u32[]{:S(2)}) collective-permute-start(bf16[512,128]{1,0:T(8,128)(2,1)S(1)} %collective-permute-done.refs_1_), channel_id=1, source_target_pairs={{0,64},{64,128},{128,192},{192,256},{256,320},{320,384},{384,448},... | collective-permute-start | bytes 393224 | tf_op jit(solution)/shard_map/ppermute | solution.py:168
  42.3 0.0 collective-permute-done.1.refs_2_
  42.3 5.5 %collective-permute-start.3 = (bf16[512,128]{1,0:T(8,128)(2,1)S(1)}, bf16[512,128]{1,0:T(8,128)(2,1)S(1)}, u32[]{:S(2)}, u32[]{:S(2)}) collective-permute-start(bf16[512,128]{1,0:T(8,128)(2,1)S(1)} %collective-permute-done.1.refs_2_), channel_id=1, source_target_pairs={{0,448},{64,0},{128,64},{192,128},{256,192},{320,256},{384,320},{4... | collective-permute-start | bytes 393224 | tf_op jit(solution)/shard_map/ppermute | solution.py:169
  47.8 1.4 %collective-permute-done.2.refs_3_ = bf16[512,128]{1,0:T(8,128)(2,1)S(1)} collective-permute-done((bf16[512,128]{1,0:T(8,128)(2,1)S(1)}, bf16[512,128]{1,0:T(8,128)(2,1)S(1)}, u32[]{:S(2)}, u32[]{:S(2)}) %collective-permute-start.2) | collective-permute-done | bytes 131104 | tf_op jit(solution)/shard_map/ppermute | solution.py:168
  49.3 1.9 %collective-permute-start.4 = (bf16[512,128]{1,0:T(8,128)(2,1)S(1)}, bf16[512,128]{1,0:T(8,128)(2,1)S(1)}, u32[]{:S(2)}, u32[]{:S(2)}) collective-permute-start(bf16[512,128]{1,0:T(8,128)(2,1)S(1)} %collective-permute-done.2.refs_3_), channel_id=1, source_target_pairs={{0,64},{64,128},{128,192},{192,256},{256,320},{320,384},{384,448},... | collective-permute-start | bytes 393224 | tf_op jit(solution)/shard_map/ppermute | solution.py:168
  51.2 0.2 collective-permute-done.3.refs_4_
  51.4 6.8 %collective-permute-start.5 = (bf16[512,128]{1,0:T(8,128)(2,1)S(1)}, bf16[512,128]{1,0:T(8,128)(2,1)S(1)}, u32[]{:S(2)}, u32[]{:S(2)}) collective-permute-start(bf16[512,128]{1,0:T(8,128)(2,1)S(1)} %collective-permute-done.3.refs_4_), channel_id=1, source_target_pairs={{0,448},{64,0},{128,64},{192,128},{256,192},{320,256},{384,320},{4... | collective-permute-start | bytes 393224 | tf_op jit(solution)/shard_map/ppermute | solution.py:169
  58.2 0.0 collective-permute-done.4.refs_5_
  58.2 1.9 %collective-permute-start.6 = (bf16[256,128]{1,0:T(8,128)(2,1)S(1)}, bf16[256,128]{1,0:T(8,128)(2,1)S(1)}, u32[]{:S(2)}, u32[]{:S(2)}) collective-permute-start(bf16[256,128]{1,0:T(8,128)(2,1)S(1)} %slice.32), channel_id=1, source_target_pairs={{0,64},{64,128},{128,192},{192,256},{256,320},{320,384},{384,448},... | collective-permute-start | bytes 196616 | tf_op jit(solution)/shard_map/ppermute | solution.py:171
  60.1 0.0 collective-permute-done.5.refs_6_
  60.1 5.9 %collective-permute-start.7 = (bf16[256,128]{1,0:T(8,128)(2,1)S(1)}, bf16[256,128]{1,0:T(8,128)(2,1)S(1)}, u32[]{:S(2)}, u32[]{:S(2)}) collective-permute-start(bf16[256,128]{1,0:T(8,128)(2,1)S(1)} %slice.33), channel_id=1, source_target_pairs={{0,448},{64,0},{128,64},{192,128},{256,192},{320,256},{384,320},{4... | collective-permute-start | bytes 196616 | tf_op jit(solution)/shard_map/ppermute | solution.py:172
  66.1 0.1 concatenate.6.info
  66.2 0.0 collective-permute-done.6.refs_7_
  66.2 1.1 collective-permute-done.7.refs_8_
  67.3 0.0 all-to-all-done.queries
  67.3 20.1 %shard_map.73 = bf16[8,528,128]{2,1,0:T(8,128)(2,1)} custom-call(s32[17]{0:T(128)S(1)} %concatenate.6.info, bf16[8,4,128,128]{3,2,1,0:T(8,128)(2,1)S(1)} %all-to-all-done.queries, bf16[512,128]{1,0:T(8,128)(2,1)S(1)} %constant_dynamic-update-slice_fusion.refs_0_, bf16[512,128]{1,0:T(8,128)(2,1)S(1)} %collective-permute-done.refs_1_, ...), custom_call_target="tpu_custom_call" | custom-call | flops 2147483648 | bytes 4194304 | tf_op jit(solution)/shard_map/pallas_call | solution.py:132
  87.4 3.6 %all-to-all-start.1 = ((bf16[8,528,128]{2,1,0:T(8,128)(2,1)}), bf16[8,528,128]{2,1,0:T(8,128)(2,1)S(1)}, u32[]{:S(2)}, u32[]{:S(2)}) async-start(bf16[8,528,128]{2,1,0:T(8,128)(2,1)} %shard_map.73), calls=%async_computation.1 | async-start | bytes 2162688 | tf_op jit(solution)/shard_map/all_to_all | solution.py:186
  91.0 9.5 %all-to-all-done.1 = bf16[8,528,128]{2,1,0:T(8,128)(2,1)S(1)} async-done(((bf16[8,528,128]{2,1,0:T(8,128)(2,1)}), bf16[8,528,128]{2,1,0:T(8,128)(2,1)S(1)}, u32[]{:S(2)}, u32[]{:S(2)}) %all-to-all-start.1) | async-done | bytes 1081376 | tf_op jit(solution)/shard_map/all_to_all | solution.py:186
  100.5 0.1 fusion.2
  100.7 0.2 fusion
  100.9 0.6 gather_fusion.1
  101.5 0.1 broadcast_select_fusion
  101.5 2.9 %convolution_convert_fusion = bf16[128,4096]{1,0:T(8,128)(2,1)S(1)} fusion(bf16[512,128]{1,0:T(8,128)(2,1)S(1)} %bitcast.40, bf16[512,4096]{1,0:T(8,128)(2,1)} %param.15), kind=kOutput, calls=%fused_computation.2 | convolution fusion | flops 537395200 | bytes 5373952 | tf_op jit(solution)/shard_map/dot_general | solution.py:195
  104.5 0.1 copy.23
  104.6 26.2 %all_to_all.15 = bf16[8,512,128]{1,2,0:T(8,128)(2,1)S(1)} all-to-all(bf16[8,512,128]{1,2,0:T(8,128)(2,1)S(1)} %bitcast.35), channel_id=1, replica_groups=mesh['k'=8,'e'=2,'x'=4,'y'=4,'c'=2] {'y','c'}, dimensions={0} | all-to-all | bytes 2097152 | tf_op jit(solution)/shard_map/all_to_all | solution.py:198
  130.8 0.1 reduce_sum.52
  130.9 0.8 copy.19
  (15 shorter events, 0.1 us)
Async XLA Ops:
  3.4 8.3 %copy-start = (bf16[128,128]{1,0:T(8,128)(2,1)S(1)}, bf16[128,128]{1,0:T(8,128)(2,1)}, u32[]{:S(2)}) copy-start(bf16[128,128]{1,0:T(8,128)(2,1)} %param.12) | copy-start | bytes 98308
  3.4 8.3 %copy-start.1 = (bf16[128,128]{1,0:T(8,128)(2,1)S(1)}, bf16[128,128]{1,0:T(8,128)(2,1)}, u32[]{:S(2)}) copy-start(bf16[128,128]{1,0:T(8,128)(2,1)} %param.13) | copy-start | bytes 98308
  3.4 8.3 %copy-start.2 = (bf16[128,128]{1,0:T(8,128)(2,1)S(1)}, bf16[128,128]{1,0:T(8,128)(2,1)}, u32[]{:S(2)}) copy-start(bf16[128,128]{1,0:T(8,128)(2,1)} %param.10) | copy-start | bytes 98308
  3.4 8.3 %copy-start.3 = (bf16[128,128]{1,0:T(8,128)(2,1)S(1)}, bf16[128,128]{1,0:T(8,128)(2,1)}, u32[]{:S(2)}) copy-start(bf16[128,128]{1,0:T(8,128)(2,1)} %param.11) | copy-start | bytes 98308
  5.5 61.9 %all-to-all-start = ((bf16[8,4,128,128]{3,2,1,0:T(8,128)(2,1)}), bf16[8,4,128,128]{3,2,1,0:T(8,128)(2,1)S(1)}, u32[]{:S(2)}, u32[]{:S(2)}) async-start(bf16[8,4,128,128]{3,2,1,0:T(8,128)(2,1)} %broadcast_in_dim.45), calls=%async_computation | async-start | bytes 2097152 | tf_op jit(solution)/shard_map/all_to_all | solution.py:161
  11.7 28.7 %collective-permute-start = (bf16[512,128]{1,0:T(8,128)(2,1)S(1)}, bf16[512,128]{1,0:T(8,128)(2,1)S(1)}, u32[]{:S(2)}, u32[]{:S(2)}) collective-permute-start(bf16[512,128]{1,0:T(8,128)(2,1)S(1)} %constant_dynamic-update-slice_fusion.refs_0_), channel_id=1, source_target_pairs={{0,64},{64,128},{128,192},{192,256},{256,320},{320,384},{384,448},... | collective-permute-start | bytes 393224 | tf_op jit(solution)/shard_map/ppermute | solution.py:168
  16.7 25.7 %collective-permute-start.1 = (bf16[512,128]{1,0:T(8,128)(2,1)S(1)}, bf16[512,128]{1,0:T(8,128)(2,1)S(1)}, u32[]{:S(2)}, u32[]{:S(2)}) collective-permute-start(bf16[512,128]{1,0:T(8,128)(2,1)S(1)} %constant_dynamic-update-slice_fusion.refs_0_), channel_id=1, source_target_pairs={{0,448},{64,0},{128,64},{192,128},{256,192},{320,256},{384,320},{4... | collective-permute-start | bytes 393224 | tf_op jit(solution)/shard_map/ppermute | solution.py:169
  40.4 8.8 %collective-permute-start.2 = (bf16[512,128]{1,0:T(8,128)(2,1)S(1)}, bf16[512,128]{1,0:T(8,128)(2,1)S(1)}, u32[]{:S(2)}, u32[]{:S(2)}) collective-permute-start(bf16[512,128]{1,0:T(8,128)(2,1)S(1)} %collective-permute-done.refs_1_), channel_id=1, source_target_pairs={{0,64},{64,128},{128,192},{192,256},{256,320},{320,384},{384,448},... | collective-permute-start | bytes 393224 | tf_op jit(solution)/shard_map/ppermute | solution.py:168
  42.3 9.0 %collective-permute-start.3 = (bf16[512,128]{1,0:T(8,128)(2,1)S(1)}, bf16[512,128]{1,0:T(8,128)(2,1)S(1)}, u32[]{:S(2)}, u32[]{:S(2)}) collective-permute-start(bf16[512,128]{1,0:T(8,128)(2,1)S(1)} %collective-permute-done.1.refs_2_), channel_id=1, source_target_pairs={{0,448},{64,0},{128,64},{192,128},{256,192},{320,256},{384,320},{4... | collective-permute-start | bytes 393224 | tf_op jit(solution)/shard_map/ppermute | solution.py:169
  49.3 8.9 %collective-permute-start.4 = (bf16[512,128]{1,0:T(8,128)(2,1)S(1)}, bf16[512,128]{1,0:T(8,128)(2,1)S(1)}, u32[]{:S(2)}, u32[]{:S(2)}) collective-permute-start(bf16[512,128]{1,0:T(8,128)(2,1)S(1)} %collective-permute-done.2.refs_3_), channel_id=1, source_target_pairs={{0,64},{64,128},{128,192},{192,256},{256,320},{320,384},{384,448},... | collective-permute-start | bytes 393224 | tf_op jit(solution)/shard_map/ppermute | solution.py:168
  51.4 8.8 %collective-permute-start.5 = (bf16[512,128]{1,0:T(8,128)(2,1)S(1)}, bf16[512,128]{1,0:T(8,128)(2,1)S(1)}, u32[]{:S(2)}, u32[]{:S(2)}) collective-permute-start(bf16[512,128]{1,0:T(8,128)(2,1)S(1)} %collective-permute-done.3.refs_4_), channel_id=1, source_target_pairs={{0,448},{64,0},{128,64},{192,128},{256,192},{320,256},{384,320},{4... | collective-permute-start | bytes 393224 | tf_op jit(solution)/shard_map/ppermute | solution.py:169
  58.2 8.0 %collective-permute-start.6 = (bf16[256,128]{1,0:T(8,128)(2,1)S(1)}, bf16[256,128]{1,0:T(8,128)(2,1)S(1)}, u32[]{:S(2)}, u32[]{:S(2)}) collective-permute-start(bf16[256,128]{1,0:T(8,128)(2,1)S(1)} %slice.32), channel_id=1, source_target_pairs={{0,64},{64,128},{128,192},{192,256},{256,320},{320,384},{384,448},... | collective-permute-start | bytes 196616 | tf_op jit(solution)/shard_map/ppermute | solution.py:171
  60.1 7.2 %collective-permute-start.7 = (bf16[256,128]{1,0:T(8,128)(2,1)S(1)}, bf16[256,128]{1,0:T(8,128)(2,1)S(1)}, u32[]{:S(2)}, u32[]{:S(2)}) collective-permute-start(bf16[256,128]{1,0:T(8,128)(2,1)S(1)} %slice.33), channel_id=1, source_target_pairs={{0,448},{64,0},{128,64},{192,128},{256,192},{320,256},{384,320},{4... | collective-permute-start | bytes 196616 | tf_op jit(solution)/shard_map/ppermute | solution.py:172
  87.4 13.1 %all-to-all-start.1 = ((bf16[8,528,128]{2,1,0:T(8,128)(2,1)}), bf16[8,528,128]{2,1,0:T(8,128)(2,1)S(1)}, u32[]{:S(2)}, u32[]{:S(2)}) async-start(bf16[8,528,128]{2,1,0:T(8,128)(2,1)} %shard_map.73), calls=%async_computation.1 | async-start | bytes 2162688 | tf_op jit(solution)/shard_map/all_to_all | solution.py:186

commit v2 on v0

v2 whole, which is shorter than its diff:
```python
import math

import jax
import jax.numpy as jnp
from jax import lax
from jax.experimental import pallas as pl
from jax.experimental.pallas import tpu as pltpu
from jax.sharding import Mesh
from jax.sharding import PartitionSpec as P

HD = 128
GROUP = 4
BLOCKS = 8
RING = 8
STATS = 16
PIECE = GROUP * HD + STATS
MASKED = -1e30
FLOOR = -1e29
FACTOR = math.log2(math.e) / math.sqrt(HD)
TILE = 2 * HD
TILES = 2 * BLOCKS * HD // TILE
CACHE = 2 * RING * BLOCKS // 2 * HD
VMEM = pl.BlockSpec(memory_space=pltpu.VMEM)
SMEM = pl.BlockSpec(memory_space=pltpu.SMEM)
NT = (((1,), (1,)), ((), ()))
NN = (((1,), (0,)), ((), ()))


def dot(a, b, dims):
    return lax.dot_general(a, b, dims, preferred_element_type=jnp.float32)


def head_order(spans):
    far = [(spans[h] > 4 * HD).astype(jnp.int32) for h in range(GROUP)]
    order = [jnp.int32(0)] * GROUP
    ahead = jnp.int32(0)
    for h in range(GROUP):
        rank = jnp.where(far[h] == 1, ahead, 2 + h - ahead)
        ahead = ahead + far[h]
        order = [jnp.where(rank == s, h, order[s]) for s in range(GROUP)]
    return order


def prepare_kernel(spans, queries, keys, values, cache_keys, cache_values, own, sent):
    own[0:HD, :] = cache_keys[...]
    own[HD : 2 * HD, :] = cache_values[...]
    own[2 * HD : 3 * HD, :] = keys[...]
    own[3 * HD :, :] = values[...]
    order = head_order(spans)
    for s in range(GROUP):
        rows = queries[:, pl.ds(pl.multiple_of(order[s] * HD, HD), HD)]
        for j in range(BLOCKS):
            sent[j, s] = rows


def place(info, distance):
    k = lax.rem(info[0] + distance + RING, RING)
    return ((k * 2 + info[1]) * 4 + info[2]) * HD


def offsets():
    token = lax.broadcasted_iota(jnp.int32, (HD, TILE), 1)
    return lax.rem(token, HD), token - lax.broadcasted_iota(jnp.int32, (HD, TILE), 0)


def tile_of(t):
    per = TILE // HD
    return t // (BLOCKS // per), t % (BLOCKS // per) * per


def masked_scores(info, spans, order, offset, key_rows, rows, t, cached, start):
    slot, first = tile_of(t)
    position = CACHE + info[0] * (BLOCKS * HD) + first * HD
    found = dot(key_rows, rows, NT)
    if cached:
        allowed = offset < spans[order[slot]] - position + start
    else:
        allowed = offset >= start + CACHE - position
    return jnp.where(allowed, found, MASKED)


def highest(found):
    return jnp.max(found.reshape(HD // 8, 8, found.shape[1]), axis=0)


def first_kernel(info, spans, queries, *refs):
    kv = refs[: RING - 1]
    sums, tops, near, near_tops, keys, flipped, scores = refs[RING - 1 :]
    order = head_order(spans)
    distances = [0, -1, 1, -2, 2, -3, 3]
    blocks = []
    for i in range(RING - 1):
        for half in range(2):
            n = len(blocks)
            blocks.append((half == 0, place(info, distances[i])))
            keys[n * HD : (n + 1) * HD, :] = kv[i][2 * half * HD : (2 * half + 1) * HD, :]
            flipped[0:HD, n * HD : (n + 1) * HD] = kv[i][
                (2 * half + 1) * HD : (2 * half + 2) * HD, :
            ].T
    width = len(blocks) * HD
    flipped[HD:, :] = jnp.ones((STATS, width), jnp.bfloat16)
    column, offset = offsets()

    def score(t):
        slot, first = tile_of(t)
        rows = queries[first : first + TILE // HD, slot].reshape(TILE, HD)
        top = jnp.full((8, TILE), FLOOR, jnp.float32)
        for n, (cached, start) in enumerate(blocks):
            found = masked_scores(
                info, spans, order, offset, keys[n * HD : (n + 1) * HD, :], rows, t, cached, start
            )
            scores[t % 2, n * HD : (n + 1) * HD, :] = found
            top = jnp.maximum(top, highest(found))
        return jnp.max(top, axis=0, keepdims=True)

    def finish(t, top):
        weights = jnp.concatenate(
            [
                jnp.exp2((scores[t % 2, n * HD : (n + 1) * HD, :] - top) * FACTOR).astype(
                    jnp.bfloat16
                )
                for n in range(len(blocks))
            ],
            axis=0,
        )
        sums[t] = dot(flipped[...], weights, NN)
        tops[t] = jnp.broadcast_to(top, (8, TILE))

    own = info[1] * 4 + info[2]
    wraps = info[0] == 0
    at = jnp.where(wraps, 2 * HD, 3 * HD)
    before_keys = keys[pl.ds(pl.multiple_of(at, HD), HD), :]
    before_values = jnp.where(
        wraps, flipped[:, 2 * HD : 3 * HD], flipped[:, 3 * HD : 4 * HD]
    )
    before_start = place(info, -1) + jnp.where(wraps, 0, CACHE)
    own_start = place(info, 0) + CACHE
    span = jnp.where(
        lax.broadcasted_iota(jnp.int32, (HD, TILE), 1) < HD, spans[order[2]], spans[order[3]]
    )
    near_offset = column - lax.broadcasted_iota(jnp.int32, (HD, TILE), 0)
    for b in range(BLOCKS):
        earlier = b < own
        rows = queries[b, 2:4].reshape(TILE, HD)
        found = dot(jnp.where(earlier, before_keys, keys[HD : 2 * HD, :]), rows, NT)
        position = CACHE + (info[0] * BLOCKS + b) * HD
        behind = near_offset + (position - jnp.where(earlier, before_start, own_start))
        found = jnp.where((behind >= 0) & (behind < span), found, MASKED)
        top = jnp.maximum(jnp.max(found, axis=0, keepdims=True), FLOOR)
        weights = jnp.exp2((found - top) * FACTOR).astype(jnp.bfloat16)
        near[b] = dot(jnp.where(earlier, before_values, flipped[:, HD : 2 * HD]), weights, NN)
        near_tops[b] = jnp.broadcast_to(top, (8, TILE))

    top = score(0)
    for t in range(TILES):
        later = score(t + 1) if t + 1 < TILES else None
        finish(t, top)
        top = later


def write_stats(stats, block, slot, top, total):
    level = jnp.where(total > 0.0, top * FACTOR + jnp.log2(total), MASKED)
    for i in range(3):
        term = level.astype(jnp.bfloat16).astype(jnp.float32)
        stats[block, slot * 4 + i : slot * 4 + i + 1, :] = term
        level = level - term


def second_kernel(info, spans, queries, last, sums, tops, near, near_tops, out, stats):
    order = head_order(spans)
    start = place(info, 4)
    _, offset = offsets()
    ones = jnp.ones((STATS, HD), jnp.bfloat16)
    flipped = jnp.concatenate(
        [
            jnp.concatenate([last[HD : 2 * HD, :].T, ones], axis=0),
            jnp.concatenate([last[3 * HD :, :].T, ones], axis=0),
        ],
        axis=1,
    )
    stats[...] = jnp.zeros_like(stats)

    def emit(block, slot, top, summed):
        total = summed[HD : HD + 1, :]
        normal = summed[:HD, :] * (1.0 / jnp.maximum(total, 1e-30))
        out[block, slot * HD : (slot + 1) * HD, :] = normal.astype(jnp.bfloat16)
        write_stats(stats, block, slot, top, total)

    for b in range(BLOCKS):
        for j in range(2):
            cut = slice(j * HD, (j + 1) * HD)
            emit(b, 2 + j, near_tops[b, 0:1, cut], near[b, :, cut])
    for t in range(TILES):
        slot, first = tile_of(t)
        rows = queries[first : first + TILE // HD, slot].reshape(TILE, HD)
        found = [
            masked_scores(
                info, spans, order, offset, last[2 * half * HD : (2 * half + 1) * HD, :],
                rows, t, half == 0, start,
            )
            for half in range(2)
        ]
        before = tops[t, 0:1, :]
        top = jnp.max(jnp.maximum(highest(found[0]), highest(found[1])), axis=0, keepdims=True)
        top = jnp.maximum(top, before)
        weights = [jnp.exp2((f - top) * FACTOR).astype(jnp.bfloat16) for f in found]
        summed = sums[t] * jnp.exp2((before - top) * FACTOR) + dot(
            flipped, jnp.concatenate(weights, axis=0), NN
        )
        for j in range(TILE // HD):
            cut = slice(j * HD, (j + 1) * HD)
            emit(first + j, slot, top[:, cut], summed[:, cut])
    out[:, GROUP * HD :, :] = stats[...].astype(jnp.bfloat16)


def project_kernel(spans, parts, weight, out, attn):
    order = head_order(spans)
    for s in range(GROUP):
        terms = parts[:, GROUP * HD :, :].astype(jnp.float32)
        level = [
            terms[i, 4 * s : 4 * s + 1] + terms[i, 4 * s + 1 : 4 * s + 2] + terms[i, 4 * s + 2 : 4 * s + 3]
            for i in range(BLOCKS)
        ]
        top = level[0]
        for i in range(1, BLOCKS):
            top = jnp.maximum(top, level[i])
        share = [jnp.exp2(v - top) for v in level]
        total = share[0]
        for i in range(1, BLOCKS):
            total = total + share[i]
        summed = jnp.zeros((HD, HD), jnp.float32)
        for i in range(BLOCKS):
            summed = summed + parts[i, s * HD : (s + 1) * HD, :].astype(jnp.float32) * share[i]
        attn[:, pl.ds(pl.multiple_of(order[s] * HD, HD), HD)] = (
            (summed * (1.0 / total)).T.astype(jnp.bfloat16)
        )
    rows = attn[...]
    width = out.shape[2]
    for f in range(out.shape[0]):
        out[f] = dot(rows, weight[:, f * width : (f + 1) * width], NN).astype(jnp.bfloat16)


def total_kernel(shares, out):
    total = shares[0].astype(jnp.float32)
    for i in range(1, shares.shape[0]):
        total = total + shares[i].astype(jnp.float32)
    out[...] = total.T.astype(jnp.bfloat16)


def call(kernel, outs, specs, scratch=(), vmem=24, flops=0, moved=0, exps=0):
    single = not isinstance(outs, list)
    return pl.pallas_call(
        kernel,
        out_shape=outs,
        in_specs=specs,
        out_specs=VMEM if single else [VMEM] * len(outs),
        scratch_shapes=list(scratch),
        compiler_params=pltpu.CompilerParams(vmem_limit_bytes=vmem * 2**20),
        cost_estimate=pl.CostEstimate(flops=flops, bytes_accessed=moved, transcendentals=exps),
    )


def per_device(queries, keys, values, cache_keys, cache_values, spans, out_weight):
    info = jnp.stack([lax.axis_index("k"), lax.axis_index("e"), lax.axis_index("x")])
    bf16, f32 = jnp.bfloat16, jnp.float32
    own, sent = call(
        prepare_kernel,
        [
            jax.ShapeDtypeStruct((4 * HD, HD), bf16),
            jax.ShapeDtypeStruct((BLOCKS, GROUP, HD, HD), bf16),
        ],
        [SMEM] + [VMEM] * 5,
        moved=2**21,
    )(spans, queries, keys, values, cache_keys, cache_values)
    up_route = [(i, (i + 1) % RING) for i in range(RING)]
    down_route = [(i, (i - 1) % RING) for i in range(RING)]
    kv, up, down = [own], own, own
    for _ in range(RING // 2 - 1):
        up = lax.ppermute(up, "k", up_route)
        down = lax.ppermute(down, "k", down_route)
        kv += [up, down]
    last = lax.ppermute(up, "k", up_route)
    grouped = lax.all_to_all(sent, ("e", "x"), 0, 0, tiled=True)

    near_blocks = 2 * (RING - 1)
    state = call(
        first_kernel,
        [
            jax.ShapeDtypeStruct((TILES, HD + STATS, TILE), f32),
            jax.ShapeDtypeStruct((TILES, 8, TILE), f32),
            jax.ShapeDtypeStruct((BLOCKS, HD + STATS, TILE), f32),
            jax.ShapeDtypeStruct((BLOCKS, 8, TILE), f32),
        ],
        [SMEM, SMEM] + [VMEM] * RING,
        [
            pltpu.VMEM((near_blocks * HD, HD), bf16),
            pltpu.VMEM((HD + STATS, near_blocks * HD), bf16),
            pltpu.VMEM((2, near_blocks * HD, TILE), f32),
        ],
        flops=4 * 2048 * 1792 * 128,
        moved=4 * 2**20,
        exps=2048 * 1792,
    )(info, spans, grouped, *kv)
    partial = call(
        second_kernel,
        jax.ShapeDtypeStruct((BLOCKS, PIECE, HD), bf16),
        [SMEM, SMEM] + [VMEM] * 6,
        [pltpu.VMEM((BLOCKS, STATS, HD), f32)],
        flops=4 * 2048 * 256 * 128,
        moved=4 * 2**20,
        exps=2048 * 256,
    )(info, spans, grouped, last, *state)
    parts = lax.all_to_all(partial, ("e", "x"), 0, 0, tiled=True)
    product = call(
        project_kernel,
        jax.ShapeDtypeStruct((8, HD, out_weight.shape[1] // 8), bf16),
        [SMEM, VMEM, VMEM],
        [pltpu.VMEM((HD, GROUP * HD), bf16)],
        flops=2 * 128 * 512 * 4096,
        moved=5 * 2**20,
    )(spans, parts, out_weight)
    shares = lax.all_to_all(product, ("y", "c"), 0, 0, tiled=True)
    return call(
        total_kernel,
        jax.ShapeDtypeStruct((out_weight.shape[1] // 8, HD), bf16),
        [VMEM],
        moved=2**20,
    )(shares)


def solution(mesh):
    fine = Mesh(mesh.devices.reshape(RING, 2, 4, 4, 2), ("k", "e", "x", "y", "c"))
    seq, head = ("k", "e", "x"), ("y", "c")
    placed = (P(seq, head),) * 5 + (P(head), P(head, None))
    return jax.shard_map(
        per_device, mesh=fine, in_specs=placed, out_specs=P(head, seq), check_vma=False
    )
```

time: 634 us -> 113 us (0.18)
  waiting for transfers between devices: 545 us -> 17.8 us
  blocking collectives: 0 us -> 40.5 us
  matrix products: 21 us -> 0 us
  between operations: 13.4 us -> 0.14 us
  Pallas kernels: 0 us -> 12.9 us
  other arithmetic: 9.34 us -> 0.08 us
  local copies, waits for them, and re-layouts: 12.8 us -> 4.6 us
    all_gather x4 -> x0, waiting for transfers between devices: 495 us -> none  [the longest x1 140 us: per_device(): window_keys = lax.all_gather(keys, 'seq', axis=0, tiled=True)]
    reduce_scatter x1 -> x0, waiting for transfers between devices: 42.9 us -> none  [per_device(): lax.psum_scatter(jnp.dot(attn, out_weight, preferred_element_type=jnp.flo...]
    all_to_all x0 -> x2, blocking collectives: none -> 40.5 us  [the longest x1 27.2 us: per_device(): shares = lax.all_to_all(product, ('y', 'c'), 0, 0, tiled=True)]
    dot_general x5 -> x0, matrix products: 21 us -> none  [the longest x2 9.57 us: online_update(): jnp.dot(weights.astype(jnp.bfloat16), value_rows, preferred_element_type=...]
    pallas_call x0 -> x5, Pallas kernels: none -> 12.9 us  [the longest x1 6.2 us: per_device(): call(first_kernel, [jax.ShapeDtypeStruct((TILES, HD + STATS, TILE), f32),...]
    ppermute x8 -> x7, waiting for transfers between devices: 5.19 us -> 17.8 us  [the longest x3 17.6 us: per_device(): up = lax.ppermute(up, 'k', up_route)]
    ppermute x8 -> x7, starting transfers between devices: 30.5 us -> 30.6 us  [the longest x3 19.9 us: per_device(): down = lax.ppermute(down, 'k', down_route)]
  transfers between devices with their start and end apart: 13 -> 8, of which waited for: 7 -> 3; matrix products, arithmetic and copies ran while one was open for 3% -> 0% of each run, Pallas kernels for 0% -> 5%
where the time goes in v2:
time: 113 us
  blocking collectives  40.5 us (36%)
  starting transfers between devices  36.8 us (33%)
  waiting for transfers between devices  17.8 us (16%)
  Pallas kernels  12.9 us (11%)
  local copies, waits for them, and re-layouts  4.6 us (4%)
    all_to_all x1, blocking collectives, per_device(): shares = lax.all_to_all(product, ('y', 'c'), 0, 0, tiled=True)  27.2 us
    ppermute x3, starting transfers between devices, per_device(): down = lax.ppermute(down, 'k', down_route)  19.9 us
    ppermute x3, waiting for transfers between devices, per_device(): up = lax.ppermute(up, 'k', up_route)  17.6 us
    all_to_all x1, blocking collectives, per_device(): parts = lax.all_to_all(partial, ('e', 'x'), 0, 0, tiled=True)  13.3 us
    ppermute x3, starting transfers between devices, per_device(): up = lax.ppermute(up, 'k', up_route)  8.71 us
    all_to_all x1, starting transfers between devices, per_device(): grouped = lax.all_to_all(sent, ('e', 'x'), 0, 0, tiled=True)  6.2 us
    pallas_call x1, Pallas kernels, per_device(): call(first_kernel, [jax.ShapeDtypeStruct((TILES, HD + STATS, TILE), f32),...  6.2 us
    unnamed x16, local copies, waits for them, and re-layouts  4.6 us
  transfers between devices with their start and end apart: 8, of which 3 were waited for; matrix products, arithmetic and copies ran while one was open for 0% of the time, Pallas kernels for 5%

profile of v2, /device:TPU:1, one launch (start us, length us, event | category | flops | bytes accessed | tf_op | source)
XLA Modules:
  0.0 112.8 jit_solution(3109458519514039280)
XLA Ops:
  0.0 0.0 copy-start.1
  0.0 0.9 copy-done.1
  0.9 0.0 copy-start.2
  0.9 0.8 copy-done.2
  1.7 0.0 copy-start.3
  1.7 0.8 copy-done.3
  2.4 0.0 copy-start.4
  2.4 0.8 copy-done.4
  3.2 0.0 copy-start.5
  3.2 0.8 copy-done.5
  3.9 0.0 copy-start.6
  3.9 0.7 copy-done.6
  4.6 0.0 copy-start.7
  4.6 1.7 %shard_map.73 = (bf16[512,128]{1,0:T(8,128)(2,1)S(1)}, bf16[8,4,128,128]{3,2,1,0:T(8,128)(2,1)}) custom-call(s32[4]{0:T(128)S(1)} %copy-done.6, bf16[128,512]{1,0:T(8,128)(2,1)S(1)} %copy-done.1, bf16[128,128]{1,0:T(8,128)(2,1)S(1)} %copy-done.2, bf16[128,128]{1,0:T(8,128)(2,1)S(1)} %copy-done.3, bf16[128,128]{1,0:T(8,128)(2,1)S(1)} %copy-done.4, ...), custom_call_target="tpu_custom_call" | custom-call | bytes 2097152 | tf_op jit(solution)/shard_map/pallas_call | solution.py:266
  6.3 6.2 %all-to-all-start = ((bf16[8,4,128,128]{3,2,1,0:T(8,128)(2,1)}), bf16[8,4,128,128]{3,2,1,0:T(8,128)(2,1)S(1)}, u32[]{:S(2)}, u32[]{:S(2)}) async-start(bf16[8,4,128,128]{3,2,1,0:T(8,128)(2,1)} %get-tuple-element.11), calls=%async_computation | async-start | bytes 2097152 | tf_op jit(solution)/shard_map/all_to_all | solution.py:283
  12.5 4.9 %collective-permute-start = (bf16[512,128]{1,0:T(8,128)(2,1)S(1)}, bf16[512,128]{1,0:T(8,128)(2,1)S(1)}, u32[]{:S(2)}, u32[]{:S(2)}) collective-permute-start(bf16[512,128]{1,0:T(8,128)(2,1)S(1)} %get-tuple-element.12.refs_0_), channel_id=1, source_target_pairs={{0,64},{64,128},{128,192},{192,256},{256,320},{320,384},{384,448},... | collective-permute-start | bytes 393224 | tf_op jit(solution)/shard_map/ppermute | solution.py:279
  17.4 7.7 %collective-permute-start.4 = (bf16[512,128]{1,0:T(8,128)(2,1)S(1)}, bf16[512,128]{1,0:T(8,128)(2,1)S(1)}, u32[]{:S(2)}, u32[]{:S(2)}) collective-permute-start(bf16[512,128]{1,0:T(8,128)(2,1)S(1)} %get-tuple-element.12.refs_0_), channel_id=1, source_target_pairs={{0,448},{64,0},{128,64},{192,128},{256,192},{320,256},{384,320},{4... | collective-permute-start | bytes 393224 | tf_op jit(solution)/shard_map/ppermute | solution.py:280
  25.1 16.2 %collective-permute-done.refs_1_ = bf16[512,128]{1,0:T(8,128)(2,1)S(1)} collective-permute-done((bf16[512,128]{1,0:T(8,128)(2,1)S(1)}, bf16[512,128]{1,0:T(8,128)(2,1)S(1)}, u32[]{:S(2)}, u32[]{:S(2)}) %collective-permute-start) | collective-permute-done | bytes 131104 | tf_op jit(solution)/shard_map/ppermute | solution.py:279
  41.2 1.9 %collective-permute-start.1 = (bf16[512,128]{1,0:T(8,128)(2,1)S(1)}, bf16[512,128]{1,0:T(8,128)(2,1)S(1)}, u32[]{:S(2)}, u32[]{:S(2)}) collective-permute-start(bf16[512,128]{1,0:T(8,128)(2,1)S(1)} %collective-permute-done.refs_1_), channel_id=1, source_target_pairs={{0,64},{64,128},{128,192},{192,256},{256,320},{320,384},{384,448},... | collective-permute-start | bytes 393224 | tf_op jit(solution)/shard_map/ppermute | solution.py:279
  43.2 0.0 collective-permute-done.4.refs_2_
  43.2 5.5 %collective-permute-start.5 = (bf16[512,128]{1,0:T(8,128)(2,1)S(1)}, bf16[512,128]{1,0:T(8,128)(2,1)S(1)}, u32[]{:S(2)}, u32[]{:S(2)}) collective-permute-start(bf16[512,128]{1,0:T(8,128)(2,1)S(1)} %collective-permute-done.4.refs_2_), channel_id=1, source_target_pairs={{0,448},{64,0},{128,64},{192,128},{256,192},{320,256},{384,320},{4... | collective-permute-start | bytes 393224 | tf_op jit(solution)/shard_map/ppermute | solution.py:280
  48.6 1.4 %collective-permute-done.1.refs_3_ = bf16[512,128]{1,0:T(8,128)(2,1)S(1)} collective-permute-done((bf16[512,128]{1,0:T(8,128)(2,1)S(1)}, bf16[512,128]{1,0:T(8,128)(2,1)S(1)}, u32[]{:S(2)}, u32[]{:S(2)}) %collective-permute-start.1) | collective-permute-done | bytes 131104 | tf_op jit(solution)/shard_map/ppermute | solution.py:279
  50.1 1.9 %collective-permute-start.2 = (bf16[512,128]{1,0:T(8,128)(2,1)S(1)}, bf16[512,128]{1,0:T(8,128)(2,1)S(1)}, u32[]{:S(2)}, u32[]{:S(2)}) collective-permute-start(bf16[512,128]{1,0:T(8,128)(2,1)S(1)} %collective-permute-done.1.refs_3_), channel_id=1, source_target_pairs={{0,64},{64,128},{128,192},{192,256},{256,320},{320,384},{384,448},... | collective-permute-start | bytes 393224 | tf_op jit(solution)/shard_map/ppermute | solution.py:279
  52.0 0.2 collective-permute-done.5.refs_4_
  52.2 6.8 %collective-permute-start.6 = (bf16[512,128]{1,0:T(8,128)(2,1)S(1)}, bf16[512,128]{1,0:T(8,128)(2,1)S(1)}, u32[]{:S(2)}, u32[]{:S(2)}) collective-permute-start(bf16[512,128]{1,0:T(8,128)(2,1)S(1)} %collective-permute-done.5.refs_4_), channel_id=1, source_target_pairs={{0,448},{64,0},{128,64},{192,128},{256,192},{320,256},{384,320},{4... | collective-permute-start | bytes 393224 | tf_op jit(solution)/shard_map/ppermute | solution.py:280
  59.0 0.1 pad_add_fusion.info
  59.1 0.0 collective-permute-done.2.refs_5_
  59.1 1.9 %collective-permute-start.3 = (bf16[512,128]{1,0:T(8,128)(2,1)S(1)}, bf16[512,128]{1,0:T(8,128)(2,1)S(1)}, u32[]{:S(2)}, u32[]{:S(2)}) collective-permute-start(bf16[512,128]{1,0:T(8,128)(2,1)S(1)} %collective-permute-done.2.refs_5_), channel_id=1, source_target_pairs={{0,64},{64,128},{128,192},{192,256},{256,320},{320,384},{384,448},... | collective-permute-start | bytes 393224 | tf_op jit(solution)/shard_map/ppermute | solution.py:282
  61.0 0.0 collective-permute-done.6.refs_6_
  61.0 0.0 all-to-all-done.queries
  61.0 0.0 copy-done.7
  61.0 6.2 %shard_map.74 = (f32[8,144,256]{2,1,0:T(8,128)S(1)}, f32[8,8,256]{2,1,0:T(8,128)S(1)}, f32[8,144,256]{2,1,0:T(8,128)S(1)}, f32[8,8,256]{2,1,0:T(8,128)S(1)}) custom-call(s32[3]{0:T(128)S(1)} %pad_add_fusion.info, s32[4]{0:T(128)S(1)} %copy-done.7, bf16[8,4,128,128]{3,2,1,0:T(8,128)(2,1)S(1)} %all-to-all-done.queries, ...), custom_call_target="tpu_custom_call" | custom-call | flops 1879048192 | bytes 4194304 | tf_op jit(solution)/shard_map/pallas_call | solution.py:286
  67.2 0.0 collective-permute-done.3.last
  67.2 0.0 copy-start
  67.2 2.5 %shard_map.75 = bf16[8,528,128]{2,1,0:T(8,128)(2,1)S(1)} custom-call(s32[3]{0:T(128)S(1)} %pad_add_fusion.info, s32[4]{0:T(128)S(1)} %copy-done.7, bf16[8,4,128,128]{3,2,1,0:T(8,128)(2,1)S(1)} %all-to-all-done.queries, bf16[512,128]{1,0:T(8,128)(2,1)S(1)} %collective-permute-done.3.last, f32[8,144,256]{2,1,0:T(8,128)S(1)} %get-tuple-element.13.sums, ...), custom_call_target="tpu_custom_call" | custom-call | flops 268435456 | bytes 4194304 | tf_op jit(solution)/shard_map/pallas_call | solution.py:304
  69.8 13.3 %all_to_all.15.parts = bf16[8,528,128]{2,1,0:T(8,128)(2,1)S(1)} all-to-all(bf16[8,528,128]{2,1,0:T(8,128)(2,1)S(1)} %shard_map.75), channel_id=1, replica_groups=mesh['k'=8,'e'=2,'x'=4,'y'=4,'c'=2] {'e','x'}, dimensions={0} | all-to-all | bytes 2162688 | tf_op jit(solution)/shard_map/all_to_all | solution.py:313
  83.1 0.0 copy-done
  83.1 1.6 %shard_map.76 = bf16[8,128,512]{2,1,0:T(8,128)(2,1)S(1)} custom-call(s32[4]{0:T(128)S(1)} %copy-done.7, bf16[8,528,128]{2,1,0:T(8,128)(2,1)S(1)} %all_to_all.15.parts, bf16[512,4096]{1,0:T(8,128)(2,1)S(1)} %copy-done), custom_call_target="tpu_custom_call" | custom-call | flops 536870912 | bytes 5242880 | tf_op jit(solution)/shard_map/pallas_call | solution.py:314
  84.7 27.2 %all_to_all.16.shares = bf16[8,128,512]{2,1,0:T(8,128)(2,1)S(1)} all-to-all(bf16[8,128,512]{2,1,0:T(8,128)(2,1)S(1)} %shard_map.76), channel_id=1, replica_groups=mesh['k'=8,'e'=2,'x'=4,'y'=4,'c'=2] {'y','c'}, dimensions={0} | all-to-all | bytes 2097152 | tf_op jit(solution)/shard_map/all_to_all | solution.py:322
  111.9 0.9 shard_map.77
Async XLA Ops:
  0.0 0.9 copy-start.1
  0.9 0.8 copy-start.2
  1.7 0.8 copy-start.3
  2.4 0.8 copy-start.4
  3.2 0.8 copy-start.5
  3.9 0.7 copy-start.6
  4.6 56.4 %copy-start.7 = (s32[4]{0:T(128)S(1)}, s32[4]{0:T(128)}, u32[]{:S(2)}) copy-start(s32[4]{0:T(128)} %spans.7) | copy-start | bytes 52
  6.3 54.7 %all-to-all-start = ((bf16[8,4,128,128]{3,2,1,0:T(8,128)(2,1)}), bf16[8,4,128,128]{3,2,1,0:T(8,128)(2,1)S(1)}, u32[]{:S(2)}, u32[]{:S(2)}) async-start(bf16[8,4,128,128]{3,2,1,0:T(8,128)(2,1)} %get-tuple-element.11), calls=%async_computation | async-start | bytes 2097152 | tf_op jit(solution)/shard_map/all_to_all | solution.py:283
  12.5 28.8 %collective-permute-start = (bf16[512,128]{1,0:T(8,128)(2,1)S(1)}, bf16[512,128]{1,0:T(8,128)(2,1)S(1)}, u32[]{:S(2)}, u32[]{:S(2)}) collective-permute-start(bf16[512,128]{1,0:T(8,128)(2,1)S(1)} %get-tuple-element.12.refs_0_), channel_id=1, source_target_pairs={{0,64},{64,128},{128,192},{192,256},{256,320},{320,384},{384,448},... | collective-permute-start | bytes 393224 | tf_op jit(solution)/shard_map/ppermute | solution.py:279
  17.4 25.8 %collective-permute-start.4 = (bf16[512,128]{1,0:T(8,128)(2,1)S(1)}, bf16[512,128]{1,0:T(8,128)(2,1)S(1)}, u32[]{:S(2)}, u32[]{:S(2)}) collective-permute-start(bf16[512,128]{1,0:T(8,128)(2,1)S(1)} %get-tuple-element.12.refs_0_), channel_id=1, source_target_pairs={{0,448},{64,0},{128,64},{192,128},{256,192},{320,256},{384,320},{4... | collective-permute-start | bytes 393224 | tf_op jit(solution)/shard_map/ppermute | solution.py:280
  41.2 8.8 %collective-permute-start.1 = (bf16[512,128]{1,0:T(8,128)(2,1)S(1)}, bf16[512,128]{1,0:T(8,128)(2,1)S(1)}, u32[]{:S(2)}, u32[]{:S(2)}) collective-permute-start(bf16[512,128]{1,0:T(8,128)(2,1)S(1)} %collective-permute-done.refs_1_), channel_id=1, source_target_pairs={{0,64},{64,128},{128,192},{192,256},{256,320},{320,384},{384,448},... | collective-permute-start | bytes 393224 | tf_op jit(solution)/shard_map/ppermute | solution.py:279
  43.2 9.0 %collective-permute-start.5 = (bf16[512,128]{1,0:T(8,128)(2,1)S(1)}, bf16[512,128]{1,0:T(8,128)(2,1)S(1)}, u32[]{:S(2)}, u32[]{:S(2)}) collective-permute-start(bf16[512,128]{1,0:T(8,128)(2,1)S(1)} %collective-permute-done.4.refs_2_), channel_id=1, source_target_pairs={{0,448},{64,0},{128,64},{192,128},{256,192},{320,256},{384,320},{4... | collective-permute-start | bytes 393224 | tf_op jit(solution)/shard_map/ppermute | solution.py:280
  50.1 9.0 %collective-permute-start.2 = (bf16[512,128]{1,0:T(8,128)(2,1)S(1)}, bf16[512,128]{1,0:T(8,128)(2,1)S(1)}, u32[]{:S(2)}, u32[]{:S(2)}) collective-permute-start(bf16[512,128]{1,0:T(8,128)(2,1)S(1)} %collective-permute-done.1.refs_3_), channel_id=1, source_target_pairs={{0,64},{64,128},{128,192},{192,256},{256,320},{320,384},{384,448},... | collective-permute-start | bytes 393224 | tf_op jit(solution)/shard_map/ppermute | solution.py:279
  52.2 8.8 %collective-permute-start.6 = (bf16[512,128]{1,0:T(8,128)(2,1)S(1)}, bf16[512,128]{1,0:T(8,128)(2,1)S(1)}, u32[]{:S(2)}, u32[]{:S(2)}) collective-permute-start(bf16[512,128]{1,0:T(8,128)(2,1)S(1)} %collective-permute-done.5.refs_4_), channel_id=1, source_target_pairs={{0,448},{64,0},{128,64},{192,128},{256,192},{320,256},{384,320},{4... | collective-permute-start | bytes 393224 | tf_op jit(solution)/shard_map/ppermute | solution.py:280
  59.1 8.2 %collective-permute-start.3 = (bf16[512,128]{1,0:T(8,128)(2,1)S(1)}, bf16[512,128]{1,0:T(8,128)(2,1)S(1)}, u32[]{:S(2)}, u32[]{:S(2)}) collective-permute-start(bf16[512,128]{1,0:T(8,128)(2,1)S(1)} %collective-permute-done.2.refs_5_), channel_id=1, source_target_pairs={{0,64},{64,128},{128,192},{192,256},{256,320},{320,384},{384,448},... | collective-permute-start | bytes 393224 | tf_op jit(solution)/shard_map/ppermute | solution.py:282
  67.2 15.9 %copy-start = (bf16[512,4096]{1,0:T(8,128)(2,1)S(1)}, bf16[512,4096]{1,0:T(8,128)(2,1)}, u32[]{:S(2)}) copy-start(bf16[512,4096]{1,0:T(8,128)(2,1)} %weight.1) | copy-start | bytes 12582916

commit v3 on v2

v3 whole, which is shorter than its diff:
```python
import math

import jax
import jax.numpy as jnp
from jax import lax
from jax.experimental import pallas as pl
from jax.experimental.pallas import tpu as pltpu
from jax.sharding import Mesh
from jax.sharding import PartitionSpec as P

HD = 128
GROUP = 4
FAR = 2
BLOCKS = 8
RING = 8
STATS = 16
PIECE = FAR * HD + STATS
MASKED = -1e30
FLOOR = -1e29
FACTOR = math.log2(math.e) / math.sqrt(HD)
TILE = 2 * HD
TILES = FAR * BLOCKS * HD // TILE
CACHE = 2 * RING * BLOCKS // 2 * HD
VMEM = pl.BlockSpec(memory_space=pltpu.VMEM)
SMEM = pl.BlockSpec(memory_space=pltpu.SMEM)
ANY = pl.BlockSpec(memory_space=pl.ANY)
NT = (((1,), (1,)), ((), ()))
NN = (((1,), (0,)), ((), ()))


def dot(a, b, dims):
    return lax.dot_general(a, b, dims, preferred_element_type=jnp.float32)


def head_order(spans):
    far = [(spans[h] > 4 * HD).astype(jnp.int32) for h in range(GROUP)]
    order = [jnp.int32(0)] * GROUP
    ahead = jnp.int32(0)
    for h in range(GROUP):
        rank = jnp.where(far[h] == 1, ahead, 2 + h - ahead)
        ahead = ahead + far[h]
        order = [jnp.where(rank == s, h, order[s]) for s in range(GROUP)]
    return order


def position():
    return lax.axis_index("k"), lax.axis_index("e"), lax.axis_index("x")


def prepare_kernel(
    spans, queries, keys, values, cache_keys, cache_values, own, sent, handed, near_rows, heads, kinds, sems
):
    sources = [cache_keys, cache_values, keys, values]
    copies = [pltpu.make_async_copy(spans, kinds, sems.at[0])]
    copies.append(pltpu.make_async_copy(queries, heads, sems.at[1]))
    for i in range(4):
        copies.append(
            pltpu.make_async_copy(sources[i], own.at[i * HD : (i + 1) * HD, :], sems.at[2 + i])
        )
    for copy in copies:
        copy.start()
    for copy in copies:
        copy.wait()
    k, e, _ = position()
    ends = (k == RING - 1) & (e == 1)
    handed[...] = jnp.where(ends, own[: 2 * HD, :], own[2 * HD :, :])
    order = head_order(kinds)
    for s in range(GROUP):
        rows = heads[:, pl.ds(pl.multiple_of(order[s] * HD, HD), HD)]
        if s < 2:
            for j in range(BLOCKS):
                sent[j, s] = rows
        else:
            near_rows[(s - 2) * HD : (s - 1) * HD, :] = rows


def place(distance):
    k, e, x = position()
    return ((lax.rem(k + distance + RING, RING) * 2 + e) * 4 + x) * HD


def offsets():
    token = lax.broadcasted_iota(jnp.int32, (HD, TILE), 1)
    return lax.rem(token, HD), token - lax.broadcasted_iota(jnp.int32, (HD, TILE), 0)


def tile_of(t):
    per = TILE // HD
    return t // (BLOCKS // per), t % (BLOCKS // per) * per


def masked_scores(spans, order, offset, key_rows, rows, t, cached, start):
    slot, first = tile_of(t)
    begin = CACHE + lax.axis_index("k") * (BLOCKS * HD) + first * HD
    found = dot(key_rows, rows, NT)
    if cached:
        allowed = offset < spans[order[slot]] - begin + start
    else:
        allowed = offset >= start + CACHE - begin
    return jnp.where(allowed, found, MASKED)


def highest(found):
    return jnp.max(found.reshape(HD // 8, 8, found.shape[1]), axis=0)


def first_kernel(spans, queries, *refs):
    kv = refs[: RING - 1]
    sums, tops, keys, flipped, scores = refs[RING - 1 :]
    order = head_order(spans)
    distances = [0, -1, 1, -2, 2, -3, 3]
    blocks = []
    for i in range(RING - 1):
        for half in range(2):
            n = len(blocks)
            blocks.append((half == 0, place(distances[i])))
            keys[n * HD : (n + 1) * HD, :] = kv[i][2 * half * HD : (2 * half + 1) * HD, :]
            flipped[0:HD, n * HD : (n + 1) * HD] = kv[i][
                (2 * half + 1) * HD : (2 * half + 2) * HD, :
            ].T
    width = len(blocks) * HD
    flipped[HD:, :] = jnp.ones((STATS, width), jnp.bfloat16)
    _, offset = offsets()

    def score(t):
        slot, first = tile_of(t)
        rows = queries[first : first + TILE // HD, slot].reshape(TILE, HD)
        top = jnp.full((8, TILE), FLOOR, jnp.float32)
        for n, (cached, start) in enumerate(blocks):
            found = masked_scores(
                spans, order, offset, keys[n * HD : (n + 1) * HD, :], rows, t, cached, start
            )
            scores[t % 2, n * HD : (n + 1) * HD, :] = found
            top = jnp.maximum(top, highest(found))
        return jnp.max(top, axis=0, keepdims=True)

    def finish(t, top):
        weights = jnp.concatenate(
            [
                jnp.exp2((scores[t % 2, n * HD : (n + 1) * HD, :] - top) * FACTOR).astype(
                    jnp.bfloat16
                )
                for n in range(len(blocks))
            ],
            axis=0,
        )
        sums[t] = dot(flipped[...], weights, NN)
        tops[t] = jnp.broadcast_to(top, (8, TILE))

    top = score(0)
    for t in range(TILES):
        later = score(t + 1) if t + 1 < TILES else None
        finish(t, top)
        top = later


def near_kernel(spans, rows, own, gathered, out, blocks, sems):
    order = head_order(spans)
    _, e, x = position()
    k = lax.axis_index("k")
    copies = []
    for j in range(4):
        at = pl.multiple_of(jnp.where(j < x, 4 * HD, 0), 2 * HD)
        copies.append(
            pltpu.make_async_copy(gathered.at[j, pl.ds(at, 2 * HD), :], blocks.at[j], sems.at[j])
        )
        copies[-1].start()
    for copy in copies:
        copy.wait()
    column, _ = offsets()
    behind = column - lax.broadcasted_iota(jnp.int32, (HD, TILE), 0)
    span = jnp.where(
        lax.broadcasted_iota(jnp.int32, (HD, TILE), 1) < HD, spans[order[2]], spans[order[3]]
    )
    found, values = [], []
    for j in range(5):
        if j < 4:
            distance = jnp.where(j < x, x - j, x - j + 4) * HD
            key_rows, value_rows = blocks[j, :HD, :], blocks[j, HD:, :]
        else:
            distance = 0
            key_rows, value_rows = own[2 * HD : 3 * HD, :], own[3 * HD :, :]
        far = behind + distance
        found.append(
            jnp.where((far >= 0) & (far < span), dot(key_rows, rows[...], NT), MASKED)
        )
        values.append(value_rows)
    top = highest(found[0])
    for j in range(1, 5):
        top = jnp.maximum(top, highest(found[j]))
    top = jnp.max(top, axis=0, keepdims=True)
    weights = jnp.concatenate(
        [jnp.exp2((f - top) * FACTOR).astype(jnp.bfloat16) for f in found], axis=0
    )
    flipped = jnp.concatenate([v.T for v in values], axis=1)
    flipped = jnp.concatenate([flipped, jnp.ones((STATS, 5 * HD), jnp.bfloat16)], axis=0)
    summed = dot(flipped, weights, NN)
    normal = summed[:HD, :] * (1.0 / summed[HD : HD + 1, :])
    for s in range(2):
        out[s] = normal[:, s * HD : (s + 1) * HD].T.astype(jnp.bfloat16)


def write_stats(stats, block, slot, top, total):
    level = jnp.where(total > 0.0, top * FACTOR + jnp.log2(total), MASKED)
    for i in range(3):
        term = level.astype(jnp.bfloat16).astype(jnp.float32)
        stats[block, slot * 4 + i : slot * 4 + i + 1, :] = term
        level = level - term


def second_kernel(spans, queries, last, sums, tops, out, stats):
    order = head_order(spans)
    start = place(4)
    _, offset = offsets()
    ones = jnp.ones((STATS, HD), jnp.bfloat16)
    flipped = jnp.concatenate(
        [
            jnp.concatenate([last[HD : 2 * HD, :].T, ones], axis=0),
            jnp.concatenate([last[3 * HD :, :].T, ones], axis=0),
        ],
        axis=1,
    )
    stats[...] = jnp.zeros_like(stats)
    for t in range(TILES):
        slot, first = tile_of(t)
        rows = queries[first : first + TILE // HD, slot].reshape(TILE, HD)
        found = [
            masked_scores(
                spans, order, offset, last[2 * half * HD : (2 * half + 1) * HD, :],
                rows, t, half == 0, start,
            )
            for half in range(2)
        ]
        before = tops[t, 0:1, :]
        top = jnp.max(jnp.maximum(highest(found[0]), highest(found[1])), axis=0, keepdims=True)
        top = jnp.maximum(top, before)
        weights = [jnp.exp2((f - top) * FACTOR).astype(jnp.bfloat16) for f in found]
        summed = sums[t] * jnp.exp2((before - top) * FACTOR) + dot(
            flipped, jnp.concatenate(weights, axis=0), NN
        )
        total = summed[HD : HD + 1, :]
        normal = summed[:HD, :] * (1.0 / jnp.maximum(total, 1e-30))
        for j in range(TILE // HD):
            cut = slice(j * HD, (j + 1) * HD)
            out[first + j, slot * HD : (slot + 1) * HD, :] = normal[:, cut].astype(jnp.bfloat16)
            write_stats(stats, first + j, slot, top[:, cut], total[:, cut])
    out[:, FAR * HD :, :] = stats[...].astype(jnp.bfloat16)


def project_kernel(spans, parts, near, weight, attn, out):
    order = head_order(spans)
    terms = parts[:, FAR * HD :, :].astype(jnp.float32)
    for s in range(FAR):
        level = [
            terms[i, 4 * s : 4 * s + 1] + terms[i, 4 * s + 1 : 4 * s + 2] + terms[i, 4 * s + 2 : 4 * s + 3]
            for i in range(BLOCKS)
        ]
        top = level[0]
        for i in range(1, BLOCKS):
            top = jnp.maximum(top, level[i])
        share = [jnp.exp2(v - top) for v in level]
        total = share[0]
        for i in range(1, BLOCKS):
            total = total + share[i]
        summed = jnp.zeros((HD, HD), jnp.float32)
        for i in range(BLOCKS):
            summed = summed + parts[i, s * HD : (s + 1) * HD, :].astype(jnp.float32) * share[i]
        attn[:, pl.ds(pl.multiple_of(order[s] * HD, HD), HD)] = (
            (summed * (1.0 / total)).T.astype(jnp.bfloat16)
        )
    for s in range(FAR, GROUP):
        attn[:, pl.ds(pl.multiple_of(order[s] * HD, HD), HD)] = near[s - FAR]
    rows = attn[...]
    other = 1 - lax.axis_index("c")
    width = out.shape[2]
    for f in range(out.shape[0]):
        at = pl.multiple_of((2 * f + other) * width, width)
        out[f] = dot(rows, weight[:, pl.ds(at, width)], NN).astype(jnp.bfloat16)


def add_kernel(attn, weight, received, out):
    rows = attn[...]
    mine = lax.axis_index("c")
    width = out.shape[2]
    for f in range(out.shape[0]):
        at = pl.multiple_of((2 * f + mine) * width, width)
        product = dot(rows, weight[:, pl.ds(at, width)], NN)
        out[f] = (product + received[f].astype(jnp.float32)).astype(jnp.bfloat16)


def total_kernel(shares, out):
    total = shares[0].astype(jnp.float32)
    for i in range(1, shares.shape[0]):
        total = total + shares[i].astype(jnp.float32)
    out[...] = total.T.astype(jnp.bfloat16)


def call(kernel, outs, specs, scratch=(), vmem=24, flops=0, moved=0, exps=0):
    single = not isinstance(outs, list)
    return pl.pallas_call(
        kernel,
        out_shape=outs,
        in_specs=specs,
        out_specs=VMEM if single else [VMEM] * len(outs),
        scratch_shapes=list(scratch),
        compiler_params=pltpu.CompilerParams(vmem_limit_bytes=vmem * 2**20),
        cost_estimate=pl.CostEstimate(flops=flops, bytes_accessed=moved, transcendentals=exps),
    )


def per_device(queries, keys, values, cache_keys, cache_values, spans, out_weight):
    bf16, f32 = jnp.bfloat16, jnp.float32
    own, sent, handed, near_rows = call(
        prepare_kernel,
        [
            jax.ShapeDtypeStruct((4 * HD, HD), bf16),
            jax.ShapeDtypeStruct((BLOCKS, FAR, HD, HD), bf16),
            jax.ShapeDtypeStruct((2 * HD, HD), bf16),
            jax.ShapeDtypeStruct((2 * HD, HD), bf16),
        ],
        [ANY] * 6,
        [
            pltpu.VMEM((HD, GROUP * HD), bf16),
            pltpu.SMEM((GROUP,), jnp.int32),
            pltpu.SemaphoreType.DMA((6,)),
        ],
        moved=2**21,
    )(spans, queries, keys, values, cache_keys, cache_values)
    up_route = [(i, (i + 1) % RING) for i in range(RING)]
    down_route = [(i, (i - 1) % RING) for i in range(RING)]
    grouped = lax.all_to_all(sent, ("e", "x"), 0, 0, tiled=True)
    prior = lax.ppermute(
        handed, ("k", "e"), [(i, (i + 1) % (2 * RING)) for i in range(2 * RING)]
    )
    kv, up, down = [own], own, own
    for _ in range(RING // 2 - 1):
        up = lax.ppermute(up, "k", up_route)
        down = lax.ppermute(down, "k", down_route)
        kv += [up, down]
    last = lax.ppermute(up, "k", up_route)
    gathered = lax.all_gather(jnp.concatenate([prior, own, prior], axis=0), "x", axis=0)
    near = call(
        near_kernel,
        jax.ShapeDtypeStruct((2, HD, HD), bf16),
        [SMEM, VMEM, VMEM, ANY],
        [pltpu.VMEM((4, 2 * HD, HD), bf16), pltpu.SemaphoreType.DMA((4,))],
        flops=4 * 256 * 640 * 128,
        moved=2**19,
        exps=256 * 640,
    )(spans, near_rows, own, gathered)

    far_blocks = 2 * (RING - 1)
    state = call(
        first_kernel,
        [
            jax.ShapeDtypeStruct((TILES, HD + STATS, TILE), f32),
            jax.ShapeDtypeStruct((TILES, 8, TILE), f32),
        ],
        [SMEM] + [VMEM] * RING,
        [
            pltpu.VMEM((far_blocks * HD, HD), bf16),
            pltpu.VMEM((HD + STATS, far_blocks * HD), bf16),
            pltpu.VMEM((2, far_blocks * HD, TILE), f32),
        ],
        flops=4 * 2048 * 1792 * 128,
        moved=4 * 2**20,
        exps=2048 * 1792,
    )(spans, grouped, *kv)
    partial = call(
        second_kernel,
        jax.ShapeDtypeStruct((BLOCKS, PIECE, HD), bf16),
        [SMEM] + [VMEM] * 4,
        [pltpu.VMEM((BLOCKS, STATS, HD), f32)],
        flops=4 * 2048 * 256 * 128,
        moved=4 * 2**20,
        exps=2048 * 256,
    )(spans, grouped, last, *state)
    parts = lax.all_to_all(partial, ("e", "x"), 0, 0, tiled=True)
    width = out_weight.shape[1] // 8
    attn, product = call(
        project_kernel,
        [
            jax.ShapeDtypeStruct((HD, GROUP * HD), bf16),
            jax.ShapeDtypeStruct((4, HD, width), bf16),
        ],
        [SMEM, VMEM, VMEM, VMEM],
        flops=128 * 512 * 4096,
        moved=5 * 2**20,
    )(spans, parts, near, out_weight)
    received = lax.ppermute(product, "c", [(0, 1), (1, 0)])
    halves = call(
        add_kernel,
        jax.ShapeDtypeStruct((4, HD, width), bf16),
        [VMEM] * 3,
        flops=128 * 512 * 4096,
        moved=3 * 2**20,
    )(attn, out_weight, received)
    shares = lax.all_to_all(halves, "y", 0, 0, tiled=True)
    return call(
        total_kernel,
        jax.ShapeDtypeStruct((width, HD), bf16),
        [VMEM],
        moved=2**20,
    )(shares)


def solution(mesh):
    fine = Mesh(mesh.devices.reshape(RING, 2, 4, 4, 2), ("k", "e", "x", "y", "c"))
    seq, head = ("k", "e", "x"), ("y", "c")
    placed = (P(seq, head),) * 5 + (P(head), P(head, None))
    return jax.shard_map(
        per_device, mesh=fine, in_specs=placed, out_specs=P(head, seq), check_vma=False
    )
```

time: 113 us -> 146 us (1.29)
  waiting for transfers between devices: 17.8 us -> 46.4 us
  blocking collectives: 40.5 us -> 12.4 us
  between operations: 0.14 us -> 13.6 us
  starting transfers between devices: 36.8 us -> 48.8 us
  local copies, waits for them, and re-layouts: 4.6 us -> 8.65 us
  Pallas kernels: 12.9 us -> 14.4 us
    all_gather x0 -> x1, waiting for transfers between devices: none -> 32.1 us  [per_device(): lax.all_gather(jnp.concatenate([prior, own, prior], axis=0), 'x', axis=0)]
    all_to_all x2 -> x1, blocking collectives: 40.5 us -> 12.4 us  [per_device(): shares = lax.all_to_all(halves, 'y', 0, 0, tiled=True)]
    ppermute x3, waiting for transfers between devices: 17.6 us -> 8.09 us  [per_device(): up = lax.ppermute(up, 'k', up_route)]
    ppermute x0 -> x2, starting transfers between devices: none -> 6.94 us  [the longest x1 3.62 us: per_device(): received = lax.ppermute(product, 'c', [(0, 1), (1, 0)])]
    ppermute x0 -> x2, waiting for transfers between devices: none -> 6.11 us  [the longest x1 4.6 us: per_device(): lax.ppermute(handed, ('k', 'e'), [(i, (i + 1) % (2 * RING)) for i in rang...]
    all_to_all x0 -> x1, starting transfers between devices: none -> 4.99 us  [per_device(): parts = lax.all_to_all(partial, ('e', 'x'), 0, 0, tiled=True)]
    unnamed x16 -> x22, local copies, waits for them, and re-layouts: 4.6 us -> 8.65 us
    pallas_call x2 -> x4, Pallas kernels: 2.45 us -> 4.06 us  [the longest x1 1.62 us: per_device(): call(near_kernel, jax.ShapeDtypeStruct((2, HD, HD), bf16), [SMEM, VMEM, V...]
  transfers between devices with their start and end apart: 8 -> 12, of which waited for: 3 -> 5; matrix products, arithmetic and copies ran while one was open for 0% -> 1% of each run, Pallas kernels for 5% -> 5%
where the time goes in v3:
time: 146 us; the launch traced here: 145 us
  starting transfers between devices  48.8 us (33%)
  waiting for transfers between devices  46.4 us (32%)
  Pallas kernels  14.4 us (10%)
  between operations  13.6 us (9%)
  blocking collectives  12.4 us (8%)
  local copies, waits for them, and re-layouts  8.65 us (6%)
    all_gather x1, waiting for transfers between devices, per_device(): lax.all_gather(jnp.concatenate([prior, own, prior], axis=0), 'x', axis=0)  32.1 us
    ppermute x3, starting transfers between devices, per_device(): down = lax.ppermute(down, 'k', down_route)  19.1 us
    all_to_all x1, blocking collectives, per_device(): shares = lax.all_to_all(halves, 'y', 0, 0, tiled=True)  12.4 us
    ppermute x3, starting transfers between devices, per_device(): up = lax.ppermute(up, 'k', up_route)  8.72 us
    unnamed x22, local copies, waits for them, and re-layouts  8.65 us
    ppermute x3, waiting for transfers between devices, per_device(): up = lax.ppermute(up, 'k', up_route)  8.09 us
    all_to_all x1, starting transfers between devices, per_device(): grouped = lax.all_to_all(sent, ('e', 'x'), 0, 0, tiled=True)  6.22 us
    pallas_call x1, Pallas kernels, per_device(): call(first_kernel, [jax.ShapeDtypeStruct((TILES, HD + STATS, TILE), f32),...  5.53 us
  transfers between devices with their start and end apart: 12, of which 5 were waited for; matrix products, arithmetic and copies ran while one was open for 1% of the time, Pallas kernels for 5%

profile of v3, /device:TPU:1, one launch (start us, length us, event | category | flops | bytes accessed | tf_op | source)
XLA Modules:
  0.0 145.0 jit_solution(9899317829472651251)
XLA Ops:
  6.5 0.0 copy-start.3
  6.5 0.9 copy-done.3
  7.4 0.0 copy-start.4
  7.4 0.8 copy-done.4
  8.2 0.0 copy-start.5
  8.2 0.8 copy-done.5
  9.0 0.0 copy-start.6
  9.0 0.8 copy-done.6
  9.7 0.0 copy-start.7
  9.7 0.8 copy-done.7
  10.5 0.0 copy-start.8
  10.5 0.7 copy-done.8
  11.1 1.5 %shard_map.73 = (bf16[512,128]{1,0:T(8,128)(2,1)S(1)}, bf16[8,2,128,128]{3,2,1,0:T(8,128)(2,1)}, bf16[256,128]{1,0:T(8,128)(2,1)S(1)}, bf16[256,128]{1,0:T(8,128)(2,1)S(1)}) custom-call(s32[4]{0:T(128)S(1)} %copy-done.8, bf16[128,512]{1,0:T(8,128)(2,1)S(1)} %copy-done.3, bf16[128,128]{1,0:T(8,128)(2,1)S(1)} %copy-done.4, bf16[128,128]{1,0:T(8,128)(2,1)S(1)} %copy-done.5, ...), custom_call_target="tpu_custom_call" | custom-call | bytes 2097152 | tf_op jit(solution)/shard_map/pallas_call | solution.py:313
  12.6 6.2 %all-to-all-start = ((bf16[8,2,128,128]{3,2,1,0:T(8,128)(2,1)}), bf16[8,2,128,128]{3,2,1,0:T(8,128)(2,1)S(1)}, u32[]{:S(2)}, u32[]{:S(2)}) async-start(bf16[8,2,128,128]{3,2,1,0:T(8,128)(2,1)} %get-tuple-element.13), calls=%async_computation | async-start | bytes 1048576 | tf_op jit(solution)/shard_map/all_to_all | solution.py:331
  18.8 0.0 copy-start.10
  18.9 4.9 %collective-permute-start = (bf16[512,128]{1,0:T(8,128)(2,1)S(1)}, bf16[512,128]{1,0:T(8,128)(2,1)S(1)}, u32[]{:S(2)}, u32[]{:S(2)}) collective-permute-start(bf16[512,128]{1,0:T(8,128)(2,1)S(1)} %get-tuple-element.14.refs_0_.own), channel_id=1, source_target_pairs={{0,64},{64,128},{128,192},{192,256},{256,320},{320,384},{384,448},... | collective-permute-start | bytes 393224 | tf_op jit(solution)/shard_map/ppermute | solution.py:337
  23.8 7.7 %collective-permute-start.4 = (bf16[512,128]{1,0:T(8,128)(2,1)S(1)}, bf16[512,128]{1,0:T(8,128)(2,1)S(1)}, u32[]{:S(2)}, u32[]{:S(2)}) collective-permute-start(bf16[512,128]{1,0:T(8,128)(2,1)S(1)} %get-tuple-element.14.refs_0_.own), channel_id=1, source_target_pairs={{0,448},{64,0},{128,64},{192,128},{256,192},{320,256},{384,320},{4... | collective-permute-start | bytes 393224 | tf_op jit(solution)/shard_map/ppermute | solution.py:338
  31.5 7.7 %collective-permute-done.refs_1_ = bf16[512,128]{1,0:T(8,128)(2,1)S(1)} collective-permute-done((bf16[512,128]{1,0:T(8,128)(2,1)S(1)}, bf16[512,128]{1,0:T(8,128)(2,1)S(1)}, u32[]{:S(2)}, u32[]{:S(2)}) %collective-permute-start) | collective-permute-done | bytes 131104 | tf_op jit(solution)/shard_map/ppermute | solution.py:337
  39.1 1.9 %collective-permute-start.1 = (bf16[512,128]{1,0:T(8,128)(2,1)S(1)}, bf16[512,128]{1,0:T(8,128)(2,1)S(1)}, u32[]{:S(2)}, u32[]{:S(2)}) collective-permute-start(bf16[512,128]{1,0:T(8,128)(2,1)S(1)} %collective-permute-done.refs_1_), channel_id=1, source_target_pairs={{0,64},{64,128},{128,192},{192,256},{256,320},{320,384},{384,448},... | collective-permute-start | bytes 393224 | tf_op jit(solution)/shard_map/ppermute | solution.py:337
  41.1 0.0 collective-permute-done.4.refs_2_
  41.1 5.5 %collective-permute-start.5 = (bf16[512,128]{1,0:T(8,128)(2,1)S(1)}, bf16[512,128]{1,0:T(8,128)(2,1)S(1)}, u32[]{:S(2)}, u32[]{:S(2)}) collective-permute-start(bf16[512,128]{1,0:T(8,128)(2,1)S(1)} %collective-permute-done.4.refs_2_), channel_id=1, source_target_pairs={{0,448},{64,0},{128,64},{192,128},{256,192},{320,256},{384,320},{4... | collective-permute-start | bytes 393224 | tf_op jit(solution)/shard_map/ppermute | solution.py:338
  46.5 0.4 collective-permute-done.1.refs_3_
  47.0 1.9 %collective-permute-start.2 = (bf16[512,128]{1,0:T(8,128)(2,1)S(1)}, bf16[512,128]{1,0:T(8,128)(2,1)S(1)}, u32[]{:S(2)}, u32[]{:S(2)}) collective-permute-start(bf16[512,128]{1,0:T(8,128)(2,1)S(1)} %collective-permute-done.1.refs_3_), channel_id=1, source_target_pairs={{0,64},{64,128},{128,192},{192,256},{256,320},{320,384},{384,448},... | collective-permute-start | bytes 393224 | tf_op jit(solution)/shard_map/ppermute | solution.py:337
  48.9 0.0 collective-permute-done.5.refs_4_
  48.9 5.9 %collective-permute-start.6 = (bf16[512,128]{1,0:T(8,128)(2,1)S(1)}, bf16[512,128]{1,0:T(8,128)(2,1)S(1)}, u32[]{:S(2)}, u32[]{:S(2)}) collective-permute-start(bf16[512,128]{1,0:T(8,128)(2,1)S(1)} %collective-permute-done.5.refs_4_), channel_id=1, source_target_pairs={{0,448},{64,0},{128,64},{192,128},{256,192},{320,256},{384,320},{4... | collective-permute-start | bytes 393224 | tf_op jit(solution)/shard_map/ppermute | solution.py:338
  54.8 0.0 collective-permute-done.2.refs_5_
  54.8 2.8 %collective-permute-start.3 = (bf16[512,128]{1,0:T(8,128)(2,1)S(1)}, bf16[512,128]{1,0:T(8,128)(2,1)S(1)}, u32[]{:S(2)}, u32[]{:S(2)}) collective-permute-start(bf16[512,128]{1,0:T(8,128)(2,1)S(1)} %collective-permute-done.2.refs_5_), channel_id=1, source_target_pairs={{0,64},{64,128},{128,192},{192,256},{256,320},{320,384},{384,448},... | collective-permute-start | bytes 393224 | tf_op jit(solution)/shard_map/ppermute | solution.py:340
  57.6 0.0 collective-permute-done.6.refs_6_
  57.7 0.0 all-to-all-done.queries
  57.7 0.0 copy-start.9
  57.7 0.6 copy-done.9
  58.3 5.5 %shard_map.74 = (f32[8,144,256]{2,1,0:T(8,128)S(1)}, f32[8,8,256]{2,1,0:T(8,128)S(1)}) custom-call(s32[4]{0:T(128)S(1)} %copy-done.9, bf16[8,2,128,128]{3,2,1,0:T(8,128)(2,1)S(1)} %all-to-all-done.queries, bf16[512,128]{1,0:T(8,128)(2,1)S(1)} %get-tuple-element.14.refs_0_.own, bf16[512,128]{1,0:T(8,128)(2,1)S(1)} %collective-permute-done.refs_1_, ...), custom_call_target="tpu_custom_call" | custom-call | flops 1879048192 | bytes 4194304 | tf_op jit(solution)/shard_map/pallas_call | solution.py:353
  63.9 0.0 collective-permute-done.3.last
  63.9 3.4 %shard_map.75 = bf16[8,272,128]{2,1,0:T(8,128)(2,1)} custom-call(s32[4]{0:T(128)S(1)} %copy-done.9, bf16[8,2,128,128]{3,2,1,0:T(8,128)(2,1)S(1)} %all-to-all-done.queries, bf16[512,128]{1,0:T(8,128)(2,1)S(1)} %collective-permute-done.3.last, f32[8,144,256]{2,1,0:T(8,128)S(1)} %get-tuple-element.15.sums, f32[8,8,256]{2,1,0:T(8,128)S(1)} %get-tuple-element.16.tops), custom_call_target="tpu_custom_call" | custom-call | flops 268435456 | bytes 4194304 | tf_op jit(solution)/shard_map/pallas_call | solution.py:369
  67.2 5.0 %all-to-all-start.1 = ((bf16[8,272,128]{2,1,0:T(8,128)(2,1)}), bf16[8,272,128]{2,1,0:T(8,128)(2,1)S(1)}, u32[]{:S(2)}, u32[]{:S(2)}) async-start(bf16[8,272,128]{2,1,0:T(8,128)(2,1)} %shard_map.75), calls=%async_computation.1 | async-start | bytes 1114112 | tf_op jit(solution)/shard_map/all_to_all | solution.py:378
  72.2 0.0 all-gather.3.cloned.1.call-start
  72.3 3.3 %collective-permute-start.7 = (bf16[256,128]{1,0:T(8,128)(2,1)S(1)}, bf16[256,128]{1,0:T(8,128)(2,1)S(1)}, u32[]{:S(2)}, u32[]{:S(2)}) collective-permute-start(bf16[256,128]{1,0:T(8,128)(2,1)S(1)} %get-tuple-element.18), channel_id=1, source_target_pairs={{0,32},{32,64},{64,96},{96,128},{128,160},{160,192},{192,224},{224... | collective-permute-start | bytes 196616 | tf_op jit(solution)/shard_map/ppermute | solution.py:332
  75.6 4.6 %collective-permute-done.7 = bf16[256,128]{1,0:T(8,128)(2,1)S(1)} collective-permute-done((bf16[256,128]{1,0:T(8,128)(2,1)S(1)}, bf16[256,128]{1,0:T(8,128)(2,1)S(1)}, u32[]{:S(2)}, u32[]{:S(2)}) %collective-permute-start.7) | collective-permute-done | bytes 65568 | tf_op jit(solution)/shard_map/ppermute | solution.py:332
  80.2 0.7 pad_maximum_fusion
  80.9 0.0 all-gather.3.cloned.1.call-update
  81.0 32.1 %all-gather.3.cloned.1.call-done = bf16[4096,128]{1,0:T(8,128)(2,1)} async-done(((bf16[1024,128]{1,0:T(8,128)(2,1)}), bf16[4096,128]{1,0:T(8,128)(2,1)}) %all-gather.3.cloned.1.call-update) | async-done | bytes 1048592 | tf_op jit(solution)/shard_map/all_gather | solution.py:341
  113.1 0.0 copy-done.10
  113.1 0.0 copy-start.2
  113.1 1.2 copy-done.2
  114.3 1.6 %shard_map.76.near = bf16[2,128,128]{2,1,0:T(8,128)(2,1)S(1)} custom-call(s32[4]{0:T(128)S(1)} %copy-done.10, bf16[256,128]{1,0:T(8,128)(2,1)S(1)} %get-tuple-element.17.rows, bf16[512,128]{1,0:T(8,128)(2,1)S(1)} %get-tuple-element.14.refs_0_.own, bf16[4,1024,128]{2,1,0:T(8,128)(2,1)S(1)} %bitcast.1), custom_call_target="tpu_custom_call" | custom-call | flops 83886080 | bytes 524288 | tf_op jit(solution)/shard_map/pallas_call | solution.py:342
  115.9 0.0 all-to-all-done.1.parts
  116.0 0.0 copy-start
  116.0 2.2 %copy-done = bf16[512,4096]{1,0:T(8,128)(2,1)S(1)} copy-done((bf16[512,4096]{1,0:T(8,128)(2,1)S(1)}, bf16[512,4096]{1,0:T(8,128)(2,1)}, u32[]{:S(2)}) %copy-start) | copy-done | bytes 4194328
  118.1 0.0 copy-start.1
  118.2 1.2 shard_map.77
  119.3 3.6 %collective-permute-start.8 = (bf16[4,128,512]{2,1,0:T(8,128)(2,1)S(1)}, bf16[4,128,512]{2,1,0:T(8,128)(2,1)S(1)}, u32[]{:S(2)}, u32[]{:S(2)}) collective-permute-start(bf16[4,128,512]{2,1,0:T(8,128)(2,1)S(1)} %get-tuple-element.20), channel_id=1, source_target_pairs={{0,1},{1,0},{2,3},{3,2},{4,5},{5,4},{6,7},{7,6},{8,9},{9,8},{10,11... | collective-permute-start | bytes 1572872 | tf_op jit(solution)/shard_map/ppermute | solution.py:390
  122.9 1.5 %collective-permute-done.8.received = bf16[4,128,512]{2,1,0:T(8,128)(2,1)S(1)} collective-permute-done((bf16[4,128,512]{2,1,0:T(8,128)(2,1)S(1)}, bf16[4,128,512]{2,1,0:T(8,128)(2,1)S(1)}, u32[]{:S(2)}, u32[]{:S(2)}) %collective-permute-start.8) | collective-permute-done | bytes 524320 | tf_op jit(solution)/shard_map/ppermute | solution.py:390
  124.5 0.0 copy-done.1
  124.5 0.5 shard_map.78
  125.0 12.4 %all_to_all.15.shares = bf16[4,128,512]{2,1,0:T(8,128)(2,1)S(1)} all-to-all(bf16[4,128,512]{2,1,0:T(8,128)(2,1)S(1)} %shard_map.78), channel_id=1, replica_groups=mesh['k'=8,'e'=2,'x'=4,'y'=4,'c'=2] {'y'}, dimensions={0} | all-to-all | bytes 1048576 | tf_op jit(solution)/shard_map/all_to_all | solution.py:398
  137.4 0.8 shard_map.79
Async XLA Ops:
  6.5 0.9 copy-start.3
  7.4 0.8 copy-start.4
  8.2 0.8 copy-start.5
  9.0 0.8 copy-start.6
  9.7 0.8 copy-start.7
  10.5 0.7 copy-start.8
  12.6 45.0 %all-to-all-start = ((bf16[8,2,128,128]{3,2,1,0:T(8,128)(2,1)}), bf16[8,2,128,128]{3,2,1,0:T(8,128)(2,1)S(1)}, u32[]{:S(2)}, u32[]{:S(2)}) async-start(bf16[8,2,128,128]{3,2,1,0:T(8,128)(2,1)} %get-tuple-element.13), calls=%async_computation | async-start | bytes 1048576 | tf_op jit(solution)/shard_map/all_to_all | solution.py:331
  18.8 94.2 %copy-start.10 = (s32[4]{0:T(128)S(1)}, s32[4]{0:T(128)}, u32[]{:S(2)}) copy-start(s32[4]{0:T(128)} %spans.9) | copy-start | bytes 52
  18.9 20.3 %collective-permute-start = (bf16[512,128]{1,0:T(8,128)(2,1)S(1)}, bf16[512,128]{1,0:T(8,128)(2,1)S(1)}, u32[]{:S(2)}, u32[]{:S(2)}) collective-permute-start(bf16[512,128]{1,0:T(8,128)(2,1)S(1)} %get-tuple-element.14.refs_0_.own), channel_id=1, source_target_pairs={{0,64},{64,128},{128,192},{192,256},{256,320},{320,384},{384,448},... | collective-permute-start | bytes 393224 | tf_op jit(solution)/shard_map/ppermute | solution.py:337
  23.8 17.3 %collective-permute-start.4 = (bf16[512,128]{1,0:T(8,128)(2,1)S(1)}, bf16[512,128]{1,0:T(8,128)(2,1)S(1)}, u32[]{:S(2)}, u32[]{:S(2)}) collective-permute-start(bf16[512,128]{1,0:T(8,128)(2,1)S(1)} %get-tuple-element.14.refs_0_.own), channel_id=1, source_target_pairs={{0,448},{64,0},{128,64},{192,128},{256,192},{320,256},{384,320},{4... | collective-permute-start | bytes 393224 | tf_op jit(solution)/shard_map/ppermute | solution.py:338
  39.1 7.8 %collective-permute-start.1 = (bf16[512,128]{1,0:T(8,128)(2,1)S(1)}, bf16[512,128]{1,0:T(8,128)(2,1)S(1)}, u32[]{:S(2)}, u32[]{:S(2)}) collective-permute-start(bf16[512,128]{1,0:T(8,128)(2,1)S(1)} %collective-permute-done.refs_1_), channel_id=1, source_target_pairs={{0,64},{64,128},{128,192},{192,256},{256,320},{320,384},{384,448},... | collective-permute-start | bytes 393224 | tf_op jit(solution)/shard_map/ppermute | solution.py:337
  41.1 7.8 %collective-permute-start.5 = (bf16[512,128]{1,0:T(8,128)(2,1)S(1)}, bf16[512,128]{1,0:T(8,128)(2,1)S(1)}, u32[]{:S(2)}, u32[]{:S(2)}) collective-permute-start(bf16[512,128]{1,0:T(8,128)(2,1)S(1)} %collective-permute-done.4.refs_2_), channel_id=1, source_target_pairs={{0,448},{64,0},{128,64},{192,128},{256,192},{320,256},{384,320},{4... | collective-permute-start | bytes 393224 | tf_op jit(solution)/shard_map/ppermute | solution.py:338
  47.0 7.9 %collective-permute-start.2 = (bf16[512,128]{1,0:T(8,128)(2,1)S(1)}, bf16[512,128]{1,0:T(8,128)(2,1)S(1)}, u32[]{:S(2)}, u32[]{:S(2)}) collective-permute-start(bf16[512,128]{1,0:T(8,128)(2,1)S(1)} %collective-permute-done.1.refs_3_), channel_id=1, source_target_pairs={{0,64},{64,128},{128,192},{192,256},{256,320},{320,384},{384,448},... | collective-permute-start | bytes 393224 | tf_op jit(solution)/shard_map/ppermute | solution.py:337
  48.9 8.8 %collective-permute-start.6 = (bf16[512,128]{1,0:T(8,128)(2,1)S(1)}, bf16[512,128]{1,0:T(8,128)(2,1)S(1)}, u32[]{:S(2)}, u32[]{:S(2)}) collective-permute-start(bf16[512,128]{1,0:T(8,128)(2,1)S(1)} %collective-permute-done.5.refs_4_), channel_id=1, source_target_pairs={{0,448},{64,0},{128,64},{192,128},{256,192},{320,256},{384,320},{4... | collective-permute-start | bytes 393224 | tf_op jit(solution)/shard_map/ppermute | solution.py:338
  54.8 9.0 %collective-permute-start.3 = (bf16[512,128]{1,0:T(8,128)(2,1)S(1)}, bf16[512,128]{1,0:T(8,128)(2,1)S(1)}, u32[]{:S(2)}, u32[]{:S(2)}) collective-permute-start(bf16[512,128]{1,0:T(8,128)(2,1)S(1)} %collective-permute-done.2.refs_5_), channel_id=1, source_target_pairs={{0,64},{64,128},{128,192},{192,256},{256,320},{320,384},{384,448},... | collective-permute-start | bytes 393224 | tf_op jit(solution)/shard_map/ppermute | solution.py:340
  57.7 0.7 copy-start.9
  67.2 48.7 %all-to-all-start.1 = ((bf16[8,272,128]{2,1,0:T(8,128)(2,1)}), bf16[8,272,128]{2,1,0:T(8,128)(2,1)S(1)}, u32[]{:S(2)}, u32[]{:S(2)}) async-start(bf16[8,272,128]{2,1,0:T(8,128)(2,1)} %shard_map.75), calls=%async_computation.1 | async-start | bytes 1114112 | tf_op jit(solution)/shard_map/all_to_all | solution.py:378
  72.2 40.9 %all-gather.3.cloned.1.call-start = ((), (), s32[]{:S(2)}) async-start(), calls=%async_computation.3 | async-start | bytes 1310720 | tf_op jit(solution)/shard_map/all_gather | solution.py:341
  72.3 7.9 %collective-permute-start.7 = (bf16[256,128]{1,0:T(8,128)(2,1)S(1)}, bf16[256,128]{1,0:T(8,128)(2,1)S(1)}, u32[]{:S(2)}, u32[]{:S(2)}) collective-permute-start(bf16[256,128]{1,0:T(8,128)(2,1)S(1)} %get-tuple-element.18), channel_id=1, source_target_pairs={{0,32},{32,64},{64,96},{96,128},{128,160},{160,192},{192,224},{224... | collective-permute-start | bytes 196616 | tf_op jit(solution)/shard_map/ppermute | solution.py:332
  113.1 1.2 copy-start.2
  116.0 2.2 %copy-start = (bf16[512,4096]{1,0:T(8,128)(2,1)S(1)}, bf16[512,4096]{1,0:T(8,128)(2,1)}, u32[]{:S(2)}) copy-start(bf16[512,4096]{1,0:T(8,128)(2,1)} %weight.3) | copy-start | bytes 12582916
  118.1 6.3 %copy-start.1 = (bf16[512,4096]{1,0:T(8,128)(2,1)S(1)}, bf16[512,4096]{1,0:T(8,128)(2,1)}, u32[]{:S(2)}) copy-start(bf16[512,4096]{1,0:T(8,128)(2,1)} %weight.3) | copy-start | bytes 12582916
  119.3 5.1 %collective-permute-start.8 = (bf16[4,128,512]{2,1,0:T(8,128)(2,1)S(1)}, bf16[4,128,512]{2,1,0:T(8,128)(2,1)S(1)}, u32[]{:S(2)}, u32[]{:S(2)}) collective-permute-start(bf16[4,128,512]{2,1,0:T(8,128)(2,1)S(1)} %get-tuple-element.20), channel_id=1, source_target_pairs={{0,1},{1,0},{2,3},{3,2},{4,5},{5,4},{6,7},{7,6},{8,9},{9,8},{10,11... | collective-permute-start | bytes 1572872 | tf_op jit(solution)/shard_map/ppermute | solution.py:390
Sparse Core Ops, SparseCore 0:
  81.1 31.9 all-gather.2

commit v4 on v3

--- a/solution.py
+++ b/solution.py
@@ -23,7 +23,6 @@
 CACHE = 2 * RING * BLOCKS // 2 * HD
 VMEM = pl.BlockSpec(memory_space=pltpu.VMEM)
 SMEM = pl.BlockSpec(memory_space=pltpu.SMEM)
-ANY = pl.BlockSpec(memory_space=pl.ANY)
 NT = (((1,), (1,)), ((), ()))
 NN = (((1,), (0,)), ((), ()))
 
@@ -47,31 +46,21 @@
     return lax.axis_index("k"), lax.axis_index("e"), lax.axis_index("x")
 
 
-def prepare_kernel(
-    spans, queries, keys, values, cache_keys, cache_values, own, sent, handed, near_rows, heads, kinds, sems
-):
-    sources = [cache_keys, cache_values, keys, values]
-    copies = [pltpu.make_async_copy(spans, kinds, sems.at[0])]
-    copies.append(pltpu.make_async_copy(queries, heads, sems.at[1]))
-    for i in range(4):
-        copies.append(
-            pltpu.make_async_copy(sources[i], own.at[i * HD : (i + 1) * HD, :], sems.at[2 + i])
-        )
-    for copy in copies:
-        copy.start()
-    for copy in copies:
-        copy.wait()
-    k, e, _ = position()
-    ends = (k == RING - 1) & (e == 1)
-    handed[...] = jnp.where(ends, own[: 2 * HD, :], own[2 * HD :, :])
-    order = head_order(kinds)
+def prepare_kernel(spans, queries, own, before, sent, near_rows):
+    order = head_order(spans)
+    k, e, x = position()
+    me = e * 4 + x
+    prior = jnp.where(k == 0, before[: 2 * HD, :], before[2 * HD :, :])
+    block = own[2 * HD :, :]
     for s in range(GROUP):
-        rows = heads[:, pl.ds(pl.multiple_of(order[s] * HD, HD), HD)]
-        if s < 2:
+        rows = queries[:, pl.ds(pl.multiple_of(order[s] * HD, HD), HD)]
+        if s < FAR:
             for j in range(BLOCKS):
-                sent[j, s] = rows
+                sent[j, s * HD : (s + 1) * HD, :] = rows
         else:
-            near_rows[(s - 2) * HD : (s - 1) * HD, :] = rows
+            near_rows[(s - FAR) * HD : (s - FAR + 1) * HD, :] = rows
+    for j in range(BLOCKS):
+        sent[j, FAR * HD :, :] = jnp.where(j > me, block, prior)
 
 
 def place(distance):
@@ -124,7 +113,7 @@
 
     def score(t):
         slot, first = tile_of(t)
-        rows = queries[first : first + TILE // HD, slot].reshape(TILE, HD)
+        rows = queries[first : first + TILE // HD, slot * HD : (slot + 1) * HD, :].reshape(TILE, HD)
         top = jnp.full((8, TILE), FLOOR, jnp.float32)
         for n, (cached, start) in enumerate(blocks):
             found = masked_scores(
@@ -154,19 +143,10 @@
         top = later
 
 
-def near_kernel(spans, rows, own, gathered, out, blocks, sems):
+def near_kernel(spans, rows, own, grouped, out):
     order = head_order(spans)
     _, e, x = position()
-    k = lax.axis_index("k")
-    copies = []
-    for j in range(4):
-        at = pl.multiple_of(jnp.where(j < x, 4 * HD, 0), 2 * HD)
-        copies.append(
-            pltpu.make_async_copy(gathered.at[j, pl.ds(at, 2 * HD), :], blocks.at[j], sems.at[j])
-        )
-        copies[-1].start()
-    for copy in copies:
-        copy.wait()
+    me = e * 4 + x
     column, _ = offsets()
     behind = column - lax.broadcasted_iota(jnp.int32, (HD, TILE), 0)
     span = jnp.where(
@@ -174,17 +154,15 @@
     )
     found, values = [], []
     for j in range(5):
-        if j < 4:
-            distance = jnp.where(j < x, x - j, x - j + 4) * HD
-            key_rows, value_rows = blocks[j, :HD, :], blocks[j, HD:, :]
+        if j:
+            block = grouped[lax.rem(me - j + BLOCKS, BLOCKS), FAR * HD :, :]
         else:
-            distance = 0
-            key_rows, value_rows = own[2 * HD : 3 * HD, :], own[3 * HD :, :]
-        far = behind + distance
+            block = own[2 * HD :, :]
+        far = behind + j * HD
         found.append(
-            jnp.where((far >= 0) & (far < span), dot(key_rows, rows[...], NT), MASKED)
+            jnp.where((far >= 0) & (far < span), dot(block[:HD, :], rows[...], NT), MASKED)
         )
-        values.append(value_rows)
+        values.append(block[HD:, :])
     top = highest(found[0])
     for j in range(1, 5):
         top = jnp.maximum(top, highest(found[j]))
@@ -223,7 +201,7 @@
     stats[...] = jnp.zeros_like(stats)
     for t in range(TILES):
         slot, first = tile_of(t)
-        rows = queries[first : first + TILE // HD, slot].reshape(TILE, HD)
+        rows = queries[first : first + TILE // HD, slot * HD : (slot + 1) * HD, :].reshape(TILE, HD)
         found = [
             masked_scores(
                 spans, order, offset, last[2 * half * HD : (2 * half + 1) * HD, :],
@@ -295,7 +273,7 @@
     out[...] = total.T.astype(jnp.bfloat16)
 
 
-def call(kernel, outs, specs, scratch=(), vmem=24, flops=0, moved=0, exps=0):
+def call(kernel, outs, specs, scratch=(), vmem=12, flops=0, moved=0, exps=0):
     single = not isinstance(outs, list)
     return pl.pallas_call(
         kernel,
@@ -310,44 +288,33 @@
 
 def per_device(queries, keys, values, cache_keys, cache_values, spans, out_weight):
     bf16, f32 = jnp.bfloat16, jnp.float32
-    own, sent, handed, near_rows = call(
-        prepare_kernel,
-        [
-            jax.ShapeDtypeStruct((4 * HD, HD), bf16),
-            jax.ShapeDtypeStruct((BLOCKS, FAR, HD, HD), bf16),
-            jax.ShapeDtypeStruct((2 * HD, HD), bf16),
-            jax.ShapeDtypeStruct((2 * HD, HD), bf16),
-        ],
-        [ANY] * 6,
-        [
-            pltpu.VMEM((HD, GROUP * HD), bf16),
-            pltpu.SMEM((GROUP,), jnp.int32),
-            pltpu.SemaphoreType.DMA((6,)),
-        ],
-        moved=2**21,
-    )(spans, queries, keys, values, cache_keys, cache_values)
+    own = jnp.concatenate([cache_keys, cache_values, keys, values], axis=0)
     up_route = [(i, (i + 1) % RING) for i in range(RING)]
     down_route = [(i, (i - 1) % RING) for i in range(RING)]
-    grouped = lax.all_to_all(sent, ("e", "x"), 0, 0, tiled=True)
-    prior = lax.ppermute(
-        handed, ("k", "e"), [(i, (i + 1) % (2 * RING)) for i in range(2 * RING)]
-    )
     kv, up, down = [own], own, own
     for _ in range(RING // 2 - 1):
         up = lax.ppermute(up, "k", up_route)
         down = lax.ppermute(down, "k", down_route)
         kv += [up, down]
     last = lax.ppermute(up, "k", up_route)
-    gathered = lax.all_gather(jnp.concatenate([prior, own, prior], axis=0), "x", axis=0)
+    sent, near_rows = call(
+        prepare_kernel,
+        [
+            jax.ShapeDtypeStruct((BLOCKS, GROUP * HD, HD), bf16),
+            jax.ShapeDtypeStruct((2 * HD, HD), bf16),
+        ],
+        [SMEM] + [VMEM] * 3,
+        moved=2**21,
+    )(spans, queries, own, kv[1])
+    grouped = lax.all_to_all(sent, ("e", "x"), 0, 0, tiled=True)
     near = call(
         near_kernel,
         jax.ShapeDtypeStruct((2, HD, HD), bf16),
-        [SMEM, VMEM, VMEM, ANY],
-        [pltpu.VMEM((4, 2 * HD, HD), bf16), pltpu.SemaphoreType.DMA((4,))],
+        [SMEM] + [VMEM] * 3,
         flops=4 * 256 * 640 * 128,
         moved=2**19,
         exps=256 * 640,
-    )(spans, near_rows, own, gathered)
+    )(spans, near_rows, own, grouped)
 
     far_blocks = 2 * (RING - 1)
     state = call(

time: 146 us -> 115 us (0.79)
  waiting for transfers between devices: 46.4 us -> 27.6 us
  between operations: 13.6 us -> 0.12 us
  starting transfers between devices: 48.8 us -> 52.2 us
    all_gather x1 -> x0, waiting for transfers between devices: 32.1 us -> none  [per_device(): lax.all_gather(jnp.concatenate([prior, own, prior], axis=0), 'x', axis=0)]
    ppermute x3, waiting for transfers between devices: 8.09 us -> 17.7 us  [per_device(): up = lax.ppermute(up, 'k', up_route)]
    all_to_all x1, waiting for transfers between devices: 0.01 us -> 6.03 us  [per_device(): parts = lax.all_to_all(partial, ('e', 'x'), 0, 0, tiled=True)]
    all_to_all x1, starting transfers between devices: 4.99 us -> 10.1 us  [per_device(): parts = lax.all_to_all(partial, ('e', 'x'), 0, 0, tiled=True)]
    ppermute x1, starting transfers between devices: 3.62 us -> 8.44 us  [per_device(): received = lax.ppermute(product, 'c', [(0, 1), (1, 0)])]
    ppermute x1 -> x0, waiting for transfers between devices: 4.6 us -> none  [per_device(): lax.ppermute(handed, ('k', 'e'), [(i, (i + 1) % (2 * RING)) for i in rang...]
    ppermute x3, starting transfers between devices: 19.1 us -> 15.1 us  [per_device(): down = lax.ppermute(down, 'k', down_route)]
    ppermute x1 -> x0, starting transfers between devices: 3.32 us -> none  [per_device(): lax.ppermute(handed, ('k', 'e'), [(i, (i + 1) % (2 * RING)) for i in rang...]
  transfers between devices with their start and end apart: 12 -> 10, of which waited for: 5 -> 8; matrix products, arithmetic and copies ran while one was open for 1% -> 0% of each run, Pallas kernels for 5% -> 6%
where the time goes in v4:
time: 115 us; the launch traced here: 114 us
  starting transfers between devices  52.2 us (45%)
  waiting for transfers between devices  27.6 us (24%)
  Pallas kernels  14.3 us (12%)
  blocking collectives  12.5 us (11%)
  local copies, waits for them, and re-layouts  7.47 us (6%)
    ppermute x3, waiting for transfers between devices, per_device(): up = lax.ppermute(up, 'k', up_route)  17.7 us
    ppermute x3, starting transfers between devices, per_device(): down = lax.ppermute(down, 'k', down_route)  15.1 us
    all_to_all x1, blocking collectives, per_device(): shares = lax.all_to_all(halves, 'y', 0, 0, tiled=True)  12.5 us
    all_to_all x1, starting transfers between devices, per_device(): parts = lax.all_to_all(partial, ('e', 'x'), 0, 0, tiled=True)  10.1 us
    ppermute x3, starting transfers between devices, per_device(): up = lax.ppermute(up, 'k', up_route)  9.58 us
    ppermute x1, starting transfers between devices, per_device(): received = lax.ppermute(product, 'c', [(0, 1), (1, 0)])  8.44 us
    all_to_all x1, starting transfers between devices, per_device(): grouped = lax.all_to_all(sent, ('e', 'x'), 0, 0, tiled=True)  7.14 us
    unnamed x15, local copies, waits for them, and re-layouts  6.7 us
  transfers between devices with their start and end apart: 10, of which 8 were waited for; matrix products, arithmetic and copies ran while one was open for 0% of the time, Pallas kernels for 6%

profile of v4, /device:TPU:1, one launch (start us, length us, event | category | flops | bytes accessed | tf_op | source)
XLA Modules:
  0.0 114.2 jit_solution(7331698697351260484)
XLA Ops:
  0.0 0.8 constant_dynamic-update-slice_fusion.3
  0.8 0.8 constant_dynamic-update-slice_fusion.2
  1.5 0.8 constant_dynamic-update-slice_fusion.1
  2.3 0.8 constant_dynamic-update-slice_fusion.own.refs_0_
  3.1 5.7 %collective-permute-start = (bf16[512,128]{1,0:T(8,128)(2,1)S(1)}, bf16[512,128]{1,0:T(8,128)(2,1)S(1)}, u32[]{:S(2)}, u32[]{:S(2)}) collective-permute-start(bf16[512,128]{1,0:T(8,128)(2,1)S(1)} %constant_dynamic-update-slice_fusion.own.refs_0_), channel_id=1, source_target_pairs={{0,64},{64,128},{128,192},{192,256},{256,320},{320,384},{384,448},... | collective-permute-start | bytes 393224 | tf_op jit(solution)/shard_map/ppermute | solution.py:296
  8.8 10.5 %collective-permute-done.before.refs_1_ = bf16[512,128]{1,0:T(8,128)(2,1)S(1)} collective-permute-done((bf16[512,128]{1,0:T(8,128)(2,1)S(1)}, bf16[512,128]{1,0:T(8,128)(2,1)S(1)}, u32[]{:S(2)}, u32[]{:S(2)}) %collective-permute-start) | collective-permute-done | bytes 131104 | tf_op jit(solution)/shard_map/ppermute | solution.py:296
  19.2 0.0 copy-start.2
  19.2 0.9 copy-done.2
  20.2 0.0 copy-start.3
  20.2 0.7 copy-done.3
  20.8 1.7 %shard_map.73 = (bf16[8,512,128]{2,1,0:T(8,128)(2,1)}, bf16[256,128]{1,0:T(8,128)(2,1)S(1)}) custom-call(s32[4]{0:T(128)S(1)} %copy-done.3, bf16[128,512]{1,0:T(8,128)(2,1)S(1)} %copy-done.2, bf16[512,128]{1,0:T(8,128)(2,1)S(1)} %constant_dynamic-update-slice_fusion.own.refs_0_, bf16[512,128]{1,0:T(8,128)(2,1)S(1)} %collective-permute-done.before.refs_1_), custom_call_target="tpu_custom_call" | custom-call | bytes 2097152 | tf_op jit(solution)/shard_map/pallas_call | solution.py:300
  22.5 0.0 copy-start.5
  22.5 7.1 %all-to-all-start = ((bf16[8,512,128]{2,1,0:T(8,128)(2,1)}), bf16[8,512,128]{2,1,0:T(8,128)(2,1)S(1)}, u32[]{:S(2)}, u32[]{:S(2)}) async-start(bf16[8,512,128]{2,1,0:T(8,128)(2,1)} %get-tuple-element.11), calls=%async_computation | async-start | bytes 2097152 | tf_op jit(solution)/shard_map/all_to_all | solution.py:309
  29.7 4.2 %collective-permute-start.4 = (bf16[512,128]{1,0:T(8,128)(2,1)S(1)}, bf16[512,128]{1,0:T(8,128)(2,1)S(1)}, u32[]{:S(2)}, u32[]{:S(2)}) collective-permute-start(bf16[512,128]{1,0:T(8,128)(2,1)S(1)} %constant_dynamic-update-slice_fusion.own.refs_0_), channel_id=1, source_target_pairs={{0,448},{64,0},{128,64},{192,128},{256,192},{320,256},{384,320},{4... | collective-permute-start | bytes 393224 | tf_op jit(solution)/shard_map/ppermute | solution.py:297
  33.9 2.0 %collective-permute-start.1 = (bf16[512,128]{1,0:T(8,128)(2,1)S(1)}, bf16[512,128]{1,0:T(8,128)(2,1)S(1)}, u32[]{:S(2)}, u32[]{:S(2)}) collective-permute-start(bf16[512,128]{1,0:T(8,128)(2,1)S(1)} %collective-permute-done.before.refs_1_), channel_id=1, source_target_pairs={{0,64},{64,128},{128,192},{192,256},{256,320},{320,384},{384,448},... | collective-permute-start | bytes 393224 | tf_op jit(solution)/shard_map/ppermute | solution.py:296
  35.8 0.8 collective-permute-done.4.refs_2_
  36.6 5.4 %collective-permute-start.5 = (bf16[512,128]{1,0:T(8,128)(2,1)S(1)}, bf16[512,128]{1,0:T(8,128)(2,1)S(1)}, u32[]{:S(2)}, u32[]{:S(2)}) collective-permute-start(bf16[512,128]{1,0:T(8,128)(2,1)S(1)} %collective-permute-done.4.refs_2_), channel_id=1, source_target_pairs={{0,448},{64,0},{128,64},{192,128},{256,192},{320,256},{384,320},{4... | collective-permute-start | bytes 393224 | tf_op jit(solution)/shard_map/ppermute | solution.py:297
  42.0 6.8 %collective-permute-done.1.refs_3_ = bf16[512,128]{1,0:T(8,128)(2,1)S(1)} collective-permute-done((bf16[512,128]{1,0:T(8,128)(2,1)S(1)}, bf16[512,128]{1,0:T(8,128)(2,1)S(1)}, u32[]{:S(2)}, u32[]{:S(2)}) %collective-permute-start.1) | collective-permute-done | bytes 131104 | tf_op jit(solution)/shard_map/ppermute | solution.py:296
  48.8 1.9 %collective-permute-start.2 = (bf16[512,128]{1,0:T(8,128)(2,1)S(1)}, bf16[512,128]{1,0:T(8,128)(2,1)S(1)}, u32[]{:S(2)}, u32[]{:S(2)}) collective-permute-start(bf16[512,128]{1,0:T(8,128)(2,1)S(1)} %collective-permute-done.1.refs_3_), channel_id=1, source_target_pairs={{0,64},{64,128},{128,192},{192,256},{256,320},{320,384},{384,448},... | collective-permute-start | bytes 393224 | tf_op jit(solution)/shard_map/ppermute | solution.py:296
  50.7 0.0 collective-permute-done.5.refs_4_
  50.7 5.5 %collective-permute-start.6 = (bf16[512,128]{1,0:T(8,128)(2,1)S(1)}, bf16[512,128]{1,0:T(8,128)(2,1)S(1)}, u32[]{:S(2)}, u32[]{:S(2)}) collective-permute-start(bf16[512,128]{1,0:T(8,128)(2,1)S(1)} %collective-permute-done.5.refs_4_), channel_id=1, source_target_pairs={{0,448},{64,0},{128,64},{192,128},{256,192},{320,256},{384,320},{4... | collective-permute-start | bytes 393224 | tf_op jit(solution)/shard_map/ppermute | solution.py:297
  56.2 0.4 collective-permute-done.2.refs_5_
  56.6 1.9 %collective-permute-start.3 = (bf16[512,128]{1,0:T(8,128)(2,1)S(1)}, bf16[512,128]{1,0:T(8,128)(2,1)S(1)}, u32[]{:S(2)}, u32[]{:S(2)}) collective-permute-start(bf16[512,128]{1,0:T(8,128)(2,1)S(1)} %collective-permute-done.2.refs_5_), channel_id=1, source_target_pairs={{0,64},{64,128},{128,192},{192,256},{256,320},{320,384},{384,448},... | collective-permute-start | bytes 393224 | tf_op jit(solution)/shard_map/ppermute | solution.py:299
  58.5 0.9 collective-permute-done.6.refs_6_
  59.5 0.0 all-to-all-done.queries.grouped
  59.5 0.0 copy-start.4
  59.5 0.7 copy-done.4
  60.1 5.5 %shard_map.74 = (f32[8,144,256]{2,1,0:T(8,128)S(1)}, f32[8,8,256]{2,1,0:T(8,128)S(1)}) custom-call(s32[4]{0:T(128)S(1)} %copy-done.4, bf16[8,512,128]{2,1,0:T(8,128)(2,1)S(1)} %all-to-all-done.queries.grouped, bf16[512,128]{1,0:T(8,128)(2,1)S(1)} %constant_dynamic-update-slice_fusion.own.refs_0_, bf16[512,128]{1,0:T(8,128)(2,1)S(1)} %collective-permute-done.before.refs_1_, ...), custom_call_target="tpu_custom_call" | custom-call | flops 1879048192 | bytes 4194304 | tf_op jit(solution)/shard_map/pallas_call | solution.py:320
  65.7 0.6 collective-permute-done.3.last
  66.3 3.3 %shard_map.75 = bf16[8,272,128]{2,1,0:T(8,128)(2,1)} custom-call(s32[4]{0:T(128)S(1)} %copy-done.4, bf16[8,512,128]{2,1,0:T(8,128)(2,1)S(1)} %all-to-all-done.queries.grouped, bf16[512,128]{1,0:T(8,128)(2,1)S(1)} %collective-permute-done.3.last, f32[8,144,256]{2,1,0:T(8,128)S(1)} %get-tuple-element.12.sums, f32[8,8,256]{2,1,0:T(8,128)S(1)} %get-tuple-element.13.tops), custom_call_target="tpu_custom_call" | custom-call | flops 268435456 | bytes 4194304 | tf_op jit(solution)/shard_map/pallas_call | solution.py:336
  69.7 10.1 %all-to-all-start.1 = ((bf16[8,272,128]{2,1,0:T(8,128)(2,1)}), bf16[8,272,128]{2,1,0:T(8,128)(2,1)S(1)}, u32[]{:S(2)}, u32[]{:S(2)}) async-start(bf16[8,272,128]{2,1,0:T(8,128)(2,1)} %shard_map.75), calls=%async_computation.1 | async-start | bytes 1114112 | tf_op jit(solution)/shard_map/all_to_all | solution.py:345
  79.8 0.0 copy-done.5
  79.8 1.2 %shard_map.76.near = bf16[2,128,128]{2,1,0:T(8,128)(2,1)S(1)} custom-call(s32[4]{0:T(128)S(1)} %copy-done.5, bf16[256,128]{1,0:T(8,128)(2,1)S(1)} %get-tuple-element.14.rows, bf16[512,128]{1,0:T(8,128)(2,1)S(1)} %constant_dynamic-update-slice_fusion.own.refs_0_, bf16[8,512,128]{2,1,0:T(8,128)(2,1)S(1)} %all-to-all-done.queries.grouped), custom_call_target="tpu_custom_call" | custom-call | flops 83886080 | bytes 524288 | tf_op jit(solution)/shard_map/pallas_call | solution.py:310
  81.0 6.0 %all-to-all-done.1.parts = bf16[8,272,128]{2,1,0:T(8,128)(2,1)S(1)} async-done(((bf16[8,272,128]{2,1,0:T(8,128)(2,1)}), bf16[8,272,128]{2,1,0:T(8,128)(2,1)S(1)}, u32[]{:S(2)}, u32[]{:S(2)}) %all-to-all-start.1) | async-done | bytes 557088 | tf_op jit(solution)/shard_map/all_to_all | solution.py:345
  87.0 0.0 copy-start
  87.0 2.2 %copy-done = bf16[512,4096]{1,0:T(8,128)(2,1)S(1)} copy-done((bf16[512,4096]{1,0:T(8,128)(2,1)S(1)}, bf16[512,4096]{1,0:T(8,128)(2,1)}, u32[]{:S(2)}) %copy-start) | copy-done | bytes 4194328
  89.2 0.0 copy-start.1
  89.2 1.2 %shard_map.77 = (bf16[128,512]{1,0:T(8,128)(2,1)S(1)}, bf16[4,128,512]{2,1,0:T(8,128)(2,1)S(1)}) custom-call(s32[4]{0:T(128)S(1)} %copy-done.5, bf16[8,272,128]{2,1,0:T(8,128)(2,1)S(1)} %all-to-all-done.1.parts, bf16[2,128,128]{2,1,0:T(8,128)(2,1)S(1)} %shard_map.76.near, bf16[512,4096]{1,0:T(8,128)(2,1)S(1)} %copy-done), custom_call_target="tpu_custom_call" | custom-call | flops 268435456 | bytes 5242880 | tf_op jit(solution)/shard_map/pallas_call | solution.py:347
  90.4 8.4 %collective-permute-start.7 = (bf16[4,128,512]{2,1,0:T(8,128)(2,1)S(1)}, bf16[4,128,512]{2,1,0:T(8,128)(2,1)S(1)}, u32[]{:S(2)}, u32[]{:S(2)}) collective-permute-start(bf16[4,128,512]{2,1,0:T(8,128)(2,1)S(1)} %get-tuple-element.16), channel_id=1, source_target_pairs={{0,1},{1,0},{2,3},{3,2},{4,5},{5,4},{6,7},{7,6},{8,9},{9,8},{10,11... | collective-permute-start | bytes 1572872 | tf_op jit(solution)/shard_map/ppermute | solution.py:357
  98.8 1.5 %collective-permute-done.7.received = bf16[4,128,512]{2,1,0:T(8,128)(2,1)S(1)} collective-permute-done((bf16[4,128,512]{2,1,0:T(8,128)(2,1)S(1)}, bf16[4,128,512]{2,1,0:T(8,128)(2,1)S(1)}, u32[]{:S(2)}, u32[]{:S(2)}) %collective-permute-start.7) | collective-permute-done | bytes 524320 | tf_op jit(solution)/shard_map/ppermute | solution.py:357
  100.3 0.0 copy-done.1
  100.3 0.5 shard_map.78
  100.8 12.5 %all_to_all.15.shares = bf16[4,128,512]{2,1,0:T(8,128)(2,1)S(1)} all-to-all(bf16[4,128,512]{2,1,0:T(8,128)(2,1)S(1)} %shard_map.78), channel_id=1, replica_groups=mesh['k'=8,'e'=2,'x'=4,'y'=4,'c'=2] {'y'}, dimensions={0} | all-to-all | bytes 1048576 | tf_op jit(solution)/shard_map/all_to_all | solution.py:365
  113.4 0.8 shard_map.79
Async XLA Ops:
  3.1 16.2 %collective-permute-start = (bf16[512,128]{1,0:T(8,128)(2,1)S(1)}, bf16[512,128]{1,0:T(8,128)(2,1)S(1)}, u32[]{:S(2)}, u32[]{:S(2)}) collective-permute-start(bf16[512,128]{1,0:T(8,128)(2,1)S(1)} %constant_dynamic-update-slice_fusion.own.refs_0_), channel_id=1, source_target_pairs={{0,64},{64,128},{128,192},{192,256},{256,320},{320,384},{384,448},... | collective-permute-start | bytes 393224 | tf_op jit(solution)/shard_map/ppermute | solution.py:296
  19.2 0.9 copy-start.2
  20.2 0.7 copy-start.3
  22.5 57.2 %copy-start.5 = (s32[4]{0:T(128)S(1)}, s32[4]{0:T(128)}, u32[]{:S(2)}) copy-start(s32[4]{0:T(128)} %spans.9) | copy-start | bytes 52
  22.5 37.0 %all-to-all-start = ((bf16[8,512,128]{2,1,0:T(8,128)(2,1)}), bf16[8,512,128]{2,1,0:T(8,128)(2,1)S(1)}, u32[]{:S(2)}, u32[]{:S(2)}) async-start(bf16[8,512,128]{2,1,0:T(8,128)(2,1)} %get-tuple-element.11), calls=%async_computation | async-start | bytes 2097152 | tf_op jit(solution)/shard_map/all_to_all | solution.py:309
  29.7 6.9 %collective-permute-start.4 = (bf16[512,128]{1,0:T(8,128)(2,1)S(1)}, bf16[512,128]{1,0:T(8,128)(2,1)S(1)}, u32[]{:S(2)}, u32[]{:S(2)}) collective-permute-start(bf16[512,128]{1,0:T(8,128)(2,1)S(1)} %constant_dynamic-update-slice_fusion.own.refs_0_), channel_id=1, source_target_pairs={{0,448},{64,0},{128,64},{192,128},{256,192},{320,256},{384,320},{4... | collective-permute-start | bytes 393224 | tf_op jit(solution)/shard_map/ppermute | solution.py:297
  33.9 14.9 %collective-permute-start.1 = (bf16[512,128]{1,0:T(8,128)(2,1)S(1)}, bf16[512,128]{1,0:T(8,128)(2,1)S(1)}, u32[]{:S(2)}, u32[]{:S(2)}) collective-permute-start(bf16[512,128]{1,0:T(8,128)(2,1)S(1)} %collective-permute-done.before.refs_1_), channel_id=1, source_target_pairs={{0,64},{64,128},{128,192},{192,256},{256,320},{320,384},{384,448},... | collective-permute-start | bytes 393224 | tf_op jit(solution)/shard_map/ppermute | solution.py:296
  36.6 14.1 %collective-permute-start.5 = (bf16[512,128]{1,0:T(8,128)(2,1)S(1)}, bf16[512,128]{1,0:T(8,128)(2,1)S(1)}, u32[]{:S(2)}, u32[]{:S(2)}) collective-permute-start(bf16[512,128]{1,0:T(8,128)(2,1)S(1)} %collective-permute-done.4.refs_2_), channel_id=1, source_target_pairs={{0,448},{64,0},{128,64},{192,128},{256,192},{320,256},{384,320},{4... | collective-permute-start | bytes 393224 | tf_op jit(solution)/shard_map/ppermute | solution.py:297
  48.8 7.8 %collective-permute-start.2 = (bf16[512,128]{1,0:T(8,128)(2,1)S(1)}, bf16[512,128]{1,0:T(8,128)(2,1)S(1)}, u32[]{:S(2)}, u32[]{:S(2)}) collective-permute-start(bf16[512,128]{1,0:T(8,128)(2,1)S(1)} %collective-permute-done.1.refs_3_), channel_id=1, source_target_pairs={{0,64},{64,128},{128,192},{192,256},{256,320},{320,384},{384,448},... | collective-permute-start | bytes 393224 | tf_op jit(solution)/shard_map/ppermute | solution.py:296
  50.7 8.7 %collective-permute-start.6 = (bf16[512,128]{1,0:T(8,128)(2,1)S(1)}, bf16[512,128]{1,0:T(8,128)(2,1)S(1)}, u32[]{:S(2)}, u32[]{:S(2)}) collective-permute-start(bf16[512,128]{1,0:T(8,128)(2,1)S(1)} %collective-permute-done.5.refs_4_), channel_id=1, source_target_pairs={{0,448},{64,0},{128,64},{192,128},{256,192},{320,256},{384,320},{4... | collective-permute-start | bytes 393224 | tf_op jit(solution)/shard_map/ppermute | solution.py:297
  56.6 9.7 %collective-permute-start.3 = (bf16[512,128]{1,0:T(8,128)(2,1)S(1)}, bf16[512,128]{1,0:T(8,128)(2,1)S(1)}, u32[]{:S(2)}, u32[]{:S(2)}) collective-permute-start(bf16[512,128]{1,0:T(8,128)(2,1)S(1)} %collective-permute-done.2.refs_5_), channel_id=1, source_target_pairs={{0,64},{64,128},{128,192},{192,256},{256,320},{320,384},{384,448},... | collective-permute-start | bytes 393224 | tf_op jit(solution)/shard_map/ppermute | solution.py:299
  59.5 0.7 copy-start.4
  69.7 17.4 %all-to-all-start.1 = ((bf16[8,272,128]{2,1,0:T(8,128)(2,1)}), bf16[8,272,128]{2,1,0:T(8,128)(2,1)S(1)}, u32[]{:S(2)}, u32[]{:S(2)}) async-start(bf16[8,272,128]{2,1,0:T(8,128)(2,1)} %shard_map.75), calls=%async_computation.1 | async-start | bytes 1114112 | tf_op jit(solution)/shard_map/all_to_all | solution.py:345
  87.0 2.2 %copy-start = (bf16[512,4096]{1,0:T(8,128)(2,1)S(1)}, bf16[512,4096]{1,0:T(8,128)(2,1)}, u32[]{:S(2)}) copy-start(bf16[512,4096]{1,0:T(8,128)(2,1)} %weight.3) | copy-start | bytes 12582916
  89.2 11.1 %copy-start.1 = (bf16[512,4096]{1,0:T(8,128)(2,1)S(1)}, bf16[512,4096]{1,0:T(8,128)(2,1)}, u32[]{:S(2)}) copy-start(bf16[512,4096]{1,0:T(8,128)(2,1)} %weight.3) | copy-start | bytes 12582916
  90.4 10.0 %collective-permute-start.7 = (bf16[4,128,512]{2,1,0:T(8,128)(2,1)S(1)}, bf16[4,128,512]{2,1,0:T(8,128)(2,1)S(1)}, u32[]{:S(2)}, u32[]{:S(2)}) collective-permute-start(bf16[4,128,512]{2,1,0:T(8,128)(2,1)S(1)} %get-tuple-element.16), channel_id=1, source_target_pairs={{0,1},{1,0},{2,3},{3,2},{4,5},{5,4},{6,7},{7,6},{8,9},{9,8},{10,11... | collective-permute-start | bytes 1572872 | tf_op jit(solution)/shard_map/ppermute | solution.py:357

commit v5 on v4

--- a/solution.py
+++ b/solution.py
@@ -23,6 +23,7 @@
 CACHE = 2 * RING * BLOCKS // 2 * HD
 VMEM = pl.BlockSpec(memory_space=pltpu.VMEM)
 SMEM = pl.BlockSpec(memory_space=pltpu.SMEM)
+ANY = pl.BlockSpec(memory_space=pl.ANY)
 NT = (((1,), (1,)), ((), ()))
 NN = (((1,), (0,)), ((), ()))
 
@@ -46,21 +47,39 @@
     return lax.axis_index("k"), lax.axis_index("e"), lax.axis_index("x")
 
 
-def prepare_kernel(spans, queries, own, before, sent, near_rows):
-    order = head_order(spans)
-    k, e, x = position()
-    me = e * 4 + x
-    prior = jnp.where(k == 0, before[: 2 * HD, :], before[2 * HD :, :])
-    block = own[2 * HD :, :]
+def prepare_kernel(
+    spans, queries, keys, values, cache_keys, cache_values, own, sent, near_rows, heads, kinds, sems
+):
+    copies = [
+        pltpu.make_async_copy(spans, kinds, sems.at[0]),
+        pltpu.make_async_copy(queries, heads, sems.at[1]),
+    ]
+    for i, source in enumerate([cache_keys, cache_values, keys, values]):
+        copies.append(
+            pltpu.make_async_copy(source, own.at[i * HD : (i + 1) * HD, :], sems.at[2 + i])
+        )
+    for copy in copies:
+        copy.start()
+    for copy in copies:
+        copy.wait()
+    order = head_order(kinds)
     for s in range(GROUP):
-        rows = queries[:, pl.ds(pl.multiple_of(order[s] * HD, HD), HD)]
+        rows = heads[:, pl.ds(pl.multiple_of(order[s] * HD, HD), HD)]
         if s < FAR:
             for j in range(BLOCKS):
                 sent[j, s * HD : (s + 1) * HD, :] = rows
         else:
             near_rows[(s - FAR) * HD : (s - FAR + 1) * HD, :] = rows
+
+
+def hand_kernel(own, before, sent, held):
+    k, e, x = position()
+    me = e * 4 + x
+    prior = jnp.where(k == 0, before[: 2 * HD, :], before[2 * HD :, :])
+    block = own[2 * HD :, :]
     for j in range(BLOCKS):
-        sent[j, FAR * HD :, :] = jnp.where(j > me, block, prior)
+        sent[j] = jnp.where(j > me, block, prior)
+    held[...] = own[...]
 
 
 def place(distance):
@@ -155,7 +174,7 @@
     found, values = [], []
     for j in range(5):
         if j:
-            block = grouped[lax.rem(me - j + BLOCKS, BLOCKS), FAR * HD :, :]
+            block = grouped[lax.rem(me - j + BLOCKS, BLOCKS)]
         else:
             block = own[2 * HD :, :]
         far = behind + j * HD
@@ -225,7 +244,17 @@
     out[:, FAR * HD :, :] = stats[...].astype(jnp.bfloat16)
 
 
-def project_kernel(spans, parts, near, weight, attn, out):
+def project_kernel(spans, parts, near, weight, out, kept, attn, columns, sems):
+    mine = lax.axis_index("c")
+    width = out.shape[2]
+    copies = []
+    for i in range(2 * out.shape[0]):
+        core = mine if i >= out.shape[0] else 1 - mine
+        at = pl.multiple_of((2 * (i % out.shape[0]) + core) * width, width)
+        copies.append(
+            pltpu.make_async_copy(weight.at[:, pl.ds(at, width)], columns.at[i], sems.at[i])
+        )
+        copies[-1].start()
     order = head_order(spans)
     terms = parts[:, FAR * HD :, :].astype(jnp.float32)
     for s in range(FAR):
@@ -249,21 +278,14 @@
     for s in range(FAR, GROUP):
         attn[:, pl.ds(pl.multiple_of(order[s] * HD, HD), HD)] = near[s - FAR]
     rows = attn[...]
-    other = 1 - lax.axis_index("c")
-    width = out.shape[2]
-    for f in range(out.shape[0]):
-        at = pl.multiple_of((2 * f + other) * width, width)
-        out[f] = dot(rows, weight[:, pl.ds(at, width)], NN).astype(jnp.bfloat16)
-
-
-def add_kernel(attn, weight, received, out):
-    rows = attn[...]
-    mine = lax.axis_index("c")
-    width = out.shape[2]
-    for f in range(out.shape[0]):
-        at = pl.multiple_of((2 * f + mine) * width, width)
-        product = dot(rows, weight[:, pl.ds(at, width)], NN)
-        out[f] = (product + received[f].astype(jnp.float32)).astype(jnp.bfloat16)
+    for i, copy in enumerate(copies):
+        target = kept if i >= out.shape[0] else out
+        copy.wait()
+        target[i % out.shape[0]] = dot(rows, columns[i], NN).astype(target.dtype)
+
+
+def add_kernel(kept, received, out):
+    out[...] = (kept[...] + received[...].astype(jnp.float32)).astype(jnp.bfloat16)
 
 
 def total_kernel(shares, out):
@@ -273,7 +295,7 @@
     out[...] = total.T.astype(jnp.bfloat16)
 
 
-def call(kernel, outs, specs, scratch=(), vmem=12, flops=0, moved=0, exps=0):
+def call(kernel, outs, specs, scratch=(), vmem=24, flops=0, moved=0, exps=0):
     single = not isinstance(outs, list)
     return pl.pallas_call(
         kernel,
@@ -288,34 +310,42 @@
 
 def per_device(queries, keys, values, cache_keys, cache_values, spans, out_weight):
     bf16, f32 = jnp.bfloat16, jnp.float32
-    own = jnp.concatenate([cache_keys, cache_values, keys, values], axis=0)
+    own, sent, near_rows = call(
+        prepare_kernel,
+        [
+            jax.ShapeDtypeStruct((4 * HD, HD), bf16),
+            jax.ShapeDtypeStruct((BLOCKS, FAR * HD, HD), bf16),
+            jax.ShapeDtypeStruct((2 * HD, HD), bf16),
+        ],
+        [ANY] * 6,
+        [
+            pltpu.VMEM((HD, GROUP * HD), bf16),
+            pltpu.SMEM((GROUP,), jnp.int32),
+            pltpu.SemaphoreType.DMA((6,)),
+        ],
+        vmem=52,
+        moved=2**21,
+    )(spans, queries, keys, values, cache_keys, cache_values)
+    grouped = lax.all_to_all(sent, ("e", "x"), 0, 0, tiled=True)
     up_route = [(i, (i + 1) % RING) for i in range(RING)]
     down_route = [(i, (i - 1) % RING) for i in range(RING)]
     kv, up, down = [own], own, own
     for _ in range(RING // 2 - 1):
         up = lax.ppermute(up, "k", up_route)
         down = lax.ppermute(down, "k", down_route)
+        up, down = lax.optimization_barrier((up, down))
         kv += [up, down]
     last = lax.ppermute(up, "k", up_route)
-    sent, near_rows = call(
-        prepare_kernel,
-        [
-            jax.ShapeDtypeStruct((BLOCKS, GROUP * HD, HD), bf16),
-            jax.ShapeDtypeStruct((2 * HD, HD), bf16),
-        ],
-        [SMEM] + [VMEM] * 3,
-        moved=2**21,
-    )(spans, queries, own, kv[1])
-    grouped = lax.all_to_all(sent, ("e", "x"), 0, 0, tiled=True)
-    near = call(
-        near_kernel,
-        jax.ShapeDtypeStruct((2, HD, HD), bf16),
-        [SMEM] + [VMEM] * 3,
-        flops=4 * 256 * 640 * 128,
-        moved=2**19,
-        exps=256 * 640,
-    )(spans, near_rows, own, grouped)
-
+    handed, held = call(
+        hand_kernel,
+        [
+            jax.ShapeDtypeStruct((BLOCKS, 2 * HD, HD), bf16),
+            jax.ShapeDtypeStruct((4 * HD, HD), bf16),
+        ],
+        [VMEM] * 2,
+        moved=2**20,
+    )(own, kv[1])
+    kv[0] = held
     far_blocks = 2 * (RING - 1)
     state = call(
         first_kernel,
@@ -333,6 +363,8 @@
         moved=4 * 2**20,
         exps=2048 * 1792,
     )(spans, grouped, *kv)
+    handed, last, state = lax.optimization_barrier((handed, last, state))
+    blocks = lax.all_to_all(handed, ("e", "x"), 0, 0, tiled=True)
     partial = call(
         second_kernel,
         jax.ShapeDtypeStruct((BLOCKS, PIECE, HD), bf16),
@@ -343,25 +375,38 @@
         exps=2048 * 256,
     )(spans, grouped, last, *state)
     parts = lax.all_to_all(partial, ("e", "x"), 0, 0, tiled=True)
+    near = call(
+        near_kernel,
+        jax.ShapeDtypeStruct((2, HD, HD), bf16),
+        [SMEM] + [VMEM] * 3,
+        flops=4 * 256 * 640 * 128,
+        moved=2**20,
+        exps=256 * 640,
+    )(spans, near_rows, held, blocks)
     width = out_weight.shape[1] // 8
-    attn, product = call(
+    product, kept = call(
         project_kernel,
         [
-            jax.ShapeDtypeStruct((HD, GROUP * HD), bf16),
             jax.ShapeDtypeStruct((4, HD, width), bf16),
-        ],
-        [SMEM, VMEM, VMEM, VMEM],
-        flops=128 * 512 * 4096,
+            jax.ShapeDtypeStruct((4, HD, width), f32),
+        ],
+        [SMEM, VMEM, VMEM, ANY],
+        [
+            pltpu.VMEM((HD, GROUP * HD), bf16),
+            pltpu.VMEM((8, GROUP * HD, width), bf16),
+            pltpu.SemaphoreType.DMA((8,)),
+        ],
+        vmem=52,
+        flops=2 * 128 * 512 * 4096,
         moved=5 * 2**20,
     )(spans, parts, near, out_weight)
     received = lax.ppermute(product, "c", [(0, 1), (1, 0)])
     halves = call(
         add_kernel,
         jax.ShapeDtypeStruct((4, HD, width), bf16),
-        [VMEM] * 3,
-        flops=128 * 512 * 4096,
-        moved=3 * 2**20,
-    )(attn, out_weight, received)
+        [VMEM] * 2,
+        moved=2 * 2**20,
+    )(kept, received)
     shares = lax.all_to_all(halves, "y", 0, 0, tiled=True)
     return call(
         total_kernel,

time: 115 us -> 121 us (1.052)
  starting transfers between devices: 52.2 us -> 58.1 us
  Pallas kernels: 14.3 us -> 18 us
  waiting for transfers between devices: 27.6 us -> 24.7 us
    all_to_all x0 -> x1, starting transfers between devices: none -> 7.7 us  [per_device(): blocks = lax.all_to_all(handed, ('e', 'x'), 0, 0, tiled=True)]
    ppermute x3, waiting for transfers between devices: 17.7 us -> 10.1 us  [per_device(): up = lax.ppermute(up, 'k', up_route)]
    all_to_all x1, starting transfers between devices: 10.1 us -> 3.54 us  [per_device(): parts = lax.all_to_all(partial, ('e', 'x'), 0, 0, tiled=True)]
    pallas_call x3 -> x4, Pallas kernels: 3.36 us -> 7.16 us  [the longest x1 4.67 us: per_device(): call(project_kernel, [jax.ShapeDtypeStruct((4, HD, width), bf16), jax.Sha...]
    all_to_all x0 -> x1, waiting for transfers between devices: none -> 3.77 us  [per_device(): blocks = lax.all_to_all(handed, ('e', 'x'), 0, 0, tiled=True)]
    ppermute x3, starting transfers between devices: 15.1 us -> 18.4 us  [per_device(): down = lax.ppermute(down, 'k', down_route)]
    ppermute x1, starting transfers between devices: 8.44 us -> 10 us  [per_device(): received = lax.ppermute(product, 'c', [(0, 1), (1, 0)])]
    ppermute x1, starting transfers between devices: 1.91 us -> 3.22 us  [per_device(): last = lax.ppermute(up, 'k', up_route)]
  transfers between devices with their start and end apart: 10 -> 11, of which waited for: 8 -> 9; matrix products, arithmetic and copies ran while one was open for 0% -> 0% of each run, Pallas kernels for 6% -> 9%
where the time goes in v5:
time: 121 us; the launch traced here: 120 us
  starting transfers between devices  58.1 us (48%)
  waiting for transfers between devices  24.7 us (20%)
  Pallas kernels  18 us (15%)
  blocking collectives  12.6 us (10%)
  local copies, waits for them, and re-layouts  6.47 us (5%)
    ppermute x3, starting transfers between devices, per_device(): down = lax.ppermute(down, 'k', down_route)  18.4 us
    all_to_all x1, blocking collectives, per_device(): shares = lax.all_to_all(halves, 'y', 0, 0, tiled=True)  12.6 us
    ppermute x3, waiting for transfers between devices, per_device(): up = lax.ppermute(up, 'k', up_route)  10.1 us
    ppermute x1, starting transfers between devices, per_device(): received = lax.ppermute(product, 'c', [(0, 1), (1, 0)])  10 us
    ppermute x3, starting transfers between devices, per_device(): up = lax.ppermute(up, 'k', up_route)  8.92 us
    all_to_all x1, starting transfers between devices, per_device(): blocks = lax.all_to_all(handed, ('e', 'x'), 0, 0, tiled=True)  7.7 us
    unnamed x18, local copies, waits for them, and re-layouts  6.47 us
    all_to_all x1, starting transfers between devices, per_device(): grouped = lax.all_to_all(sent, ('e', 'x'), 0, 0, tiled=True)  6.22 us
  transfers between devices with their start and end apart: 11, of which 9 were waited for; matrix products, arithmetic and copies ran while one was open for 0% of the time, Pallas kernels for 9%

profile of v5, /device:TPU:1, one launch (start us, length us, event | category | flops | bytes accessed | tf_op | source)
XLA Modules:
  0.0 120.0 jit_solution(15893968196567473632)
XLA Ops:
  0.0 0.0 copy-start.1
  0.0 0.9 copy-done.1
  0.9 0.0 copy-start.2
  0.9 0.8 copy-done.2
  1.7 0.0 copy-start.3
  1.7 0.8 copy-done.3
  2.4 0.0 copy-start.4
  2.4 0.8 copy-done.4
  3.2 0.0 copy-start.5
  3.2 0.8 copy-done.5
  3.9 0.0 copy-start.6
  3.9 0.7 copy-done.6
  4.6 1.5 %shard_map.73 = (bf16[512,128]{1,0:T(8,128)(2,1)S(1)}, bf16[8,256,128]{2,1,0:T(8,128)(2,1)}, bf16[256,128]{1,0:T(8,128)(2,1)S(1)}) custom-call(s32[4]{0:T(128)S(1)} %copy-done.6, bf16[128,512]{1,0:T(8,128)(2,1)S(1)} %copy-done.1, bf16[128,128]{1,0:T(8,128)(2,1)S(1)} %copy-done.2, bf16[128,128]{1,0:T(8,128)(2,1)S(1)} %copy-done.3, ...), custom_call_target="tpu_custom_call" | custom-call | bytes 2097152 | tf_op jit(solution)/shard_map/pallas_call | solution.py:313
  6.1 6.2 %all-to-all-start = ((bf16[8,256,128]{2,1,0:T(8,128)(2,1)}), bf16[8,256,128]{2,1,0:T(8,128)(2,1)S(1)}, u32[]{:S(2)}, u32[]{:S(2)}) async-start(bf16[8,256,128]{2,1,0:T(8,128)(2,1)} %get-tuple-element.24), calls=%async_computation | async-start | bytes 1048576 | tf_op jit(solution)/shard_map/all_to_all | solution.py:329
  12.3 0.0 copy-start.8
  12.3 4.9 %collective-permute-start = (bf16[512,128]{1,0:T(8,128)(2,1)S(1)}, bf16[512,128]{1,0:T(8,128)(2,1)S(1)}, u32[]{:S(2)}, u32[]{:S(2)}) collective-permute-start(bf16[512,128]{1,0:T(8,128)(2,1)S(1)} %get-tuple-element.25.own), channel_id=1, source_target_pairs={{0,64},{64,128},{128,192},{192,256},{256,320},{320,384},{384,448},... | collective-permute-start | bytes 393224 | tf_op jit(solution)/shard_map/ppermute | solution.py:334
  17.2 7.7 %collective-permute-start.1 = (bf16[512,128]{1,0:T(8,128)(2,1)S(1)}, bf16[512,128]{1,0:T(8,128)(2,1)S(1)}, u32[]{:S(2)}, u32[]{:S(2)}) collective-permute-start(bf16[512,128]{1,0:T(8,128)(2,1)S(1)} %get-tuple-element.25.own), channel_id=1, source_target_pairs={{0,448},{64,0},{128,64},{192,128},{256,192},{320,256},{384,320},{4... | collective-permute-start | bytes 393224 | tf_op jit(solution)/shard_map/ppermute | solution.py:335
  24.9 7.7 %collective-permute-done.before.refs_1_ = bf16[512,128]{1,0:T(8,128)(2,1)S(1)} collective-permute-done((bf16[512,128]{1,0:T(8,128)(2,1)S(1)}, bf16[512,128]{1,0:T(8,128)(2,1)S(1)}, u32[]{:S(2)}, u32[]{:S(2)}) %collective-permute-start) | collective-permute-done | bytes 131104 | tf_op jit(solution)/shard_map/ppermute | solution.py:334
  32.6 0.0 collective-permute-done.1.refs_2_
  32.6 1.9 %collective-permute-start.2 = (bf16[512,128]{1,0:T(8,128)(2,1)S(1)}, bf16[512,128]{1,0:T(8,128)(2,1)S(1)}, u32[]{:S(2)}, u32[]{:S(2)}) collective-permute-start(bf16[512,128]{1,0:T(8,128)(2,1)S(1)} %collective-permute-done.before.refs_1_), channel_id=1, source_target_pairs={{0,64},{64,128},{128,192},{192,256},{256,320},{320,384},{384,448},... | collective-permute-start | bytes 393224 | tf_op jit(solution)/shard_map/ppermute | solution.py:334
  34.5 5.5 %collective-permute-start.3 = (bf16[512,128]{1,0:T(8,128)(2,1)S(1)}, bf16[512,128]{1,0:T(8,128)(2,1)S(1)}, u32[]{:S(2)}, u32[]{:S(2)}) collective-permute-start(bf16[512,128]{1,0:T(8,128)(2,1)S(1)} %collective-permute-done.1.refs_2_), channel_id=1, source_target_pairs={{0,448},{64,0},{128,64},{192,128},{256,192},{320,256},{384,320},{4... | collective-permute-start | bytes 393224 | tf_op jit(solution)/shard_map/ppermute | solution.py:335
  40.0 1.8 %collective-permute-done.2.refs_3_ = bf16[512,128]{1,0:T(8,128)(2,1)S(1)} collective-permute-done((bf16[512,128]{1,0:T(8,128)(2,1)S(1)}, bf16[512,128]{1,0:T(8,128)(2,1)S(1)}, u32[]{:S(2)}, u32[]{:S(2)}) %collective-permute-start.2) | collective-permute-done | bytes 131104 | tf_op jit(solution)/shard_map/ppermute | solution.py:334
  41.8 1.2 %collective-permute-done.3.refs_4_ = bf16[512,128]{1,0:T(8,128)(2,1)S(1)} collective-permute-done((bf16[512,128]{1,0:T(8,128)(2,1)S(1)}, bf16[512,128]{1,0:T(8,128)(2,1)S(1)}, u32[]{:S(2)}, u32[]{:S(2)}) %collective-permute-start.3) | collective-permute-done | bytes 131104 | tf_op jit(solution)/shard_map/ppermute | solution.py:335
  43.0 2.1 %collective-permute-start.4 = (bf16[512,128]{1,0:T(8,128)(2,1)S(1)}, bf16[512,128]{1,0:T(8,128)(2,1)S(1)}, u32[]{:S(2)}, u32[]{:S(2)}) collective-permute-start(bf16[512,128]{1,0:T(8,128)(2,1)S(1)} %collective-permute-done.2.refs_3_), channel_id=1, source_target_pairs={{0,64},{64,128},{128,192},{192,256},{256,320},{320,384},{384,448},... | collective-permute-start | bytes 393224 | tf_op jit(solution)/shard_map/ppermute | solution.py:334
  45.1 5.3 %collective-permute-start.5 = (bf16[512,128]{1,0:T(8,128)(2,1)S(1)}, bf16[512,128]{1,0:T(8,128)(2,1)S(1)}, u32[]{:S(2)}, u32[]{:S(2)}) collective-permute-start(bf16[512,128]{1,0:T(8,128)(2,1)S(1)} %collective-permute-done.3.refs_4_), channel_id=1, source_target_pairs={{0,448},{64,0},{128,64},{192,128},{256,192},{320,256},{384,320},{4... | collective-permute-start | bytes 393224 | tf_op jit(solution)/shard_map/ppermute | solution.py:335
  50.4 0.9 shard_map.74
  51.4 0.7 collective-permute-done.4.refs_5_
  52.0 1.7 %collective-permute-done.5.refs_6_ = bf16[512,128]{1,0:T(8,128)(2,1)S(1)} collective-permute-done((bf16[512,128]{1,0:T(8,128)(2,1)S(1)}, bf16[512,128]{1,0:T(8,128)(2,1)S(1)}, u32[]{:S(2)}, u32[]{:S(2)}) %collective-permute-start.5) | collective-permute-done | bytes 131104 | tf_op jit(solution)/shard_map/ppermute | solution.py:335
  53.7 3.2 %collective-permute-start.6 = (bf16[512,128]{1,0:T(8,128)(2,1)S(1)}, bf16[512,128]{1,0:T(8,128)(2,1)S(1)}, u32[]{:S(2)}, u32[]{:S(2)}) collective-permute-start(bf16[512,128]{1,0:T(8,128)(2,1)S(1)} %collective-permute-done.4.refs_5_), channel_id=1, source_target_pairs={{0,64},{64,128},{128,192},{192,256},{256,320},{320,384},{384,448},... | collective-permute-start | bytes 393224 | tf_op jit(solution)/shard_map/ppermute | solution.py:338
  56.9 0.0 all-to-all-done.queries
  56.9 0.0 copy-start.7
  56.9 0.6 copy-done.7
  57.6 5.5 %shard_map.75 = (f32[8,144,256]{2,1,0:T(8,128)S(1)}, f32[8,8,256]{2,1,0:T(8,128)S(1)}) custom-call(s32[4]{0:T(128)S(1)} %copy-done.7, bf16[8,256,128]{2,1,0:T(8,128)(2,1)S(1)} %all-to-all-done.queries, bf16[512,128]{1,0:T(8,128)(2,1)S(1)} %get-tuple-element.32.refs_0_.own, bf16[512,128]{1,0:T(8,128)(2,1)S(1)} %collective-permute-done.before.refs_1_, ...), custom_call_target="tpu_custom_call" | custom-call | flops 1879048192 | bytes 4194304 | tf_op jit(solution)/shard_map/pallas_call | solution.py:350
  63.1 0.4 collective-permute-done.6.last
  63.5 7.7 %all-to-all-start.2 = ((bf16[8,256,128]{2,1,0:T(8,128)(2,1)}), bf16[8,256,128]{2,1,0:T(8,128)(2,1)S(1)}, u32[]{:S(2)}, u32[]{:S(2)}) async-start(bf16[8,256,128]{2,1,0:T(8,128)(2,1)} %get-tuple-element.40), calls=%async_computation.2 | async-start | bytes 1048576 | tf_op jit(solution)/shard_map/all_to_all | solution.py:367
  71.2 0.0 copy-done.8
  71.2 3.3 %shard_map.76 = bf16[8,272,128]{2,1,0:T(8,128)(2,1)} custom-call(s32[4]{0:T(128)S(1)} %copy-done.8, bf16[8,256,128]{2,1,0:T(8,128)(2,1)S(1)} %all-to-all-done.queries, bf16[512,128]{1,0:T(8,128)(2,1)S(1)} %collective-permute-done.6.last, f32[8,144,256]{2,1,0:T(8,128)S(1)} %get-tuple-element.37.sums, f32[8,8,256]{2,1,0:T(8,128)S(1)} %get-tuple-element.38.tops), custom_call_target="tpu_custom_call" | custom-call | flops 268435456 | bytes 4194304 | tf_op jit(solution)/shard_map/pallas_call | solution.py:368
  74.5 3.8 %all-to-all-done.2.grouped = bf16[8,256,128]{2,1,0:T(8,128)(2,1)S(1)} async-done(((bf16[8,256,128]{2,1,0:T(8,128)(2,1)}), bf16[8,256,128]{2,1,0:T(8,128)(2,1)S(1)}, u32[]{:S(2)}, u32[]{:S(2)}) %all-to-all-start.2) | async-done | bytes 524320 | tf_op jit(solution)/shard_map/all_to_all | solution.py:367
  78.3 3.5 %all-to-all-start.1 = ((bf16[8,272,128]{2,1,0:T(8,128)(2,1)}), bf16[8,272,128]{2,1,0:T(8,128)(2,1)S(1)}, u32[]{:S(2)}, u32[]{:S(2)}) async-start(bf16[8,272,128]{2,1,0:T(8,128)(2,1)} %shard_map.76), calls=%async_computation.1 | async-start | bytes 1114112 | tf_op jit(solution)/shard_map/all_to_all | solution.py:377
  81.8 1.2 %shard_map.77.near = bf16[2,128,128]{2,1,0:T(8,128)(2,1)S(1)} custom-call(s32[4]{0:T(128)S(1)} %copy-done.8, bf16[256,128]{1,0:T(8,128)(2,1)S(1)} %get-tuple-element.39.rows, bf16[512,128]{1,0:T(8,128)(2,1)S(1)} %get-tuple-element.32.refs_0_.own, bf16[8,256,128]{2,1,0:T(8,128)(2,1)S(1)} %all-to-all-done.2.grouped), custom_call_target="tpu_custom_call" | custom-call | flops 83886080 | bytes 1048576 | tf_op jit(solution)/shard_map/pallas_call | solution.py:378
  83.1 6.0 %all-to-all-done.1.parts = bf16[8,272,128]{2,1,0:T(8,128)(2,1)S(1)} async-done(((bf16[8,272,128]{2,1,0:T(8,128)(2,1)}), bf16[8,272,128]{2,1,0:T(8,128)(2,1)S(1)}, u32[]{:S(2)}, u32[]{:S(2)}) %all-to-all-start.1) | async-done | bytes 557088 | tf_op jit(solution)/shard_map/all_to_all | solution.py:377
  89.0 4.7 %shard_map.78 = (bf16[4,128,512]{2,1,0:T(8,128)(2,1)S(1)}, f32[4,128,512]{2,1,0:T(8,128)}) custom-call(s32[4]{0:T(128)S(1)} %copy-done.8, bf16[8,272,128]{2,1,0:T(8,128)(2,1)S(1)} %all-to-all-done.1.parts, bf16[2,128,128]{2,1,0:T(8,128)(2,1)S(1)} %shard_map.77.near, bf16[512,4096]{1,0:T(8,128)(2,1)} %weight.1), custom_call_target="tpu_custom_call" | custom-call | flops 536870912 | bytes 5242880 | tf_op jit(solution)/shard_map/pallas_call | solution.py:387
  93.7 10.0 %collective-permute-start.7 = (bf16[4,128,512]{2,1,0:T(8,128)(2,1)S(1)}, bf16[4,128,512]{2,1,0:T(8,128)(2,1)S(1)}, u32[]{:S(2)}, u32[]{:S(2)}) collective-permute-start(bf16[4,128,512]{2,1,0:T(8,128)(2,1)S(1)} %get-tuple-element.42), channel_id=1, source_target_pairs={{0,1},{1,0},{2,3},{3,2},{4,5},{5,4},{6,7},{7,6},{8,9},{9,8},{10,11... | collective-permute-start | bytes 1572872 | tf_op jit(solution)/shard_map/ppermute | solution.py:403
  103.8 1.5 %collective-permute-done.7.received = bf16[4,128,512]{2,1,0:T(8,128)(2,1)S(1)} collective-permute-done((bf16[4,128,512]{2,1,0:T(8,128)(2,1)S(1)}, bf16[4,128,512]{2,1,0:T(8,128)(2,1)S(1)}, u32[]{:S(2)}, u32[]{:S(2)}) %collective-permute-start.7) | collective-permute-done | bytes 524320 | tf_op jit(solution)/shard_map/ppermute | solution.py:403
  105.3 0.0 copy-start
  105.3 1.2 %copy-done = f32[4,128,512]{2,1,0:T(8,128)S(1)} copy-done((f32[4,128,512]{2,1,0:T(8,128)S(1)}, f32[4,128,512]{2,1,0:T(8,128)}, u32[]{:S(2)}) %copy-start) | copy-done | bytes 1048600
  106.5 0.1 shard_map.79
  106.6 12.6 %all_to_all.20.shares = bf16[4,128,512]{2,1,0:T(8,128)(2,1)S(1)} all-to-all(bf16[4,128,512]{2,1,0:T(8,128)(2,1)S(1)} %shard_map.79), channel_id=1, replica_groups=mesh['k'=8,'e'=2,'x'=4,'y'=4,'c'=2] {'y'}, dimensions={0} | all-to-all | bytes 1048576 | tf_op jit(solution)/shard_map/all_to_all | solution.py:410
  119.2 0.8 shard_map.80
Async XLA Ops:
  0.0 0.9 copy-start.1
  0.9 0.8 copy-start.2
  1.7 0.8 copy-start.3
  2.4 0.8 copy-start.4
  3.2 0.8 copy-start.5
  3.9 0.7 copy-start.6
  6.1 50.8 %all-to-all-start = ((bf16[8,256,128]{2,1,0:T(8,128)(2,1)}), bf16[8,256,128]{2,1,0:T(8,128)(2,1)S(1)}, u32[]{:S(2)}, u32[]{:S(2)}) async-start(bf16[8,256,128]{2,1,0:T(8,128)(2,1)} %get-tuple-element.24), calls=%async_computation | async-start | bytes 1048576 | tf_op jit(solution)/shard_map/all_to_all | solution.py:329
  12.3 58.9 %copy-start.8 = (s32[4]{0:T(128)S(1)}, s32[4]{0:T(128)}, u32[]{:S(2)}) copy-start(s32[4]{0:T(128)} %spans.9) | copy-start | bytes 52
  12.3 20.3 %collective-permute-start = (bf16[512,128]{1,0:T(8,128)(2,1)S(1)}, bf16[512,128]{1,0:T(8,128)(2,1)S(1)}, u32[]{:S(2)}, u32[]{:S(2)}) collective-permute-start(bf16[512,128]{1,0:T(8,128)(2,1)S(1)} %get-tuple-element.25.own), channel_id=1, source_target_pairs={{0,64},{64,128},{128,192},{192,256},{256,320},{320,384},{384,448},... | collective-permute-start | bytes 393224 | tf_op jit(solution)/shard_map/ppermute | solution.py:334
  17.2 15.4 %collective-permute-start.1 = (bf16[512,128]{1,0:T(8,128)(2,1)S(1)}, bf16[512,128]{1,0:T(8,128)(2,1)S(1)}, u32[]{:S(2)}, u32[]{:S(2)}) collective-permute-start(bf16[512,128]{1,0:T(8,128)(2,1)S(1)} %get-tuple-element.25.own), channel_id=1, source_target_pairs={{0,448},{64,0},{128,64},{192,128},{256,192},{320,256},{384,320},{4... | collective-permute-start | bytes 393224 | tf_op jit(solution)/shard_map/ppermute | solution.py:335
  32.6 9.2 %collective-permute-start.2 = (bf16[512,128]{1,0:T(8,128)(2,1)S(1)}, bf16[512,128]{1,0:T(8,128)(2,1)S(1)}, u32[]{:S(2)}, u32[]{:S(2)}) collective-permute-start(bf16[512,128]{1,0:T(8,128)(2,1)S(1)} %collective-permute-done.before.refs_1_), channel_id=1, source_target_pairs={{0,64},{64,128},{128,192},{192,256},{256,320},{320,384},{384,448},... | collective-permute-start | bytes 393224 | tf_op jit(solution)/shard_map/ppermute | solution.py:334
  34.5 8.5 %collective-permute-start.3 = (bf16[512,128]{1,0:T(8,128)(2,1)S(1)}, bf16[512,128]{1,0:T(8,128)(2,1)S(1)}, u32[]{:S(2)}, u32[]{:S(2)}) collective-permute-start(bf16[512,128]{1,0:T(8,128)(2,1)S(1)} %collective-permute-done.1.refs_2_), channel_id=1, source_target_pairs={{0,448},{64,0},{128,64},{192,128},{256,192},{320,256},{384,320},{4... | collective-permute-start | bytes 393224 | tf_op jit(solution)/shard_map/ppermute | solution.py:335
  43.0 9.0 %collective-permute-start.4 = (bf16[512,128]{1,0:T(8,128)(2,1)S(1)}, bf16[512,128]{1,0:T(8,128)(2,1)S(1)}, u32[]{:S(2)}, u32[]{:S(2)}) collective-permute-start(bf16[512,128]{1,0:T(8,128)(2,1)S(1)} %collective-permute-done.2.refs_3_), channel_id=1, source_target_pairs={{0,64},{64,128},{128,192},{192,256},{256,320},{320,384},{384,448},... | collective-permute-start | bytes 393224 | tf_op jit(solution)/shard_map/ppermute | solution.py:334
  45.1 8.5 %collective-permute-start.5 = (bf16[512,128]{1,0:T(8,128)(2,1)S(1)}, bf16[512,128]{1,0:T(8,128)(2,1)S(1)}, u32[]{:S(2)}, u32[]{:S(2)}) collective-permute-start(bf16[512,128]{1,0:T(8,128)(2,1)S(1)} %collective-permute-done.3.refs_4_), channel_id=1, source_target_pairs={{0,448},{64,0},{128,64},{192,128},{256,192},{320,256},{384,320},{4... | collective-permute-start | bytes 393224 | tf_op jit(solution)/shard_map/ppermute | solution.py:335
  53.7 9.8 %collective-permute-start.6 = (bf16[512,128]{1,0:T(8,128)(2,1)S(1)}, bf16[512,128]{1,0:T(8,128)(2,1)S(1)}, u32[]{:S(2)}, u32[]{:S(2)}) collective-permute-start(bf16[512,128]{1,0:T(8,128)(2,1)S(1)} %collective-permute-done.4.refs_5_), channel_id=1, source_target_pairs={{0,64},{64,128},{128,192},{192,256},{256,320},{320,384},{384,448},... | collective-permute-start | bytes 393224 | tf_op jit(solution)/shard_map/ppermute | solution.py:338
  56.9 0.7 copy-start.7
  63.5 14.8 %all-to-all-start.2 = ((bf16[8,256,128]{2,1,0:T(8,128)(2,1)}), bf16[8,256,128]{2,1,0:T(8,128)(2,1)S(1)}, u32[]{:S(2)}, u32[]{:S(2)}) async-start(bf16[8,256,128]{2,1,0:T(8,128)(2,1)} %get-tuple-element.40), calls=%async_computation.2 | async-start | bytes 1048576 | tf_op jit(solution)/shard_map/all_to_all | solution.py:367
  78.3 10.7 %all-to-all-start.1 = ((bf16[8,272,128]{2,1,0:T(8,128)(2,1)}), bf16[8,272,128]{2,1,0:T(8,128)(2,1)S(1)}, u32[]{:S(2)}, u32[]{:S(2)}) async-start(bf16[8,272,128]{2,1,0:T(8,128)(2,1)} %shard_map.76), calls=%async_computation.1 | async-start | bytes 1114112 | tf_op jit(solution)/shard_map/all_to_all | solution.py:377
  93.7 11.5 %collective-permute-start.7 = (bf16[4,128,512]{2,1,0:T(8,128)(2,1)S(1)}, bf16[4,128,512]{2,1,0:T(8,128)(2,1)S(1)}, u32[]{:S(2)}, u32[]{:S(2)}) collective-permute-start(bf16[4,128,512]{2,1,0:T(8,128)(2,1)S(1)} %get-tuple-element.42), channel_id=1, source_target_pairs={{0,1},{1,0},{2,3},{3,2},{4,5},{5,4},{6,7},{7,6},{8,9},{9,8},{10,11... | collective-permute-start | bytes 1572872 | tf_op jit(solution)/shard_map/ppermute | solution.py:403
  105.3 1.2 %copy-start = (f32[4,128,512]{2,1,0:T(8,128)S(1)}, f32[4,128,512]{2,1,0:T(8,128)}, u32[]{:S(2)}) copy-start(f32[4,128,512]{2,1,0:T(8,128)} %get-tuple-element.41.kept) | copy-start | bytes 3145732

commit v6 on v2

--- a/solution.py
+++ b/solution.py
@@ -22,6 +22,7 @@
 CACHE = 2 * RING * BLOCKS // 2 * HD
 VMEM = pl.BlockSpec(memory_space=pltpu.VMEM)
 SMEM = pl.BlockSpec(memory_space=pltpu.SMEM)
+ANY = pl.BlockSpec(memory_space=pl.ANY)
 NT = (((1,), (1,)), ((), ()))
 NN = (((1,), (0,)), ((), ()))
 
@@ -41,21 +42,40 @@
     return order
 
 
-def prepare_kernel(spans, queries, keys, values, cache_keys, cache_values, own, sent):
-    own[0:HD, :] = cache_keys[...]
-    own[HD : 2 * HD, :] = cache_values[...]
-    own[2 * HD : 3 * HD, :] = keys[...]
-    own[3 * HD :, :] = values[...]
-    order = head_order(spans)
+def prepare_kernel(
+    spans, queries, keys, values, cache_keys, cache_values, own, sent, heads, kinds, sems
+):
+    copies = [
+        pltpu.make_async_copy(spans, kinds, sems.at[0]),
+        pltpu.make_async_copy(queries, heads, sems.at[1]),
+    ]
+    for i, source in enumerate([cache_keys, cache_values, keys, values]):
+        copies.append(
+            pltpu.make_async_copy(source, own.at[i * HD : (i + 1) * HD, :], sems.at[2 + i])
+        )
+    for copy in copies:
+        copy.start()
+    for copy in copies:
+        copy.wait()
+    order = head_order(kinds)
     for s in range(GROUP):
-        rows = queries[:, pl.ds(pl.multiple_of(order[s] * HD, HD), HD)]
+        rows = heads[:, pl.ds(pl.multiple_of(order[s] * HD, HD), HD)]
         for j in range(BLOCKS):
             sent[j, s] = rows
 
 
-def place(info, distance):
-    k = lax.rem(info[0] + distance + RING, RING)
-    return ((k * 2 + info[1]) * 4 + info[2]) * HD
+def position():
+    return lax.axis_index("k"), lax.axis_index("e"), lax.axis_index("x")
+
+
+def place(distance):
+    k, e, x = position()
+    return ((lax.rem(k + distance + RING, RING) * 2 + e) * 4 + x) * HD
+
+
+def sources():
+    first = jnp.where(lax.axis_index("c") == 0, -1, 1)
+    return [0 * first, first, -first, 2 * first, -2 * first, 3 * first, -3 * first, 4 * first]
 
 
 def offsets():
@@ -68,14 +88,14 @@
     return t // (BLOCKS // per), t % (BLOCKS // per) * per
 
 
-def masked_scores(info, spans, order, offset, key_rows, rows, t, cached, start):
+def masked_scores(spans, order, offset, key_rows, rows, t, cached, start):
     slot, first = tile_of(t)
-    position = CACHE + info[0] * (BLOCKS * HD) + first * HD
+    begin = CACHE + lax.axis_index("k") * (BLOCKS * HD) + first * HD
     found = dot(key_rows, rows, NT)
     if cached:
-        allowed = offset < spans[order[slot]] - position + start
+        allowed = offset < spans[order[slot]] - begin + start
     else:
-        allowed = offset >= start + CACHE - position
+        allowed = offset >= start + CACHE - begin
     return jnp.where(allowed, found, MASKED)
 
 
@@ -83,16 +103,16 @@
     return jnp.max(found.reshape(HD // 8, 8, found.shape[1]), axis=0)
 
 
-def first_kernel(info, spans, queries, *refs):
+def first_kernel(spans, queries, *refs):
     kv = refs[: RING - 1]
     sums, tops, near, near_tops, keys, flipped, scores = refs[RING - 1 :]
     order = head_order(spans)
-    distances = [0, -1, 1, -2, 2, -3, 3]
+    distances = sources()
     blocks = []
     for i in range(RING - 1):
         for half in range(2):
             n = len(blocks)
-            blocks.append((half == 0, place(info, distances[i])))
+            blocks.append((half == 0, place(distances[i])))
             keys[n * HD : (n + 1) * HD, :] = kv[i][2 * half * HD : (2 * half + 1) * HD, :]
             flipped[0:HD, n * HD : (n + 1) * HD] = kv[i][
                 (2 * half + 1) * HD : (2 * half + 2) * HD, :
@@ -107,7 +127,7 @@
         top = jnp.full((8, TILE), FLOOR, jnp.float32)
         for n, (cached, start) in enumerate(blocks):
             found = masked_scores(
-                info, spans, order, offset, keys[n * HD : (n + 1) * HD, :], rows, t, cached, start
+                spans, order, offset, keys[n * HD : (n + 1) * HD, :], rows, t, cached, start
             )
             scores[t % 2, n * HD : (n + 1) * HD, :] = found
             top = jnp.maximum(top, highest(found))
@@ -126,15 +146,15 @@
         sums[t] = dot(flipped[...], weights, NN)
         tops[t] = jnp.broadcast_to(top, (8, TILE))
 
-    own = info[1] * 4 + info[2]
-    wraps = info[0] == 0
-    at = jnp.where(wraps, 2 * HD, 3 * HD)
-    before_keys = keys[pl.ds(pl.multiple_of(at, HD), HD), :]
-    before_values = jnp.where(
-        wraps, flipped[:, 2 * HD : 3 * HD], flipped[:, 3 * HD : 4 * HD]
-    )
-    before_start = place(info, -1) + jnp.where(wraps, 0, CACHE)
-    own_start = place(info, 0) + CACHE
+    k, e, x = position()
+    own = e * 4 + x
+    wraps = k == 0
+    n = jnp.where(lax.axis_index("c") == 0, 2, 4) + jnp.where(wraps, 0, 1)
+    at = pl.multiple_of(n * HD, HD)
+    before_keys = keys[pl.ds(at, HD), :]
+    before_values = flipped[:, pl.ds(at, HD)]
+    before_start = place(-1) + jnp.where(wraps, 0, CACHE)
+    own_start = place(0) + CACHE
     span = jnp.where(
         lax.broadcasted_iota(jnp.int32, (HD, TILE), 1) < HD, spans[order[2]], spans[order[3]]
     )
@@ -143,8 +163,8 @@
         earlier = b < own
         rows = queries[b, 2:4].reshape(TILE, HD)
         found = dot(jnp.where(earlier, before_keys, keys[HD : 2 * HD, :]), rows, NT)
-        position = CACHE + (info[0] * BLOCKS + b) * HD
-        behind = near_offset + (position - jnp.where(earlier, before_start, own_start))
+        begin = CACHE + (k * BLOCKS + b) * HD
+        behind = near_offset + (begin - jnp.where(earlier, before_start, own_start))
         found = jnp.where((behind >= 0) & (behind < span), found, MASKED)
         top = jnp.maximum(jnp.max(found, axis=0, keepdims=True), FLOOR)
         weights = jnp.exp2((found - top) * FACTOR).astype(jnp.bfloat16)
@@ -166,9 +186,9 @@
         level = level - term
 
 
-def second_kernel(info, spans, queries, last, sums, tops, near, near_tops, out, stats):
+def second_kernel(spans, queries, last, sums, tops, near, near_tops, out, stats):
     order = head_order(spans)
-    start = place(info, 4)
+    start = place(sources()[-1])
     _, offset = offsets()
     ones = jnp.ones((STATS, HD), jnp.bfloat16)
     flipped = jnp.concatenate(
@@ -195,7 +215,7 @@
         rows = queries[first : first + TILE // HD, slot].reshape(TILE, HD)
         found = [
             masked_scores(
-                info, spans, order, offset, last[2 * half * HD : (2 * half + 1) * HD, :],
+                spans, order, offset, last[2 * half * HD : (2 * half + 1) * HD, :],
                 rows, t, half == 0, start,
             )
             for half in range(2)
@@ -213,7 +233,7 @@
     out[:, GROUP * HD :, :] = stats[...].astype(jnp.bfloat16)
 
 
-def project_kernel(spans, parts, weight, out, attn):
+def project_kernel(spans, parts, weight, out, kept, attn):
     order = head_order(spans)
     for s in range(GROUP):
         terms = parts[:, GROUP * HD :, :].astype(jnp.float32)
@@ -235,9 +255,17 @@
             (summed * (1.0 / total)).T.astype(jnp.bfloat16)
         )
     rows = attn[...]
+    mine = lax.axis_index("c")
     width = out.shape[2]
-    for f in range(out.shape[0]):
-        out[f] = dot(rows, weight[:, f * width : (f + 1) * width], NN).astype(jnp.bfloat16)
+    for core, target in ((1 - mine, out), (mine, kept)):
+        for f in range(out.shape[0]):
+            at = pl.multiple_of((2 * f + core) * width, width)
+            product = dot(rows, weight[:, pl.ds(at, width)], NN)
+            target[f] = product.astype(target.dtype)
+
+
+def add_kernel(kept, received, out):
+    out[...] = (kept[...] + received[...].astype(jnp.float32)).astype(jnp.bfloat16)
 
 
 def total_kernel(shares, out):
@@ -261,7 +289,6 @@
 
 
 def per_device(queries, keys, values, cache_keys, cache_values, spans, out_weight):
-    info = jnp.stack([lax.axis_index("k"), lax.axis_index("e"), lax.axis_index("x")])
     bf16, f32 = jnp.bfloat16, jnp.float32
     own, sent = call(
         prepare_kernel,
@@ -269,17 +296,29 @@
             jax.ShapeDtypeStruct((4 * HD, HD), bf16),
             jax.ShapeDtypeStruct((BLOCKS, GROUP, HD, HD), bf16),
         ],
-        [SMEM] + [VMEM] * 5,
+        [ANY] * 6,
+        [
+            pltpu.VMEM((HD, GROUP * HD), bf16),
+            pltpu.SMEM((GROUP,), jnp.int32),
+            pltpu.SemaphoreType.DMA((6,)),
+        ],
+        vmem=60,
         moved=2**21,
     )(spans, queries, keys, values, cache_keys, cache_values)
-    up_route = [(i, (i + 1) % RING) for i in range(RING)]
-    down_route = [(i, (i - 1) % RING) for i in range(RING)]
-    kv, up, down = [own], own, own
+    routes = [
+        [
+            (2 * i + c, (i + (1 if c == turn else -1)) % RING * 2 + c)
+            for i in range(RING)
+            for c in range(2)
+        ]
+        for turn in range(2)
+    ]
+    kv, one, two = [own], own, own
     for _ in range(RING // 2 - 1):
-        up = lax.ppermute(up, "k", up_route)
-        down = lax.ppermute(down, "k", down_route)
-        kv += [up, down]
-    last = lax.ppermute(up, "k", up_route)
+        one = lax.ppermute(one, ("k", "c"), routes[0])
+        two = lax.ppermute(two, ("k", "c"), routes[1])
+        kv += [one, two]
+    last = lax.ppermute(one, ("k", "c"), routes[0])
     grouped = lax.all_to_all(sent, ("e", "x"), 0, 0, tiled=True)
 
     near_blocks = 2 * (RING - 1)
@@ -291,7 +330,7 @@
             jax.ShapeDtypeStruct((BLOCKS, HD + STATS, TILE), f32),
             jax.ShapeDtypeStruct((BLOCKS, 8, TILE), f32),
         ],
-        [SMEM, SMEM] + [VMEM] * RING,
+        [SMEM] + [VMEM] * RING,
         [
             pltpu.VMEM((near_blocks * HD, HD), bf16),
             pltpu.VMEM((HD + STATS, near_blocks * HD), bf16),
@@ -300,29 +339,40 @@
         flops=4 * 2048 * 1792 * 128,
         moved=4 * 2**20,
         exps=2048 * 1792,
-    )(info, spans, grouped, *kv)
+    )(spans, grouped, *kv)
     partial = call(
         second_kernel,
         jax.ShapeDtypeStruct((BLOCKS, PIECE, HD), bf16),
-        [SMEM, SMEM] + [VMEM] * 6,
+        [SMEM] + [VMEM] * 6,
         [pltpu.VMEM((BLOCKS, STATS, HD), f32)],
         flops=4 * 2048 * 256 * 128,
         moved=4 * 2**20,
         exps=2048 * 256,
-    )(info, spans, grouped, last, *state)
+    )(spans, grouped, last, *state)
     parts = lax.all_to_all(partial, ("e", "x"), 0, 0, tiled=True)
-    product = call(
+    width = out_weight.shape[1] // 8
+    product, kept = call(
         project_kernel,
-        jax.ShapeDtypeStruct((8, HD, out_weight.shape[1] // 8), bf16),
+        [
+            jax.ShapeDtypeStruct((4, HD, width), bf16),
+            jax.ShapeDtypeStruct((4, HD, width), f32),
+        ],
         [SMEM, VMEM, VMEM],
         [pltpu.VMEM((HD, GROUP * HD), bf16)],
         flops=2 * 128 * 512 * 4096,
         moved=5 * 2**20,
     )(spans, parts, out_weight)
-    shares = lax.all_to_all(product, ("y", "c"), 0, 0, tiled=True)
+    received = lax.ppermute(product, "c", [(0, 1), (1, 0)])
+    halves = call(
+        add_kernel,
+        jax.ShapeDtypeStruct((4, HD, width), bf16),
+        [VMEM] * 2,
+        moved=2 * 2**20,
+    )(kept, received)
+    shares = lax.all_to_all(halves, "y", 0, 0, tiled=True)
     return call(
         total_kernel,
-        jax.ShapeDtypeStruct((out_weight.shape[1] // 8, HD), bf16),
+        jax.ShapeDtypeStruct((width, HD), bf16),
         [VMEM],
         moved=2**20,
     )(shares)

time: 113 us -> 104 us (0.920)
  starting transfers between devices: 36.8 us -> 48.2 us
  blocking collectives: 40.5 us -> 30.7 us
  waiting for transfers between devices: 17.8 us -> 10.8 us
  local copies, waits for them, and re-layouts: 4.6 us -> 0.02 us
    all_to_all x1, blocking collectives: 27.2 us -> 12.6 us  [per_device(): shares = lax.all_to_all(halves, 'y', 0, 0, tiled=True)]
    ppermute x7 -> x8, starting transfers between devices: 30.6 us -> 41.8 us  [the longest x3 22.5 us: per_device(): one = lax.ppermute(one, ('k', 'c'), routes[0])]
    ppermute x7 -> x8, waiting for transfers between devices: 17.8 us -> 10.8 us  [the longest x3 9.26 us: per_device(): two = lax.ppermute(two, ('k', 'c'), routes[1])]
    all_to_all x1, blocking collectives: 13.3 us -> 18.1 us  [per_device(): parts = lax.all_to_all(partial, ('e', 'x'), 0, 0, tiled=True)]
    unnamed x16 -> x6, local copies, waits for them, and re-layouts: 4.6 us -> 0.02 us
    pallas_call x2 -> x3, Pallas kernels: 2.45 us -> 2.45 us  [the longest x1 1.57 us: per_device(): call(project_kernel, [jax.ShapeDtypeStruct((4, HD, width), bf16), jax.Sha...]
  transfers between devices with their start and end apart: 8 -> 9, of which waited for: 3 -> 4; matrix products, arithmetic and copies ran while one was open for 0% -> 0% of each run, Pallas kernels for 5% -> 6%
where the time goes in v6:
time: 104 us; the launch traced here: 103 us
  starting transfers between devices  48.2 us (46%)
  blocking collectives  30.7 us (30%)
  Pallas kernels  13.5 us (13%)
  waiting for transfers between devices  10.8 us (10%)
    ppermute x3, starting transfers between devices, per_device(): one = lax.ppermute(one, ('k', 'c'), routes[0])  22.5 us
    all_to_all x1, blocking collectives, per_device(): parts = lax.all_to_all(partial, ('e', 'x'), 0, 0, tiled=True)  18.1 us
    all_to_all x1, blocking collectives, per_device(): shares = lax.all_to_all(halves, 'y', 0, 0, tiled=True)  12.6 us
    ppermute x3, waiting for transfers between devices, per_device(): two = lax.ppermute(two, ('k', 'c'), routes[1])  9.26 us
    ppermute x1, starting transfers between devices, per_device(): received = lax.ppermute(product, 'c', [(0, 1), (1, 0)])  8.16 us
    pallas_call x1, Pallas kernels, per_device(): call(first_kernel, [jax.ShapeDtypeStruct((TILES, HD + STATS, TILE), f32),...  6.4 us
    all_to_all x1, starting transfers between devices, per_device(): grouped = lax.all_to_all(sent, ('e', 'x'), 0, 0, tiled=True)  6.35 us
    ppermute x3, starting transfers between devices, per_device(): two = lax.ppermute(two, ('k', 'c'), routes[1])  5.74 us
  transfers between devices with their start and end apart: 9, of which 4 were waited for; matrix products, arithmetic and copies ran while one was open for 0% of the time, Pallas kernels for 6%

profile of v6, /device:TPU:1, one launch (start us, length us, event | category | flops | bytes accessed | tf_op | source)
XLA Modules:
  0.0 103.3 jit_solution(6907200000051849514)
XLA Ops:
  0.0 0.0 copy-start.1
  0.0 2.1 %shard_map.73 = (bf16[512,128]{1,0:T(8,128)(2,1)}, bf16[8,4,128,128]{3,2,1,0:T(8,128)(2,1)}) custom-call(s32[4]{0:T(128)} %spans.7, bf16[128,512]{1,0:T(8,128)(2,1)} %queries.1, bf16[128,128]{1,0:T(8,128)(2,1)} %keys.1, bf16[128,128]{1,0:T(8,128)(2,1)} %values.1, bf16[128,128]{1,0:T(8,128)(2,1)} %cache_keys.1, bf16[128,128]{1,0:T(8,128)(2,1)} %cache_values.1), custom_call_target="tpu_custom_call" | custom-call | bytes 2097152 | tf_op jit(solution)/shard_map/pallas_call | solution.py:293
  2.1 0.0 copy-start.2
  2.1 6.3 %all-to-all-start = ((bf16[8,4,128,128]{3,2,1,0:T(8,128)(2,1)}), bf16[8,4,128,128]{3,2,1,0:T(8,128)(2,1)S(1)}, u32[]{:S(2)}, u32[]{:S(2)}) async-start(bf16[8,4,128,128]{3,2,1,0:T(8,128)(2,1)} %get-tuple-element.13), calls=%async_computation | async-start | bytes 2097152 | tf_op jit(solution)/shard_map/all_to_all | solution.py:322
  8.5 0.0 copy-done.2
  8.5 10.7 %collective-permute-start = (bf16[512,128]{1,0:T(8,128)(2,1)S(1)}, bf16[512,128]{1,0:T(8,128)(2,1)S(1)}, u32[]{:S(2)}, u32[]{:S(2)}) collective-permute-start(bf16[512,128]{1,0:T(8,128)(2,1)S(1)} %copy-done.2), channel_id=1, source_target_pairs={{0,64},{1,449},{64,128},{65,1},{128,192},{129,65},{192,256},{193,1... | collective-permute-start | bytes 393224 | tf_op jit(solution)/shard_map/ppermute | solution.py:318
  19.1 1.9 %collective-permute-start.4 = (bf16[512,128]{1,0:T(8,128)(2,1)S(1)}, bf16[512,128]{1,0:T(8,128)(2,1)S(1)}, u32[]{:S(2)}, u32[]{:S(2)}) collective-permute-start(bf16[512,128]{1,0:T(8,128)(2,1)S(1)} %copy-done.2), channel_id=1, source_target_pairs={{0,448},{1,65},{64,0},{65,129},{128,64},{129,193},{192,128},{193,2... | collective-permute-start | bytes 393224 | tf_op jit(solution)/shard_map/ppermute | solution.py:319
  21.1 0.0 collective-permute-done.refs_1_
  21.1 6.3 %collective-permute-start.1 = (bf16[512,128]{1,0:T(8,128)(2,1)S(1)}, bf16[512,128]{1,0:T(8,128)(2,1)S(1)}, u32[]{:S(2)}, u32[]{:S(2)}) collective-permute-start(bf16[512,128]{1,0:T(8,128)(2,1)S(1)} %collective-permute-done.refs_1_), channel_id=1, source_target_pairs={{0,64},{1,449},{64,128},{65,1},{128,192},{129,65},{192,256},{193,1... | collective-permute-start | bytes 393224 | tf_op jit(solution)/shard_map/ppermute | solution.py:318
  27.4 8.5 %collective-permute-done.4.refs_2_ = bf16[512,128]{1,0:T(8,128)(2,1)S(1)} collective-permute-done((bf16[512,128]{1,0:T(8,128)(2,1)S(1)}, bf16[512,128]{1,0:T(8,128)(2,1)S(1)}, u32[]{:S(2)}, u32[]{:S(2)}) %collective-permute-start.4) | collective-permute-done | bytes 131104 | tf_op jit(solution)/shard_map/ppermute | solution.py:319
  35.9 1.9 %collective-permute-start.5 = (bf16[512,128]{1,0:T(8,128)(2,1)S(1)}, bf16[512,128]{1,0:T(8,128)(2,1)S(1)}, u32[]{:S(2)}, u32[]{:S(2)}) collective-permute-start(bf16[512,128]{1,0:T(8,128)(2,1)S(1)} %collective-permute-done.4.refs_2_), channel_id=1, source_target_pairs={{0,448},{1,65},{64,0},{65,129},{128,64},{129,193},{192,128},{193,2... | collective-permute-start | bytes 393224 | tf_op jit(solution)/shard_map/ppermute | solution.py:319
  37.8 0.0 collective-permute-done.1.refs_3_
  37.8 5.5 %collective-permute-start.2 = (bf16[512,128]{1,0:T(8,128)(2,1)S(1)}, bf16[512,128]{1,0:T(8,128)(2,1)S(1)}, u32[]{:S(2)}, u32[]{:S(2)}) collective-permute-start(bf16[512,128]{1,0:T(8,128)(2,1)S(1)} %collective-permute-done.1.refs_3_), channel_id=1, source_target_pairs={{0,64},{1,449},{64,128},{65,1},{128,192},{129,65},{192,256},{193,1... | collective-permute-start | bytes 393224 | tf_op jit(solution)/shard_map/ppermute | solution.py:318
  43.3 0.4 collective-permute-done.5.refs_4_
  43.7 1.9 %collective-permute-start.6 = (bf16[512,128]{1,0:T(8,128)(2,1)S(1)}, bf16[512,128]{1,0:T(8,128)(2,1)S(1)}, u32[]{:S(2)}, u32[]{:S(2)}) collective-permute-start(bf16[512,128]{1,0:T(8,128)(2,1)S(1)} %collective-permute-done.5.refs_4_), channel_id=1, source_target_pairs={{0,448},{1,65},{64,0},{65,129},{128,64},{129,193},{192,128},{193,2... | collective-permute-start | bytes 393224 | tf_op jit(solution)/shard_map/ppermute | solution.py:319
  45.6 0.0 collective-permute-done.2.refs_5_
  45.6 5.5 %collective-permute-start.3 = (bf16[512,128]{1,0:T(8,128)(2,1)S(1)}, bf16[512,128]{1,0:T(8,128)(2,1)S(1)}, u32[]{:S(2)}, u32[]{:S(2)}) collective-permute-start(bf16[512,128]{1,0:T(8,128)(2,1)S(1)} %collective-permute-done.2.refs_5_), channel_id=1, source_target_pairs={{0,64},{1,449},{64,128},{65,1},{128,192},{129,65},{192,256},{193,1... | collective-permute-start | bytes 393224 | tf_op jit(solution)/shard_map/ppermute | solution.py:321
  51.1 0.4 collective-permute-done.6.refs_6_
  51.5 0.0 all-to-all-done.queries
  51.5 0.0 copy-done.1
  51.5 6.4 %shard_map.74 = (f32[8,144,256]{2,1,0:T(8,128)S(1)}, f32[8,8,256]{2,1,0:T(8,128)S(1)}, f32[8,144,256]{2,1,0:T(8,128)S(1)}, f32[8,8,256]{2,1,0:T(8,128)S(1)}) custom-call(s32[4]{0:T(128)S(1)} %copy-done.1, bf16[8,4,128,128]{3,2,1,0:T(8,128)(2,1)S(1)} %all-to-all-done.queries, bf16[512,128]{1,0:T(8,128)(2,1)S(1)} %copy-done.2, ...), custom_call_target="tpu_custom_call" | custom-call | flops 1879048192 | bytes 4194304 | tf_op jit(solution)/shard_map/pallas_call | solution.py:325
  57.9 0.0 collective-permute-done.3.last
  57.9 0.0 copy-start
  57.9 2.5 %shard_map.75 = bf16[8,528,128]{2,1,0:T(8,128)(2,1)S(1)} custom-call(s32[4]{0:T(128)S(1)} %copy-done.1, bf16[8,4,128,128]{3,2,1,0:T(8,128)(2,1)S(1)} %all-to-all-done.queries, bf16[512,128]{1,0:T(8,128)(2,1)S(1)} %collective-permute-done.3.last, f32[8,144,256]{2,1,0:T(8,128)S(1)} %get-tuple-element.15.sums, f32[8,8,256]{2,1,0:T(8,128)S(1)} %get-tuple-element.16.tops, ...), custom_call_target="tpu_custom_call" | custom-call | flops 268435456 | bytes 4194304 | tf_op jit(solution)/shard_map/pallas_call | solution.py:343
  60.5 18.1 %all_to_all.15.parts = bf16[8,528,128]{2,1,0:T(8,128)(2,1)S(1)} all-to-all(bf16[8,528,128]{2,1,0:T(8,128)(2,1)S(1)} %shard_map.75), channel_id=1, replica_groups=mesh['k'=8,'e'=2,'x'=4,'y'=4,'c'=2] {'e','x'}, dimensions={0} | all-to-all | bytes 2162688 | tf_op jit(solution)/shard_map/all_to_all | solution.py:352
  78.6 0.0 copy-done
  78.6 1.6 %shard_map.76 = (bf16[4,128,512]{2,1,0:T(8,128)(2,1)S(1)}, f32[4,128,512]{2,1,0:T(8,128)S(1)}) custom-call(s32[4]{0:T(128)S(1)} %copy-done.1, bf16[8,528,128]{2,1,0:T(8,128)(2,1)S(1)} %all_to_all.15.parts, bf16[512,4096]{1,0:T(8,128)(2,1)S(1)} %copy-done), custom_call_target="tpu_custom_call" | custom-call | flops 536870912 | bytes 5242880 | tf_op jit(solution)/shard_map/pallas_call | solution.py:354
  80.2 8.2 %collective-permute-start.7 = (bf16[4,128,512]{2,1,0:T(8,128)(2,1)S(1)}, bf16[4,128,512]{2,1,0:T(8,128)(2,1)S(1)}, u32[]{:S(2)}, u32[]{:S(2)}) collective-permute-start(bf16[4,128,512]{2,1,0:T(8,128)(2,1)S(1)} %get-tuple-element.20), channel_id=1, source_target_pairs={{0,1},{1,0},{2,3},{3,2},{4,5},{5,4},{6,7},{7,6},{8,9},{9,8},{10,11... | collective-permute-start | bytes 1572872 | tf_op jit(solution)/shard_map/ppermute | solution.py:365
  88.3 1.5 %collective-permute-done.7.received = bf16[4,128,512]{2,1,0:T(8,128)(2,1)S(1)} collective-permute-done((bf16[4,128,512]{2,1,0:T(8,128)(2,1)S(1)}, bf16[4,128,512]{2,1,0:T(8,128)(2,1)S(1)}, u32[]{:S(2)}, u32[]{:S(2)}) %collective-permute-start.7) | collective-permute-done | bytes 524320 | tf_op jit(solution)/shard_map/ppermute | solution.py:365
  89.9 0.1 shard_map.77
  89.9 12.6 %all_to_all.16.shares = bf16[4,128,512]{2,1,0:T(8,128)(2,1)S(1)} all-to-all(bf16[4,128,512]{2,1,0:T(8,128)(2,1)S(1)} %shard_map.77), channel_id=1, replica_groups=mesh['k'=8,'e'=2,'x'=4,'y'=4,'c'=2] {'y'}, dimensions={0} | all-to-all | bytes 1048576 | tf_op jit(solution)/shard_map/all_to_all | solution.py:372
  102.5 0.8 shard_map.78
Async XLA Ops:
  0.0 51.5 %copy-start.1 = (s32[4]{0:T(128)S(1)}, s32[4]{0:T(128)}, u32[]{:S(2)}) copy-start(s32[4]{0:T(128)} %spans.7) | copy-start | bytes 52
  2.1 6.4 %copy-start.2 = (bf16[512,128]{1,0:T(8,128)(2,1)S(1)}, bf16[512,128]{1,0:T(8,128)(2,1)}, u32[]{:S(2)}) copy-start(bf16[512,128]{1,0:T(8,128)(2,1)} %get-tuple-element.14.refs_0_) | copy-start | bytes 393220
  2.1 49.4 %all-to-all-start = ((bf16[8,4,128,128]{3,2,1,0:T(8,128)(2,1)}), bf16[8,4,128,128]{3,2,1,0:T(8,128)(2,1)S(1)}, u32[]{:S(2)}, u32[]{:S(2)}) async-start(bf16[8,4,128,128]{3,2,1,0:T(8,128)(2,1)} %get-tuple-element.13), calls=%async_computation | async-start | bytes 2097152 | tf_op jit(solution)/shard_map/all_to_all | solution.py:322
  8.5 12.6 %collective-permute-start = (bf16[512,128]{1,0:T(8,128)(2,1)S(1)}, bf16[512,128]{1,0:T(8,128)(2,1)S(1)}, u32[]{:S(2)}, u32[]{:S(2)}) collective-permute-start(bf16[512,128]{1,0:T(8,128)(2,1)S(1)} %copy-done.2), channel_id=1, source_target_pairs={{0,64},{1,449},{64,128},{65,1},{128,192},{129,65},{192,256},{193,1... | collective-permute-start | bytes 393224 | tf_op jit(solution)/shard_map/ppermute | solution.py:318
  19.1 16.7 %collective-permute-start.4 = (bf16[512,128]{1,0:T(8,128)(2,1)S(1)}, bf16[512,128]{1,0:T(8,128)(2,1)S(1)}, u32[]{:S(2)}, u32[]{:S(2)}) collective-permute-start(bf16[512,128]{1,0:T(8,128)(2,1)S(1)} %copy-done.2), channel_id=1, source_target_pairs={{0,448},{1,65},{64,0},{65,129},{128,64},{129,193},{192,128},{193,2... | collective-permute-start | bytes 393224 | tf_op jit(solution)/shard_map/ppermute | solution.py:319
  21.1 16.7 %collective-permute-start.1 = (bf16[512,128]{1,0:T(8,128)(2,1)S(1)}, bf16[512,128]{1,0:T(8,128)(2,1)S(1)}, u32[]{:S(2)}, u32[]{:S(2)}) collective-permute-start(bf16[512,128]{1,0:T(8,128)(2,1)S(1)} %collective-permute-done.refs_1_), channel_id=1, source_target_pairs={{0,64},{1,449},{64,128},{65,1},{128,192},{129,65},{192,256},{193,1... | collective-permute-start | bytes 393224 | tf_op jit(solution)/shard_map/ppermute | solution.py:318
  35.9 7.8 %collective-permute-start.5 = (bf16[512,128]{1,0:T(8,128)(2,1)S(1)}, bf16[512,128]{1,0:T(8,128)(2,1)S(1)}, u32[]{:S(2)}, u32[]{:S(2)}) collective-permute-start(bf16[512,128]{1,0:T(8,128)(2,1)S(1)} %collective-permute-done.4.refs_2_), channel_id=1, source_target_pairs={{0,448},{1,65},{64,0},{65,129},{128,64},{129,193},{192,128},{193,2... | collective-permute-start | bytes 393224 | tf_op jit(solution)/shard_map/ppermute | solution.py:319
  37.8 7.8 %collective-permute-start.2 = (bf16[512,128]{1,0:T(8,128)(2,1)S(1)}, bf16[512,128]{1,0:T(8,128)(2,1)S(1)}, u32[]{:S(2)}, u32[]{:S(2)}) collective-permute-start(bf16[512,128]{1,0:T(8,128)(2,1)S(1)} %collective-permute-done.1.refs_3_), channel_id=1, source_target_pairs={{0,64},{1,449},{64,128},{65,1},{128,192},{129,65},{192,256},{193,1... | collective-permute-start | bytes 393224 | tf_op jit(solution)/shard_map/ppermute | solution.py:318
  43.7 7.8 %collective-permute-start.6 = (bf16[512,128]{1,0:T(8,128)(2,1)S(1)}, bf16[512,128]{1,0:T(8,128)(2,1)S(1)}, u32[]{:S(2)}, u32[]{:S(2)}) collective-permute-start(bf16[512,128]{1,0:T(8,128)(2,1)S(1)} %collective-permute-done.5.refs_4_), channel_id=1, source_target_pairs={{0,448},{1,65},{64,0},{65,129},{128,64},{129,193},{192,128},{193,2... | collective-permute-start | bytes 393224 | tf_op jit(solution)/shard_map/ppermute | solution.py:319
  45.6 12.3 %collective-permute-start.3 = (bf16[512,128]{1,0:T(8,128)(2,1)S(1)}, bf16[512,128]{1,0:T(8,128)(2,1)S(1)}, u32[]{:S(2)}, u32[]{:S(2)}) collective-permute-start(bf16[512,128]{1,0:T(8,128)(2,1)S(1)} %collective-permute-done.2.refs_5_), channel_id=1, source_target_pairs={{0,64},{1,449},{64,128},{65,1},{128,192},{129,65},{192,256},{193,1... | collective-permute-start | bytes 393224 | tf_op jit(solution)/shard_map/ppermute | solution.py:321
  57.9 20.7 %copy-start = (bf16[512,4096]{1,0:T(8,128)(2,1)S(1)}, bf16[512,4096]{1,0:T(8,128)(2,1)}, u32[]{:S(2)}) copy-start(bf16[512,4096]{1,0:T(8,128)(2,1)} %weight.1) | copy-start | bytes 12582916
  80.2 9.7 %collective-permute-start.7 = (bf16[4,128,512]{2,1,0:T(8,128)(2,1)S(1)}, bf16[4,128,512]{2,1,0:T(8,128)(2,1)S(1)}, u32[]{:S(2)}, u32[]{:S(2)}) collective-permute-start(bf16[4,128,512]{2,1,0:T(8,128)(2,1)S(1)} %get-tuple-element.20), channel_id=1, source_target_pairs={{0,1},{1,0},{2,3},{3,2},{4,5},{5,4},{6,7},{7,6},{8,9},{9,8},{10,11... | collective-permute-start | bytes 1572872 | tf_op jit(solution)/shard_map/ppermute | solution.py:365

commit v7 on v6

--- a/solution.py
+++ b/solution.py
@@ -10,10 +10,11 @@
 
 HD = 128
 GROUP = 4
+FAR = 2
 BLOCKS = 8
 RING = 8
 STATS = 16
-PIECE = GROUP * HD + STATS
+PIECE = FAR * HD + STATS
 MASKED = -1e30
 FLOOR = -1e29
 FACTOR = math.log2(math.e) / math.sqrt(HD)
@@ -43,7 +44,7 @@
 
 
 def prepare_kernel(
-    spans, queries, keys, values, cache_keys, cache_values, own, sent, heads, kinds, sems
+    spans, queries, keys, values, cache_keys, cache_values, own, far_rows, near_rows, handed, heads, kinds, sems
 ):
     copies = [
         pltpu.make_async_copy(spans, kinds, sems.at[0]),
@@ -57,11 +58,31 @@
         copy.start()
     for copy in copies:
         copy.wait()
+    k, e, _ = position()
+    ends = (k == RING - 1) & (e == 1)
+    handed[...] = jnp.where(ends, own[: 2 * HD, :], own[2 * HD :, :])
     order = head_order(kinds)
     for s in range(GROUP):
         rows = heads[:, pl.ds(pl.multiple_of(order[s] * HD, HD), HD)]
-        for j in range(BLOCKS):
-            sent[j, s] = rows
+        target = far_rows if s < FAR else near_rows
+        target[s % FAR * HD : (s % FAR + 1) * HD, :] = rows
+
+
+def spread_kernel(far_rows, other_rows, own, prior, after, after_too, sent):
+    del after, after_too
+    first = lax.axis_index("e") == 0
+    lower = jnp.where(first, far_rows[...], other_rows[...])
+    upper = jnp.where(first, other_rows[...], far_rows[...])
+    for j in range(4):
+        sent[j, : 2 * HD, :] = lower
+        sent[j, 2 * HD : 4 * HD, :] = upper
+        sent[j, 4 * HD : 6 * HD, :] = own[2 * HD :, :]
+        sent[j, 6 * HD :, :] = prior[...]
+
+
+def query_rows(gathered, slot, first):
+    at = first // 4 * 2 * HD + slot * HD
+    return gathered[first % 4 : first % 4 + TILE // HD, at : at + HD, :].reshape(TILE, HD)
 
 
 def position():
@@ -105,7 +126,7 @@
 
 def first_kernel(spans, queries, *refs):
     kv = refs[: RING - 1]
-    sums, tops, near, near_tops, keys, flipped, scores = refs[RING - 1 :]
+    sums, tops, keys, flipped, scores = refs[RING - 1 :]
     order = head_order(spans)
     distances = sources()
     blocks = []
@@ -119,11 +140,11 @@
             ].T
     width = len(blocks) * HD
     flipped[HD:, :] = jnp.ones((STATS, width), jnp.bfloat16)
-    column, offset = offsets()
+    _, offset = offsets()
 
     def score(t):
         slot, first = tile_of(t)
-        rows = queries[first : first + TILE // HD, slot].reshape(TILE, HD)
+        rows = query_rows(queries, slot, first)
         top = jnp.full((8, TILE), FLOOR, jnp.float32)
         for n, (cached, start) in enumerate(blocks):
             found = masked_scores(
@@ -146,36 +167,48 @@
         sums[t] = dot(flipped[...], weights, NN)
         tops[t] = jnp.broadcast_to(top, (8, TILE))
 
-    k, e, x = position()
-    own = e * 4 + x
-    wraps = k == 0
-    n = jnp.where(lax.axis_index("c") == 0, 2, 4) + jnp.where(wraps, 0, 1)
-    at = pl.multiple_of(n * HD, HD)
-    before_keys = keys[pl.ds(at, HD), :]
-    before_values = flipped[:, pl.ds(at, HD)]
-    before_start = place(-1) + jnp.where(wraps, 0, CACHE)
-    own_start = place(0) + CACHE
-    span = jnp.where(
-        lax.broadcasted_iota(jnp.int32, (HD, TILE), 1) < HD, spans[order[2]], spans[order[3]]
-    )
-    near_offset = column - lax.broadcasted_iota(jnp.int32, (HD, TILE), 0)
-    for b in range(BLOCKS):
-        earlier = b < own
-        rows = queries[b, 2:4].reshape(TILE, HD)
-        found = dot(jnp.where(earlier, before_keys, keys[HD : 2 * HD, :]), rows, NT)
-        begin = CACHE + (k * BLOCKS + b) * HD
-        behind = near_offset + (begin - jnp.where(earlier, before_start, own_start))
-        found = jnp.where((behind >= 0) & (behind < span), found, MASKED)
-        top = jnp.maximum(jnp.max(found, axis=0, keepdims=True), FLOOR)
-        weights = jnp.exp2((found - top) * FACTOR).astype(jnp.bfloat16)
-        near[b] = dot(jnp.where(earlier, before_values, flipped[:, HD : 2 * HD]), weights, NN)
-        near_tops[b] = jnp.broadcast_to(top, (8, TILE))
-
     top = score(0)
     for t in range(TILES):
         later = score(t + 1) if t + 1 < TILES else None
         finish(t, top)
         top = later
+
+
+def near_kernel(spans, rows, own, gathered, out):
+    order = head_order(spans)
+    x = lax.axis_index("x")
+    column, _ = offsets()
+    behind = column - lax.broadcasted_iota(jnp.int32, (HD, TILE), 0)
+    span = jnp.where(
+        lax.broadcasted_iota(jnp.int32, (HD, TILE), 1) < HD, spans[order[2]], spans[order[3]]
+    )
+    found, values = [], []
+    for j in range(5):
+        if j < 4:
+            distance = jnp.where(j < x, x - j, x - j + 4) * HD
+            block = jnp.where(j < x, gathered[j, 4 * HD : 6 * HD, :], gathered[j, 6 * HD :, :])
+            key_rows, value_rows = block[:HD, :], block[HD:, :]
+        else:
+            distance = 0
+            key_rows, value_rows = own[2 * HD : 3 * HD, :], own[3 * HD :, :]
+        far = behind + distance
+        found.append(
+            jnp.where((far >= 0) & (far < span), dot(key_rows, rows[...], NT), MASKED)
+        )
+        values.append(value_rows)
+    top = highest(found[0])
+    for j in range(1, 5):
+        top = jnp.maximum(top, highest(found[j]))
+    top = jnp.max(top, axis=0, keepdims=True)
+    weights = jnp.concatenate(
+        [jnp.exp2((f - top) * FACTOR).astype(jnp.bfloat16) for f in found], axis=0
+    )
+    flipped = jnp.concatenate([v.T for v in values], axis=1)
+    flipped = jnp.concatenate([flipped, jnp.ones((STATS, 5 * HD), jnp.bfloat16)], axis=0)
+    summed = dot(flipped, weights, NN)
+    normal = summed[:HD, :] * (1.0 / summed[HD : HD + 1, :])
+    for s in range(2):
+        out[s] = normal[:, s * HD : (s + 1) * HD].T.astype(jnp.bfloat16)
 
 
 def write_stats(stats, block, slot, top, total):
@@ -186,7 +219,8 @@
         level = level - term
 
 
-def second_kernel(spans, queries, last, sums, tops, near, near_tops, out, stats):
+def second_kernel(spans, queries, last, sums, tops, after, out, stats):
+    del after
     order = head_order(spans)
     start = place(sources()[-1])
     _, offset = offsets()
@@ -199,20 +233,9 @@
         axis=1,
     )
     stats[...] = jnp.zeros_like(stats)
-
-    def emit(block, slot, top, summed):
-        total = summed[HD : HD + 1, :]
-        normal = summed[:HD, :] * (1.0 / jnp.maximum(total, 1e-30))
-        out[block, slot * HD : (slot + 1) * HD, :] = normal.astype(jnp.bfloat16)
-        write_stats(stats, block, slot, top, total)
-
-    for b in range(BLOCKS):
-        for j in range(2):
-            cut = slice(j * HD, (j + 1) * HD)
-            emit(b, 2 + j, near_tops[b, 0:1, cut], near[b, :, cut])
     for t in range(TILES):
         slot, first = tile_of(t)
-        rows = queries[first : first + TILE // HD, slot].reshape(TILE, HD)
+        rows = query_rows(queries, slot, first)
         found = [
             masked_scores(
                 spans, order, offset, last[2 * half * HD : (2 * half + 1) * HD, :],
@@ -227,16 +250,19 @@
         summed = sums[t] * jnp.exp2((before - top) * FACTOR) + dot(
             flipped, jnp.concatenate(weights, axis=0), NN
         )
+        total = summed[HD : HD + 1, :]
+        normal = summed[:HD, :] * (1.0 / jnp.maximum(total, 1e-30))
         for j in range(TILE // HD):
             cut = slice(j * HD, (j + 1) * HD)
-            emit(first + j, slot, top[:, cut], summed[:, cut])
-    out[:, GROUP * HD :, :] = stats[...].astype(jnp.bfloat16)
-
-
-def project_kernel(spans, parts, weight, out, kept, attn):
+            out[first + j, slot * HD : (slot + 1) * HD, :] = normal[:, cut].astype(jnp.bfloat16)
+            write_stats(stats, first + j, slot, top[:, cut], total[:, cut])
+    out[:, FAR * HD :, :] = stats[...].astype(jnp.bfloat16)
+
+
+def project_kernel(spans, parts, near, weight, out, kept, attn):
     order = head_order(spans)
-    for s in range(GROUP):
-        terms = parts[:, GROUP * HD :, :].astype(jnp.float32)
+    terms = parts[:, FAR * HD :, :].astype(jnp.float32)
+    for s in range(FAR):
         level = [
             terms[i, 4 * s : 4 * s + 1] + terms[i, 4 * s + 1 : 4 * s + 2] + terms[i, 4 * s + 2 : 4 * s + 3]
             for i in range(BLOCKS)
@@ -254,6 +280,8 @@
         attn[:, pl.ds(pl.multiple_of(order[s] * HD, HD), HD)] = (
             (summed * (1.0 / total)).T.astype(jnp.bfloat16)
         )
+    for s in range(FAR, GROUP):
+        attn[:, pl.ds(pl.multiple_of(order[s] * HD, HD), HD)] = near[s - FAR]
     rows = attn[...]
     mine = lax.axis_index("c")
     width = out.shape[2]
@@ -290,11 +318,13 @@
 
 def per_device(queries, keys, values, cache_keys, cache_values, spans, out_weight):
     bf16, f32 = jnp.bfloat16, jnp.float32
-    own, sent = call(
+    own, far_rows, near_rows, handed = call(
         prepare_kernel,
         [
             jax.ShapeDtypeStruct((4 * HD, HD), bf16),
-            jax.ShapeDtypeStruct((BLOCKS, GROUP, HD, HD), bf16),
+            jax.ShapeDtypeStruct((FAR * HD, HD), bf16),
+            jax.ShapeDtypeStruct((FAR * HD, HD), bf16),
+            jax.ShapeDtypeStruct((2 * HD, HD), bf16),
         ],
         [ANY] * 6,
         [
@@ -303,8 +333,12 @@
             pltpu.SemaphoreType.DMA((6,)),
         ],
         vmem=60,
-        moved=2**21,
+        moved=2**20,
     )(spans, queries, keys, values, cache_keys, cache_values)
+    other_rows = lax.ppermute(far_rows, "e", [(0, 1), (1, 0)])
+    prior = lax.ppermute(
+        handed, ("k", "e"), [(i, (i + 1) % (2 * RING)) for i in range(2 * RING)]
+    )
     routes = [
         [
             (2 * i + c, (i + (1 if c == turn else -1)) % RING * 2 + c)
@@ -319,7 +353,21 @@
         two = lax.ppermute(two, ("k", "c"), routes[1])
         kv += [one, two]
     last = lax.ppermute(one, ("k", "c"), routes[0])
-    grouped = lax.all_to_all(sent, ("e", "x"), 0, 0, tiled=True)
+    sent = call(
+        spread_kernel,
+        jax.ShapeDtypeStruct((4, 8 * HD, HD), bf16),
+        [VMEM] * 4 + [ANY] * 2,
+        moved=2**20,
+    )(far_rows, other_rows, own, prior, kv[3], kv[4])
+    grouped = lax.all_to_all(sent, "x", 0, 0, tiled=True)
+    near = call(
+        near_kernel,
+        jax.ShapeDtypeStruct((2, HD, HD), bf16),
+        [SMEM] + [VMEM] * 3,
+        flops=4 * 256 * 640 * 128,
+        moved=2**20,
+        exps=256 * 640,
+    )(spans, near_rows, own, grouped)
 
     near_blocks = 2 * (RING - 1)
     state = call(
@@ -327,8 +375,6 @@
         [
             jax.ShapeDtypeStruct((TILES, HD + STATS, TILE), f32),
             jax.ShapeDtypeStruct((TILES, 8, TILE), f32),
-            jax.ShapeDtypeStruct((BLOCKS, HD + STATS, TILE), f32),
-            jax.ShapeDtypeStruct((BLOCKS, 8, TILE), f32),
         ],
         [SMEM] + [VMEM] * RING,
         [
@@ -343,12 +389,12 @@
     partial = call(
         second_kernel,
         jax.ShapeDtypeStruct((BLOCKS, PIECE, HD), bf16),
-        [SMEM] + [VMEM] * 6,
+        [SMEM] + [VMEM] * 4 + [ANY],
         [pltpu.VMEM((BLOCKS, STATS, HD), f32)],
         flops=4 * 2048 * 256 * 128,
         moved=4 * 2**20,
         exps=2048 * 256,
-    )(spans, grouped, last, *state)
+    )(spans, grouped, last, *state, near)
     parts = lax.all_to_all(partial, ("e", "x"), 0, 0, tiled=True)
     width = out_weight.shape[1] // 8
     product, kept = call(
@@ -357,11 +403,11 @@
             jax.ShapeDtypeStruct((4, HD, width), bf16),
             jax.ShapeDtypeStruct((4, HD, width), f32),
         ],
-        [SMEM, VMEM, VMEM],
+        [SMEM, VMEM, VMEM, VMEM],
         [pltpu.VMEM((HD, GROUP * HD), bf16)],
         flops=2 * 128 * 512 * 4096,
         moved=5 * 2**20,
-    )(spans, parts, out_weight)
+    )(spans, parts, near, out_weight)
     received = lax.ppermute(product, "c", [(0, 1), (1, 0)])
     halves = call(
         add_kernel,

time: 104 us -> 104 us (level)
  blocking collectives: 30.7 us -> 25.6 us
  local copies, waits for them, and re-layouts: 0.02 us -> 4.14 us
  waiting for transfers between devices: 10.8 us -> 7.71 us
  starting transfers between devices: 48.2 us -> 51.2 us
    ppermute x3, waiting for transfers between devices: 9.26 us -> 0.01 us  [per_device(): two = lax.ppermute(two, ('k', 'c'), routes[1])]
    ppermute x0 -> x2, starting transfers between devices: none -> 5.28 us  [the longest x1 2.7 us: per_device(): other_rows = lax.ppermute(far_rows, 'e', [(0, 1), (1, 0)])]
    all_to_all x1, blocking collectives: 18.1 us -> 13.7 us  [per_device(): parts = lax.all_to_all(partial, ('e', 'x'), 0, 0, tiled=True)]
    ppermute x0 -> x2, waiting for transfers between devices: none -> 4.23 us  [the longest x1 3.94 us: per_device(): lax.ppermute(handed, ('k', 'e'), [(i, (i + 1) % (2 * RING)) for i in rang...]
    unnamed x6 -> x12, local copies, waits for them, and re-layouts: 0.02 us -> 4.14 us
    all_to_all x1, starting transfers between devices: 6.35 us -> 3.62 us  [per_device(): grouped = lax.all_to_all(sent, 'x', 0, 0, tiled=True)]
    pallas_call x0 -> x2, Pallas kernels: none -> 2.36 us  [the longest x1 1.22 us: per_device(): call(near_kernel, jax.ShapeDtypeStruct((2, HD, HD), bf16), [SMEM] + [VMEM...]
    ppermute x3, waiting for transfers between devices: 0.01 us -> 1.96 us  [per_device(): one = lax.ppermute(one, ('k', 'c'), routes[0])]
  transfers between devices with their start and end apart: 9 -> 11, of which waited for: 4 -> 5; matrix products, arithmetic and copies ran while one was open for 0% -> 0% of each run, Pallas kernels for 6% -> 7%
where the time goes in v7:
time: 104 us; the launch traced here: 103 us
  starting transfers between devices  51.2 us (49%)
  blocking collectives  25.6 us (25%)
  Pallas kernels  14.5 us (14%)
  waiting for transfers between devices  7.71 us (7%)
  local copies, waits for them, and re-layouts  4.14 us (4%)
    ppermute x3, starting transfers between devices, per_device(): one = lax.ppermute(one, ('k', 'c'), routes[0])  23.3 us
    all_to_all x1, blocking collectives, per_device(): parts = lax.all_to_all(partial, ('e', 'x'), 0, 0, tiled=True)  13.7 us
    all_to_all x1, blocking collectives, per_device(): shares = lax.all_to_all(halves, 'y', 0, 0, tiled=True)  11.9 us
    ppermute x1, starting transfers between devices, per_device(): received = lax.ppermute(product, 'c', [(0, 1), (1, 0)])  8.41 us
    ppermute x3, starting transfers between devices, per_device(): two = lax.ppermute(two, ('k', 'c'), routes[1])  5.76 us
    pallas_call x1, Pallas kernels, per_device(): call(first_kernel, [jax.ShapeDtypeStruct((TILES, HD + STATS, TILE), f32),...  5.52 us
    ppermute x1, starting transfers between devices, per_device(): last = lax.ppermute(one, ('k', 'c'), routes[0])  4.79 us
    unnamed x12, local copies, waits for them, and re-layouts  4.14 us
  transfers between devices with their start and end apart: 11, of which 5 were waited for; matrix products, arithmetic and copies ran while one was open for 0% of the time, Pallas kernels for 7%

profile of v7, /device:TPU:1, one launch (start us, length us, event | category | flops | bytes accessed | tf_op | source)
XLA Modules:
  0.0 103.3 jit_solution(15843572469300608981)
XLA Ops:
  0.0 1.7 %shard_map.73 = (bf16[512,128]{1,0:T(8,128)(2,1)}, bf16[256,128]{1,0:T(8,128)(2,1)}, bf16[256,128]{1,0:T(8,128)(2,1)}, bf16[256,128]{1,0:T(8,128)(2,1)}) custom-call(s32[4]{0:T(128)} %spans.9, bf16[128,512]{1,0:T(8,128)(2,1)} %queries.1, bf16[128,128]{1,0:T(8,128)(2,1)} %keys.1, bf16[128,128]{1,0:T(8,128)(2,1)} %values.1, bf16[128,128]{1,0:T(8,128)(2,1)} %cache_keys.1, ...), custom_call_target="tpu_custom_call" | custom-call | bytes 1048576 | tf_op jit(solution)/shard_map/pallas_call | solution.py:321
  1.7 12.4 %collective-permute-start.2 = (bf16[512,128]{1,0:T(8,128)(2,1)}, bf16[512,128]{1,0:T(8,128)(2,1)S(1)}, u32[]{:S(2)}, u32[]{:S(2)}) collective-permute-start(bf16[512,128]{1,0:T(8,128)(2,1)} %get-tuple-element.14.own.refs_0_), channel_id=1, source_target_pairs={{0,64},{1,449},{64,128},{65,1},{128,192},{129,65},{192,256},{193,1... | collective-permute-start | bytes 393224 | tf_op jit(solution)/shard_map/ppermute | solution.py:352
  14.1 1.9 %collective-permute-start.4 = (bf16[512,128]{1,0:T(8,128)(2,1)}, bf16[512,128]{1,0:T(8,128)(2,1)S(1)}, u32[]{:S(2)}, u32[]{:S(2)}) collective-permute-start(bf16[512,128]{1,0:T(8,128)(2,1)} %get-tuple-element.14.own.refs_0_), channel_id=1, source_target_pairs={{0,448},{1,65},{64,0},{65,129},{128,64},{129,193},{192,128},{193,2... | collective-permute-start | bytes 393224 | tf_op jit(solution)/shard_map/ppermute | solution.py:353
  16.1 0.8 collective-permute-done.2.refs_1_
  16.9 6.7 %collective-permute-start.3 = (bf16[512,128]{1,0:T(8,128)(2,1)S(1)}, bf16[512,128]{1,0:T(8,128)(2,1)S(1)}, u32[]{:S(2)}, u32[]{:S(2)}) collective-permute-start(bf16[512,128]{1,0:T(8,128)(2,1)S(1)} %collective-permute-done.2.refs_1_), channel_id=1, source_target_pairs={{0,64},{1,449},{64,128},{65,1},{128,192},{129,65},{192,256},{193,1... | collective-permute-start | bytes 393224 | tf_op jit(solution)/shard_map/ppermute | solution.py:352
  23.6 0.0 collective-permute-done.4.refs_2_
  23.6 1.9 %collective-permute-start.5 = (bf16[512,128]{1,0:T(8,128)(2,1)S(1)}, bf16[512,128]{1,0:T(8,128)(2,1)S(1)}, u32[]{:S(2)}, u32[]{:S(2)}) collective-permute-start(bf16[512,128]{1,0:T(8,128)(2,1)S(1)} %collective-permute-done.4.refs_2_), channel_id=1, source_target_pairs={{0,448},{1,65},{64,0},{65,129},{128,64},{129,193},{192,128},{193,2... | collective-permute-start | bytes 393224 | tf_op jit(solution)/shard_map/ppermute | solution.py:353
  25.5 2.7 %collective-permute-start = (bf16[256,128]{1,0:T(8,128)(2,1)}, bf16[256,128]{1,0:T(8,128)(2,1)S(1)}, u32[]{:S(2)}, u32[]{:S(2)}) collective-permute-start(bf16[256,128]{1,0:T(8,128)(2,1)} %get-tuple-element.13.far_rows), channel_id=1, source_target_pairs={{0,32},{32,0},{1,33},{33,1},{2,34},{34,2},{3,35},{35,3},{4,36},{36... | collective-permute-start | bytes 196616 | tf_op jit(solution)/shard_map/ppermute | solution.py:338
  28.2 2.6 %collective-permute-start.1 = (bf16[256,128]{1,0:T(8,128)(2,1)}, bf16[256,128]{1,0:T(8,128)(2,1)S(1)}, u32[]{:S(2)}, u32[]{:S(2)}) collective-permute-start(bf16[256,128]{1,0:T(8,128)(2,1)} %get-tuple-element.15), channel_id=1, source_target_pairs={{0,32},{32,64},{64,96},{96,128},{128,160},{160,192},{192,224},{224... | collective-permute-start | bytes 196616 | tf_op jit(solution)/shard_map/ppermute | solution.py:339
  30.8 0.3 collective-permute-done.other_rows
  31.1 3.9 %collective-permute-done.1.prior = bf16[256,128]{1,0:T(8,128)(2,1)S(1)} collective-permute-done((bf16[256,128]{1,0:T(8,128)(2,1)}, bf16[256,128]{1,0:T(8,128)(2,1)S(1)}, u32[]{:S(2)}, u32[]{:S(2)}) %collective-permute-start.1) | collective-permute-done | bytes 65568 | tf_op jit(solution)/shard_map/ppermute | solution.py:339
  35.0 0.0 collective-permute-done.3.after.refs_3_
  35.0 0.0 collective-permute-done.5.after_too.refs_4_
  35.0 0.0 copy-start.1
  35.0 0.9 copy-done.1
  35.9 0.0 copy-start.4
  35.9 0.8 copy-done.4
  36.8 1.1 %shard_map.74 = bf16[4,1024,128]{2,1,0:T(8,128)(2,1)} custom-call(bf16[256,128]{1,0:T(8,128)(2,1)S(1)} %copy-done.4, bf16[256,128]{1,0:T(8,128)(2,1)S(1)} %collective-permute-done.other_rows, bf16[512,128]{1,0:T(8,128)(2,1)S(1)} %copy-done.1, bf16[256,128]{1,0:T(8,128)(2,1)S(1)} %collective-permute-done.1.prior, ...), custom_call_target="tpu_custom_call" | custom-call | bytes 1048576 | tf_op jit(solution)/shard_map/pallas_call | solution.py:356
  37.9 3.6 %all-to-all-start = ((bf16[4,1024,128]{2,1,0:T(8,128)(2,1)}), bf16[4,1024,128]{2,1,0:T(8,128)(2,1)S(1)}, u32[]{:S(2)}, u32[]{:S(2)}) async-start(bf16[4,1024,128]{2,1,0:T(8,128)(2,1)} %shard_map.74), calls=%async_computation | async-start | bytes 2097152 | tf_op jit(solution)/shard_map/all_to_all | solution.py:362
  41.5 4.2 %collective-permute-start.6 = (bf16[512,128]{1,0:T(8,128)(2,1)S(1)}, bf16[512,128]{1,0:T(8,128)(2,1)S(1)}, u32[]{:S(2)}, u32[]{:S(2)}) collective-permute-start(bf16[512,128]{1,0:T(8,128)(2,1)S(1)} %collective-permute-done.3.after.refs_3_), channel_id=1, source_target_pairs={{0,64},{1,449},{64,128},{65,1},{128,192},{129,65},{192,256},{193,1... | collective-permute-start | bytes 393224 | tf_op jit(solution)/shard_map/ppermute | solution.py:352
  45.8 1.9 %collective-permute-start.8 = (bf16[512,128]{1,0:T(8,128)(2,1)S(1)}, bf16[512,128]{1,0:T(8,128)(2,1)S(1)}, u32[]{:S(2)}, u32[]{:S(2)}) collective-permute-start(bf16[512,128]{1,0:T(8,128)(2,1)S(1)} %collective-permute-done.5.after_too.refs_4_), channel_id=1, source_target_pairs={{0,448},{1,65},{64,0},{65,129},{128,64},{129,193},{192,128},{193,2... | collective-permute-start | bytes 393224 | tf_op jit(solution)/shard_map/ppermute | solution.py:353
  47.7 1.1 %collective-permute-done.6.refs_5_ = bf16[512,128]{1,0:T(8,128)(2,1)S(1)} collective-permute-done((bf16[512,128]{1,0:T(8,128)(2,1)S(1)}, bf16[512,128]{1,0:T(8,128)(2,1)S(1)}, u32[]{:S(2)}, u32[]{:S(2)}) %collective-permute-start.6) | collective-permute-done | bytes 131104 | tf_op jit(solution)/shard_map/ppermute | solution.py:352
  48.9 4.8 %collective-permute-start.7 = (bf16[512,128]{1,0:T(8,128)(2,1)S(1)}, bf16[512,128]{1,0:T(8,128)(2,1)S(1)}, u32[]{:S(2)}, u32[]{:S(2)}) collective-permute-start(bf16[512,128]{1,0:T(8,128)(2,1)S(1)} %collective-permute-done.6.refs_5_), channel_id=1, source_target_pairs={{0,64},{1,449},{64,128},{65,1},{128,192},{129,65},{192,256},{193,1... | collective-permute-start | bytes 393224 | tf_op jit(solution)/shard_map/ppermute | solution.py:355
  53.7 0.0 all-to-all-done.queries.gathered
  53.7 0.0 copy-start.2
  53.7 0.9 copy-done.2
  54.6 0.0 copy-start.3
  54.6 0.8 copy-done.3
  55.4 0.0 copy-start.5
  55.4 0.7 copy-done.5
  56.1 1.2 %shard_map.76.after.near = bf16[2,128,128]{2,1,0:T(8,128)(2,1)S(1)} custom-call(s32[4]{0:T(128)S(1)} %copy-done.5, bf16[256,128]{1,0:T(8,128)(2,1)S(1)} %copy-done.3, bf16[512,128]{1,0:T(8,128)(2,1)S(1)} %copy-done.2, bf16[4,1024,128]{2,1,0:T(8,128)(2,1)S(1)} %all-to-all-done.queries.gathered), custom_call_target="tpu_custom_call" | custom-call | flops 83886080 | bytes 1048576 | tf_op jit(solution)/shard_map/pallas_call | solution.py:363
  57.3 0.0 copy-start
  57.3 0.0 collective-permute-done.8.refs_6_
  57.3 5.5 %shard_map.75 = (f32[8,144,256]{2,1,0:T(8,128)S(1)}, f32[8,8,256]{2,1,0:T(8,128)S(1)}) custom-call(s32[4]{0:T(128)S(1)} %copy-done.5, bf16[4,1024,128]{2,1,0:T(8,128)(2,1)S(1)} %all-to-all-done.queries.gathered, bf16[512,128]{1,0:T(8,128)(2,1)S(1)} %copy-done.2, bf16[512,128]{1,0:T(8,128)(2,1)S(1)} %collective-permute-done.2.refs_1_, ...), custom_call_target="tpu_custom_call" | custom-call | flops 1879048192 | bytes 4194304 | tf_op jit(solution)/shard_map/pallas_call | solution.py:373
  62.8 0.0 collective-permute-done.7.last
  62.9 2.5 %shard_map.77 = bf16[8,272,128]{2,1,0:T(8,128)(2,1)S(1)} custom-call(s32[4]{0:T(128)S(1)} %copy-done.5, bf16[4,1024,128]{2,1,0:T(8,128)(2,1)S(1)} %all-to-all-done.queries.gathered, bf16[512,128]{1,0:T(8,128)(2,1)S(1)} %collective-permute-done.7.last, f32[8,144,256]{2,1,0:T(8,128)S(1)} %get-tuple-element.16.sums, f32[8,8,256]{2,1,0:T(8,128)S(1)} %get-tuple-element.17.tops, ...), custom_call_target="tpu_custom_call" | custom-call | flops 268435456 | bytes 4194304 | tf_op jit(solution)/shard_map/pallas_call | solution.py:389
  65.4 13.7 %all_to_all.15.parts = bf16[8,272,128]{2,1,0:T(8,128)(2,1)S(1)} all-to-all(bf16[8,272,128]{2,1,0:T(8,128)(2,1)S(1)} %shard_map.77), channel_id=1, replica_groups=mesh['k'=8,'e'=2,'x'=4,'y'=4,'c'=2] {'e','x'}, dimensions={0} | all-to-all | bytes 1114112 | tf_op jit(solution)/shard_map/all_to_all | solution.py:398
  79.1 0.0 copy-done
  79.1 1.5 %shard_map.78 = (bf16[4,128,512]{2,1,0:T(8,128)(2,1)S(1)}, f32[4,128,512]{2,1,0:T(8,128)S(1)}) custom-call(s32[4]{0:T(128)S(1)} %copy-done.5, bf16[8,272,128]{2,1,0:T(8,128)(2,1)S(1)} %all_to_all.15.parts, bf16[2,128,128]{2,1,0:T(8,128)(2,1)S(1)} %shard_map.76.after.near, bf16[512,4096]{1,0:T(8,128)(2,1)S(1)} %copy-done), custom_call_target="tpu_custom_call" | custom-call | flops 536870912 | bytes 5242880 | tf_op jit(solution)/shard_map/pallas_call | solution.py:400
  80.5 8.4 %collective-permute-start.9 = (bf16[4,128,512]{2,1,0:T(8,128)(2,1)S(1)}, bf16[4,128,512]{2,1,0:T(8,128)(2,1)S(1)}, u32[]{:S(2)}, u32[]{:S(2)}) collective-permute-start(bf16[4,128,512]{2,1,0:T(8,128)(2,1)S(1)} %get-tuple-element.20), channel_id=1, source_target_pairs={{0,1},{1,0},{2,3},{3,2},{4,5},{5,4},{6,7},{7,6},{8,9},{9,8},{10,11... | collective-permute-start | bytes 1572872 | tf_op jit(solution)/shard_map/ppermute | solution.py:411
  88.9 1.5 %collective-permute-done.9.received = bf16[4,128,512]{2,1,0:T(8,128)(2,1)S(1)} collective-permute-done((bf16[4,128,512]{2,1,0:T(8,128)(2,1)S(1)}, bf16[4,128,512]{2,1,0:T(8,128)(2,1)S(1)}, u32[]{:S(2)}, u32[]{:S(2)}) %collective-permute-start.9) | collective-permute-done | bytes 524320 | tf_op jit(solution)/shard_map/ppermute | solution.py:411
  90.5 0.1 shard_map.79
  90.6 11.9 %all_to_all.16.shares = bf16[4,128,512]{2,1,0:T(8,128)(2,1)S(1)} all-to-all(bf16[4,128,512]{2,1,0:T(8,128)(2,1)S(1)} %shard_map.79), channel_id=1, replica_groups=mesh['k'=8,'e'=2,'x'=4,'y'=4,'c'=2] {'y'}, dimensions={0} | all-to-all | bytes 1048576 | tf_op jit(solution)/shard_map/all_to_all | solution.py:418
  102.5 0.8 shard_map.80
Async XLA Ops:
  1.7 15.1 %collective-permute-start.2 = (bf16[512,128]{1,0:T(8,128)(2,1)}, bf16[512,128]{1,0:T(8,128)(2,1)S(1)}, u32[]{:S(2)}, u32[]{:S(2)}) collective-permute-start(bf16[512,128]{1,0:T(8,128)(2,1)} %get-tuple-element.14.own.refs_0_), channel_id=1, source_target_pairs={{0,64},{1,449},{64,128},{65,1},{128,192},{129,65},{192,256},{193,1... | collective-permute-start | bytes 393224 | tf_op jit(solution)/shard_map/ppermute | solution.py:352
  14.1 9.4 %collective-permute-start.4 = (bf16[512,128]{1,0:T(8,128)(2,1)}, bf16[512,128]{1,0:T(8,128)(2,1)S(1)}, u32[]{:S(2)}, u32[]{:S(2)}) collective-permute-start(bf16[512,128]{1,0:T(8,128)(2,1)} %get-tuple-element.14.own.refs_0_), channel_id=1, source_target_pairs={{0,448},{1,65},{64,0},{65,129},{128,64},{129,193},{192,128},{193,2... | collective-permute-start | bytes 393224 | tf_op jit(solution)/shard_map/ppermute | solution.py:353
  16.9 18.2 %collective-permute-start.3 = (bf16[512,128]{1,0:T(8,128)(2,1)S(1)}, bf16[512,128]{1,0:T(8,128)(2,1)S(1)}, u32[]{:S(2)}, u32[]{:S(2)}) collective-permute-start(bf16[512,128]{1,0:T(8,128)(2,1)S(1)} %collective-permute-done.2.refs_1_), channel_id=1, source_target_pairs={{0,64},{1,449},{64,128},{65,1},{128,192},{129,65},{192,256},{193,1... | collective-permute-start | bytes 393224 | tf_op jit(solution)/shard_map/ppermute | solution.py:352
  23.6 11.5 %collective-permute-start.5 = (bf16[512,128]{1,0:T(8,128)(2,1)S(1)}, bf16[512,128]{1,0:T(8,128)(2,1)S(1)}, u32[]{:S(2)}, u32[]{:S(2)}) collective-permute-start(bf16[512,128]{1,0:T(8,128)(2,1)S(1)} %collective-permute-done.4.refs_2_), channel_id=1, source_target_pairs={{0,448},{1,65},{64,0},{65,129},{128,64},{129,193},{192,128},{193,2... | collective-permute-start | bytes 393224 | tf_op jit(solution)/shard_map/ppermute | solution.py:353
  25.5 5.6 %collective-permute-start = (bf16[256,128]{1,0:T(8,128)(2,1)}, bf16[256,128]{1,0:T(8,128)(2,1)S(1)}, u32[]{:S(2)}, u32[]{:S(2)}) collective-permute-start(bf16[256,128]{1,0:T(8,128)(2,1)} %get-tuple-element.13.far_rows), channel_id=1, source_target_pairs={{0,32},{32,0},{1,33},{33,1},{2,34},{34,2},{3,35},{35,3},{4,36},{36... | collective-permute-start | bytes 196616 | tf_op jit(solution)/shard_map/ppermute | solution.py:338
  28.2 6.8 %collective-permute-start.1 = (bf16[256,128]{1,0:T(8,128)(2,1)}, bf16[256,128]{1,0:T(8,128)(2,1)S(1)}, u32[]{:S(2)}, u32[]{:S(2)}) collective-permute-start(bf16[256,128]{1,0:T(8,128)(2,1)} %get-tuple-element.15), channel_id=1, source_target_pairs={{0,32},{32,64},{64,96},{96,128},{128,160},{160,192},{192,224},{224... | collective-permute-start | bytes 196616 | tf_op jit(solution)/shard_map/ppermute | solution.py:339
  35.0 0.9 copy-start.1
  35.9 0.8 copy-start.4
  37.9 15.7 %all-to-all-start = ((bf16[4,1024,128]{2,1,0:T(8,128)(2,1)}), bf16[4,1024,128]{2,1,0:T(8,128)(2,1)S(1)}, u32[]{:S(2)}, u32[]{:S(2)}) async-start(bf16[4,1024,128]{2,1,0:T(8,128)(2,1)} %shard_map.74), calls=%async_computation | async-start | bytes 2097152 | tf_op jit(solution)/shard_map/all_to_all | solution.py:362
  41.5 7.3 %collective-permute-start.6 = (bf16[512,128]{1,0:T(8,128)(2,1)S(1)}, bf16[512,128]{1,0:T(8,128)(2,1)S(1)}, u32[]{:S(2)}, u32[]{:S(2)}) collective-permute-start(bf16[512,128]{1,0:T(8,128)(2,1)S(1)} %collective-permute-done.3.after.refs_3_), channel_id=1, source_target_pairs={{0,64},{1,449},{64,128},{65,1},{128,192},{129,65},{192,256},{193,1... | collective-permute-start | bytes 393224 | tf_op jit(solution)/shard_map/ppermute | solution.py:352
  45.8 11.5 %collective-permute-start.8 = (bf16[512,128]{1,0:T(8,128)(2,1)S(1)}, bf16[512,128]{1,0:T(8,128)(2,1)S(1)}, u32[]{:S(2)}, u32[]{:S(2)}) collective-permute-start(bf16[512,128]{1,0:T(8,128)(2,1)S(1)} %collective-permute-done.5.after_too.refs_4_), channel_id=1, source_target_pairs={{0,448},{1,65},{64,0},{65,129},{128,64},{129,193},{192,128},{193,2... | collective-permute-start | bytes 393224 | tf_op jit(solution)/shard_map/ppermute | solution.py:353
  48.9 14.0 %collective-permute-start.7 = (bf16[512,128]{1,0:T(8,128)(2,1)S(1)}, bf16[512,128]{1,0:T(8,128)(2,1)S(1)}, u32[]{:S(2)}, u32[]{:S(2)}) collective-permute-start(bf16[512,128]{1,0:T(8,128)(2,1)S(1)} %collective-permute-done.6.refs_5_), channel_id=1, source_target_pairs={{0,64},{1,449},{64,128},{65,1},{128,192},{129,65},{192,256},{193,1... | collective-permute-start | bytes 393224 | tf_op jit(solution)/shard_map/ppermute | solution.py:355
  53.7 0.9 copy-start.2
  54.6 0.8 copy-start.3
  55.4 0.7 copy-start.5
  57.3 21.8 %copy-start = (bf16[512,4096]{1,0:T(8,128)(2,1)S(1)}, bf16[512,4096]{1,0:T(8,128)(2,1)}, u32[]{:S(2)}) copy-start(bf16[512,4096]{1,0:T(8,128)(2,1)} %weight.1) | copy-start | bytes 12582916
  80.5 9.9 %collective-permute-start.9 = (bf16[4,128,512]{2,1,0:T(8,128)(2,1)S(1)}, bf16[4,128,512]{2,1,0:T(8,128)(2,1)S(1)}, u32[]{:S(2)}, u32[]{:S(2)}) collective-permute-start(bf16[4,128,512]{2,1,0:T(8,128)(2,1)S(1)} %get-tuple-element.20), channel_id=1, source_target_pairs={{0,1},{1,0},{2,3},{3,2},{4,5},{5,4},{6,7},{7,6},{8,9},{9,8},{10,11... | collective-permute-start | bytes 1572872 | tf_op jit(solution)/shard_map/ppermute | solution.py:411

commit v8 on v6

--- a/solution.py
+++ b/solution.py
@@ -10,10 +10,11 @@
 
 HD = 128
 GROUP = 4
+FAR = 2
 BLOCKS = 8
 RING = 8
 STATS = 16
-PIECE = GROUP * HD + STATS
+PIECE = FAR * HD + STATS
 MASKED = -1e30
 FLOOR = -1e29
 FACTOR = math.log2(math.e) / math.sqrt(HD)
@@ -43,7 +44,7 @@
 
 
 def prepare_kernel(
-    spans, queries, keys, values, cache_keys, cache_values, own, sent, heads, kinds, sems
+    spans, queries, keys, values, cache_keys, cache_values, own, own_rows, heads, kinds, sems
 ):
     copies = [
         pltpu.make_async_copy(spans, kinds, sems.at[0]),
@@ -60,8 +61,26 @@
     order = head_order(kinds)
     for s in range(GROUP):
         rows = heads[:, pl.ds(pl.multiple_of(order[s] * HD, HD), HD)]
-        for j in range(BLOCKS):
-            sent[j, s] = rows
+        own_rows[s * HD : (s + 1) * HD, :] = rows
+
+
+def hand_kernel(own_rows, own, one, two, sent, held, near_rows):
+    k, e, x = position()
+    me = e * 4 + x
+    below = jnp.where(lax.axis_index("c") == 0, one[...], two[...])
+    prior = jnp.where(k == 0, below[: 2 * HD, :], below[2 * HD :, :])
+    block = own[2 * HD :, :]
+    rows = own_rows[: FAR * HD, :]
+    near_rows[...] = own_rows[FAR * HD :, :]
+    held[...] = own[...]
+    for j in range(BLOCKS):
+        sent[j, : FAR * HD, :] = rows
+        sent[j, FAR * HD :, :] = jnp.where(j >= me, block, prior)
+
+
+def query_rows(grouped, slot, first):
+    at = slot * HD
+    return grouped[first : first + TILE // HD, at : at + HD, :].reshape(TILE, HD)
 
 
 def position():
@@ -103,9 +122,40 @@
     return jnp.max(found.reshape(HD // 8, 8, found.shape[1]), axis=0)
 
 
-def first_kernel(spans, queries, *refs):
+def near_heads(spans, order, rows, grouped, out):
+    _, e, x = position()
+    me = e * 4 + x
+    column, _ = offsets()
+    behind = column - lax.broadcasted_iota(jnp.int32, (HD, TILE), 0)
+    span = jnp.where(
+        lax.broadcasted_iota(jnp.int32, (HD, TILE), 1) < HD, spans[order[2]], spans[order[3]]
+    )
+    found, values = [], []
+    for j in range(5):
+        block = grouped[lax.rem(me - j + BLOCKS, BLOCKS), FAR * HD :, :]
+        far = behind + j * HD
+        found.append(
+            jnp.where((far >= 0) & (far < span), dot(block[:HD, :], rows[...], NT), MASKED)
+        )
+        values.append(block[HD:, :])
+    top = highest(found[0])
+    for j in range(1, 5):
+        top = jnp.maximum(top, highest(found[j]))
+    top = jnp.max(top, axis=0, keepdims=True)
+    weights = jnp.concatenate(
+        [jnp.exp2((f - top) * FACTOR).astype(jnp.bfloat16) for f in found], axis=0
+    )
+    flipped = jnp.concatenate([v.T for v in values], axis=1)
+    flipped = jnp.concatenate([flipped, jnp.ones((STATS, 5 * HD), jnp.bfloat16)], axis=0)
+    summed = dot(flipped, weights, NN)
+    normal = summed[:HD, :] * (1.0 / summed[HD : HD + 1, :])
+    for s in range(2):
+        out[s] = normal[:, s * HD : (s + 1) * HD].T.astype(jnp.bfloat16)
+
+
+def first_kernel(spans, near_rows, queries, *refs):
     kv = refs[: RING - 1]
-    sums, tops, near, near_tops, keys, flipped, scores = refs[RING - 1 :]
+    sums, tops, near, keys, flipped, scores = refs[RING - 1 :]
     order = head_order(spans)
     distances = sources()
     blocks = []
@@ -119,11 +169,11 @@
             ].T
     width = len(blocks) * HD
     flipped[HD:, :] = jnp.ones((STATS, width), jnp.bfloat16)
-    column, offset = offsets()
+    _, offset = offsets()
 
     def score(t):
         slot, first = tile_of(t)
-        rows = queries[first : first + TILE // HD, slot].reshape(TILE, HD)
+        rows = query_rows(queries, slot, first)
         top = jnp.full((8, TILE), FLOOR, jnp.float32)
         for n, (cached, start) in enumerate(blocks):
             found = masked_scores(
@@ -146,31 +196,7 @@
         sums[t] = dot(flipped[...], weights, NN)
         tops[t] = jnp.broadcast_to(top, (8, TILE))
 
-    k, e, x = position()
-    own = e * 4 + x
-    wraps = k == 0
-    n = jnp.where(lax.axis_index("c") == 0, 2, 4) + jnp.where(wraps, 0, 1)
-    at = pl.multiple_of(n * HD, HD)
-    before_keys = keys[pl.ds(at, HD), :]
-    before_values = flipped[:, pl.ds(at, HD)]
-    before_start = place(-1) + jnp.where(wraps, 0, CACHE)
-    own_start = place(0) + CACHE
-    span = jnp.where(
-        lax.broadcasted_iota(jnp.int32, (HD, TILE), 1) < HD, spans[order[2]], spans[order[3]]
-    )
-    near_offset = column - lax.broadcasted_iota(jnp.int32, (HD, TILE), 0)
-    for b in range(BLOCKS):
-        earlier = b < own
-        rows = queries[b, 2:4].reshape(TILE, HD)
-        found = dot(jnp.where(earlier, before_keys, keys[HD : 2 * HD, :]), rows, NT)
-        begin = CACHE + (k * BLOCKS + b) * HD
-        behind = near_offset + (begin - jnp.where(earlier, before_start, own_start))
-        found = jnp.where((behind >= 0) & (behind < span), found, MASKED)
-        top = jnp.maximum(jnp.max(found, axis=0, keepdims=True), FLOOR)
-        weights = jnp.exp2((found - top) * FACTOR).astype(jnp.bfloat16)
-        near[b] = dot(jnp.where(earlier, before_values, flipped[:, HD : 2 * HD]), weights, NN)
-        near_tops[b] = jnp.broadcast_to(top, (8, TILE))
-
+    near_heads(spans, order, near_rows, queries, near)
     top = score(0)
     for t in range(TILES):
         later = score(t + 1) if t + 1 < TILES else None
@@ -186,7 +212,7 @@
         level = level - term
 
 
-def second_kernel(spans, queries, last, sums, tops, near, near_tops, out, stats):
+def second_kernel(spans, queries, last, sums, tops, out, stats):
     order = head_order(spans)
     start = place(sources()[-1])
     _, offset = offsets()
@@ -199,20 +225,9 @@
         axis=1,
     )
     stats[...] = jnp.zeros_like(stats)
-
-    def emit(block, slot, top, summed):
-        total = summed[HD : HD + 1, :]
-        normal = summed[:HD, :] * (1.0 / jnp.maximum(total, 1e-30))
-        out[block, slot * HD : (slot + 1) * HD, :] = normal.astype(jnp.bfloat16)
-        write_stats(stats, block, slot, top, total)
-
-    for b in range(BLOCKS):
-        for j in range(2):
-            cut = slice(j * HD, (j + 1) * HD)
-            emit(b, 2 + j, near_tops[b, 0:1, cut], near[b, :, cut])
     for t in range(TILES):
         slot, first = tile_of(t)
-        rows = queries[first : first + TILE // HD, slot].reshape(TILE, HD)
+        rows = query_rows(queries, slot, first)
         found = [
             masked_scores(
                 spans, order, offset, last[2 * half * HD : (2 * half + 1) * HD, :],
@@ -227,16 +242,19 @@
         summed = sums[t] * jnp.exp2((before - top) * FACTOR) + dot(
             flipped, jnp.concatenate(weights, axis=0), NN
         )
+        total = summed[HD : HD + 1, :]
+        normal = summed[:HD, :] * (1.0 / jnp.maximum(total, 1e-30))
         for j in range(TILE // HD):
             cut = slice(j * HD, (j + 1) * HD)
-            emit(first + j, slot, top[:, cut], summed[:, cut])
-    out[:, GROUP * HD :, :] = stats[...].astype(jnp.bfloat16)
-
-
-def project_kernel(spans, parts, weight, out, kept, attn):
+            out[first + j, slot * HD : (slot + 1) * HD, :] = normal[:, cut].astype(jnp.bfloat16)
+            write_stats(stats, first + j, slot, top[:, cut], total[:, cut])
+    out[:, FAR * HD :, :] = stats[...].astype(jnp.bfloat16)
+
+
+def project_kernel(spans, parts, near, weight, out, kept, attn):
     order = head_order(spans)
-    for s in range(GROUP):
-        terms = parts[:, GROUP * HD :, :].astype(jnp.float32)
+    terms = parts[:, FAR * HD :, :].astype(jnp.float32)
+    for s in range(FAR):
         level = [
             terms[i, 4 * s : 4 * s + 1] + terms[i, 4 * s + 1 : 4 * s + 2] + terms[i, 4 * s + 2 : 4 * s + 3]
             for i in range(BLOCKS)
@@ -254,6 +272,8 @@
         attn[:, pl.ds(pl.multiple_of(order[s] * HD, HD), HD)] = (
             (summed * (1.0 / total)).T.astype(jnp.bfloat16)
         )
+    for s in range(FAR, GROUP):
+        attn[:, pl.ds(pl.multiple_of(order[s] * HD, HD), HD)] = near[s - FAR]
     rows = attn[...]
     mine = lax.axis_index("c")
     width = out.shape[2]
@@ -290,11 +310,11 @@
 
 def per_device(queries, keys, values, cache_keys, cache_values, spans, out_weight):
     bf16, f32 = jnp.bfloat16, jnp.float32
-    own, sent = call(
+    own, own_rows = call(
         prepare_kernel,
         [
             jax.ShapeDtypeStruct((4 * HD, HD), bf16),
-            jax.ShapeDtypeStruct((BLOCKS, GROUP, HD, HD), bf16),
+            jax.ShapeDtypeStruct((GROUP * HD, HD), bf16),
         ],
         [ANY] * 6,
         [
@@ -303,7 +323,7 @@
             pltpu.SemaphoreType.DMA((6,)),
         ],
         vmem=60,
-        moved=2**21,
+        moved=2**20,
     )(spans, queries, keys, values, cache_keys, cache_values)
     routes = [
         [
@@ -319,18 +339,26 @@
         two = lax.ppermute(two, ("k", "c"), routes[1])
         kv += [one, two]
     last = lax.ppermute(one, ("k", "c"), routes[0])
+    sent, kv[0], near_rows = call(
+        hand_kernel,
+        [
+            jax.ShapeDtypeStruct((BLOCKS, 4 * HD, HD), bf16),
+            jax.ShapeDtypeStruct((4 * HD, HD), bf16),
+            jax.ShapeDtypeStruct((2 * HD, HD), bf16),
+        ],
+        [VMEM] * 4,
+        moved=2**20,
+    )(own_rows, own, kv[1], kv[2])
     grouped = lax.all_to_all(sent, ("e", "x"), 0, 0, tiled=True)
-
     near_blocks = 2 * (RING - 1)
-    state = call(
+    sums, tops, near = call(
         first_kernel,
         [
             jax.ShapeDtypeStruct((TILES, HD + STATS, TILE), f32),
             jax.ShapeDtypeStruct((TILES, 8, TILE), f32),
-            jax.ShapeDtypeStruct((BLOCKS, HD + STATS, TILE), f32),
-            jax.ShapeDtypeStruct((BLOCKS, 8, TILE), f32),
-        ],
-        [SMEM] + [VMEM] * RING,
+            jax.ShapeDtypeStruct((2, HD, HD), bf16),
+        ],
+        [SMEM] + [VMEM] * (RING + 1),
         [
             pltpu.VMEM((near_blocks * HD, HD), bf16),
             pltpu.VMEM((HD + STATS, near_blocks * HD), bf16),
@@ -339,16 +367,16 @@
         flops=4 * 2048 * 1792 * 128,
         moved=4 * 2**20,
         exps=2048 * 1792,
-    )(spans, grouped, *kv)
+    )(spans, near_rows, grouped, *kv)
     partial = call(
         second_kernel,
         jax.ShapeDtypeStruct((BLOCKS, PIECE, HD), bf16),
-        [SMEM] + [VMEM] * 6,
+        [SMEM] + [VMEM] * 4,
         [pltpu.VMEM((BLOCKS, STATS, HD), f32)],
         flops=4 * 2048 * 256 * 128,
         moved=4 * 2**20,
         exps=2048 * 256,
-    )(spans, grouped, last, *state)
+    )(spans, grouped, last, sums, tops)
     parts = lax.all_to_all(partial, ("e", "x"), 0, 0, tiled=True)
     width = out_weight.shape[1] // 8
     product, kept = call(
@@ -357,11 +385,11 @@
             jax.ShapeDtypeStruct((4, HD, width), bf16),
             jax.ShapeDtypeStruct((4, HD, width), f32),
         ],
-        [SMEM, VMEM, VMEM],
+        [SMEM, VMEM, VMEM, VMEM],
         [pltpu.VMEM((HD, GROUP * HD), bf16)],
         flops=2 * 128 * 512 * 4096,
         moved=5 * 2**20,
-    )(spans, parts, out_weight)
+    )(spans, parts, near, out_weight)
     received = lax.ppermute(product, "c", [(0, 1), (1, 0)])
     halves = call(
         add_kernel,

time: 104 us -> 108 us (1.038)
  starting transfers between devices: 48.2 us -> 39.2 us
  waiting for transfers between devices: 10.8 us -> 18.3 us
  blocking collectives: 30.7 us -> 33.7 us
  local copies, waits for them, and re-layouts: 0.02 us -> 2.47 us
    ppermute x1, starting transfers between devices: 8.16 us -> 1.92 us  [per_device(): received = lax.ppermute(product, 'c', [(0, 1), (1, 0)])]
    ppermute x3, waiting for transfers between devices: 9.26 us -> 14.8 us  [per_device(): two = lax.ppermute(two, ('k', 'c'), routes[1])]
    ppermute x3, starting transfers between devices: 22.5 us -> 19.1 us  [per_device(): one = lax.ppermute(one, ('k', 'c'), routes[0])]
    all_to_all x1, blocking collectives: 18.1 us -> 20.6 us  [per_device(): parts = lax.all_to_all(partial, ('e', 'x'), 0, 0, tiled=True)]
    unnamed x6 -> x8, local copies, waits for them, and re-layouts: 0.02 us -> 2.47 us
    ppermute x3, waiting for transfers between devices: 0.01 us -> 1.57 us  [per_device(): one = lax.ppermute(one, ('k', 'c'), routes[0])]
    ppermute x3, starting transfers between devices: 5.74 us -> 7.25 us  [per_device(): two = lax.ppermute(two, ('k', 'c'), routes[1])]
    pallas_call x0 -> x1, Pallas kernels: none -> 1.15 us  [per_device(): call(hand_kernel, [jax.ShapeDtypeStruct((BLOCKS, 4 * HD, HD), bf16), jax....]
  transfers between devices with their start and end apart: 9 -> 9, of which waited for: 4 -> 6; matrix products, arithmetic and copies ran while one was open for 0% -> 0% of each run, Pallas kernels for 6% -> 6%
where the time goes in v8:
time: 108 us; the launch traced here: 107 us
  starting transfers between devices  39.2 us (36%)
  blocking collectives  33.7 us (31%)
  waiting for transfers between devices  18.3 us (17%)
  Pallas kernels  13.7 us (13%)
  local copies, waits for them, and re-layouts  2.47 us (2%)
    all_to_all x1, blocking collectives, per_device(): parts = lax.all_to_all(partial, ('e', 'x'), 0, 0, tiled=True)  20.6 us
    ppermute x3, starting transfers between devices, per_device(): one = lax.ppermute(one, ('k', 'c'), routes[0])  19.1 us
    ppermute x3, waiting for transfers between devices, per_device(): two = lax.ppermute(two, ('k', 'c'), routes[1])  14.8 us
    all_to_all x1, blocking collectives, per_device(): shares = lax.all_to_all(halves, 'y', 0, 0, tiled=True)  13.1 us
    ppermute x3, starting transfers between devices, per_device(): two = lax.ppermute(two, ('k', 'c'), routes[1])  7.25 us
    pallas_call x1, Pallas kernels, per_device(): call(first_kernel, [jax.ShapeDtypeStruct((TILES, HD + STATS, TILE), f32),...  5.96 us
    ppermute x1, starting transfers between devices, per_device(): last = lax.ppermute(one, ('k', 'c'), routes[0])  5.52 us
    all_to_all x1, starting transfers between devices, per_device(): grouped = lax.all_to_all(sent, ('e', 'x'), 0, 0, tiled=True)  5.46 us
  transfers between devices with their start and end apart: 9, of which 6 were waited for; matrix products, arithmetic and copies ran while one was open for 0% of the time, Pallas kernels for 6%

profile of v8, /device:TPU:1, one launch (start us, length us, event | category | flops | bytes accessed | tf_op | source)
XLA Modules:
  0.0 107.4 jit_solution(33077442794748313)
XLA Ops:
  0.0 1.7 %shard_map.73 = (bf16[512,128]{1,0:T(8,128)(2,1)}, bf16[512,128]{1,0:T(8,128)(2,1)}) custom-call(s32[4]{0:T(128)} %spans.7, bf16[128,512]{1,0:T(8,128)(2,1)} %queries.1, bf16[128,128]{1,0:T(8,128)(2,1)} %keys.1, bf16[128,128]{1,0:T(8,128)(2,1)} %values.1, bf16[128,128]{1,0:T(8,128)(2,1)} %cache_keys.1, bf16[128,128]{1,0:T(8,128)(2,1)} %cache_values.1), custom_call_target="tpu_custom_call" | custom-call | bytes 1048576 | tf_op jit(solution)/shard_map/pallas_call | solution.py:313
  1.7 12.4 %collective-permute-start = (bf16[512,128]{1,0:T(8,128)(2,1)}, bf16[512,128]{1,0:T(8,128)(2,1)S(1)}, u32[]{:S(2)}, u32[]{:S(2)}) collective-permute-start(bf16[512,128]{1,0:T(8,128)(2,1)} %get-tuple-element.16.own), channel_id=1, source_target_pairs={{0,64},{1,449},{64,128},{65,1},{128,192},{129,65},{192,256},{193,1... | collective-permute-start | bytes 393224 | tf_op jit(solution)/shard_map/ppermute | solution.py:338
  14.1 1.9 %collective-permute-start.1 = (bf16[512,128]{1,0:T(8,128)(2,1)}, bf16[512,128]{1,0:T(8,128)(2,1)S(1)}, u32[]{:S(2)}, u32[]{:S(2)}) collective-permute-start(bf16[512,128]{1,0:T(8,128)(2,1)} %get-tuple-element.16.own), channel_id=1, source_target_pairs={{0,448},{1,65},{64,0},{65,129},{128,64},{129,193},{192,128},{193,2... | collective-permute-start | bytes 393224 | tf_op jit(solution)/shard_map/ppermute | solution.py:339
  16.0 0.8 collective-permute-done.one.refs_1_
  16.8 5.7 %collective-permute-done.1.two.refs_2_ = bf16[512,128]{1,0:T(8,128)(2,1)S(1)} collective-permute-done((bf16[512,128]{1,0:T(8,128)(2,1)}, bf16[512,128]{1,0:T(8,128)(2,1)S(1)}, u32[]{:S(2)}, u32[]{:S(2)}) %collective-permute-start.1) | collective-permute-done | bytes 131104 | tf_op jit(solution)/shard_map/ppermute | solution.py:339
  22.5 0.0 copy-start.1
  22.5 0.9 copy-done.1
  23.4 0.0 copy-start.2
  23.4 0.9 copy-done.2
  24.3 1.2 %shard_map.74 = (bf16[8,512,128]{2,1,0:T(8,128)(2,1)}, bf16[512,128]{1,0:T(8,128)(2,1)S(1)}, bf16[256,128]{1,0:T(8,128)(2,1)S(1)}) custom-call(bf16[512,128]{1,0:T(8,128)(2,1)S(1)} %copy-done.2, bf16[512,128]{1,0:T(8,128)(2,1)S(1)} %copy-done.1, bf16[512,128]{1,0:T(8,128)(2,1)S(1)} %collective-permute-done.one.refs_1_, ...), custom_call_target="tpu_custom_call" | custom-call | bytes 1048576 | tf_op jit(solution)/shard_map/pallas_call | solution.py:342
  25.5 5.5 %all-to-all-start = ((bf16[8,512,128]{2,1,0:T(8,128)(2,1)}), bf16[8,512,128]{2,1,0:T(8,128)(2,1)S(1)}, u32[]{:S(2)}, u32[]{:S(2)}) async-start(bf16[8,512,128]{2,1,0:T(8,128)(2,1)} %get-tuple-element.17), calls=%async_computation | async-start | bytes 2097152 | tf_op jit(solution)/shard_map/all_to_all | solution.py:352
  30.9 2.7 %collective-permute-start.2 = (bf16[512,128]{1,0:T(8,128)(2,1)S(1)}, bf16[512,128]{1,0:T(8,128)(2,1)S(1)}, u32[]{:S(2)}, u32[]{:S(2)}) collective-permute-start(bf16[512,128]{1,0:T(8,128)(2,1)S(1)} %collective-permute-done.one.refs_1_), channel_id=1, source_target_pairs={{0,64},{1,449},{64,128},{65,1},{128,192},{129,65},{192,256},{193,1... | collective-permute-start | bytes 393224 | tf_op jit(solution)/shard_map/ppermute | solution.py:338
  33.7 3.4 %collective-permute-start.5 = (bf16[512,128]{1,0:T(8,128)(2,1)S(1)}, bf16[512,128]{1,0:T(8,128)(2,1)S(1)}, u32[]{:S(2)}, u32[]{:S(2)}) collective-permute-start(bf16[512,128]{1,0:T(8,128)(2,1)S(1)} %collective-permute-done.1.two.refs_2_), channel_id=1, source_target_pairs={{0,448},{1,65},{64,0},{65,129},{128,64},{129,193},{192,128},{193,2... | collective-permute-start | bytes 393224 | tf_op jit(solution)/shard_map/ppermute | solution.py:339
  37.1 0.8 collective-permute-done.2.refs_3_
  37.9 3.9 %collective-permute-start.3 = (bf16[512,128]{1,0:T(8,128)(2,1)S(1)}, bf16[512,128]{1,0:T(8,128)(2,1)S(1)}, u32[]{:S(2)}, u32[]{:S(2)}) collective-permute-start(bf16[512,128]{1,0:T(8,128)(2,1)S(1)} %collective-permute-done.2.refs_3_), channel_id=1, source_target_pairs={{0,64},{1,449},{64,128},{65,1},{128,192},{129,65},{192,256},{193,1... | collective-permute-start | bytes 393224 | tf_op jit(solution)/shard_map/ppermute | solution.py:338
  41.8 8.7 %collective-permute-done.5.refs_4_ = bf16[512,128]{1,0:T(8,128)(2,1)S(1)} collective-permute-done((bf16[512,128]{1,0:T(8,128)(2,1)S(1)}, bf16[512,128]{1,0:T(8,128)(2,1)S(1)}, u32[]{:S(2)}, u32[]{:S(2)}) %collective-permute-start.5) | collective-permute-done | bytes 131104 | tf_op jit(solution)/shard_map/ppermute | solution.py:339
  50.5 1.9 %collective-permute-start.6 = (bf16[512,128]{1,0:T(8,128)(2,1)S(1)}, bf16[512,128]{1,0:T(8,128)(2,1)S(1)}, u32[]{:S(2)}, u32[]{:S(2)}) collective-permute-start(bf16[512,128]{1,0:T(8,128)(2,1)S(1)} %collective-permute-done.5.refs_4_), channel_id=1, source_target_pairs={{0,448},{1,65},{64,0},{65,129},{128,64},{129,193},{192,128},{193,2... | collective-permute-start | bytes 393224 | tf_op jit(solution)/shard_map/ppermute | solution.py:339
  52.5 0.0 collective-permute-done.3.refs_5_
  52.5 5.5 %collective-permute-start.4 = (bf16[512,128]{1,0:T(8,128)(2,1)S(1)}, bf16[512,128]{1,0:T(8,128)(2,1)S(1)}, u32[]{:S(2)}, u32[]{:S(2)}) collective-permute-start(bf16[512,128]{1,0:T(8,128)(2,1)S(1)} %collective-permute-done.3.refs_5_), channel_id=1, source_target_pairs={{0,64},{1,449},{64,128},{65,1},{128,192},{129,65},{192,256},{193,1... | collective-permute-start | bytes 393224 | tf_op jit(solution)/shard_map/ppermute | solution.py:341
  58.0 0.4 collective-permute-done.6.refs_6_
  58.4 0.0 all-to-all-done.queries
  58.4 0.0 copy-start.3
  58.4 0.7 copy-done.3
  59.1 0.0 copy-start
  59.1 6.0 %shard_map.75 = (f32[8,144,256]{2,1,0:T(8,128)S(1)}, f32[8,8,256]{2,1,0:T(8,128)S(1)}, bf16[2,128,128]{2,1,0:T(8,128)(2,1)S(1)}) custom-call(s32[4]{0:T(128)S(1)} %copy-done.3, bf16[256,128]{1,0:T(8,128)(2,1)S(1)} %get-tuple-element.18.near_rows, bf16[8,512,128]{2,1,0:T(8,128)(2,1)S(1)} %all-to-all-done.queries, ...), custom_call_target="tpu_custom_call" | custom-call | flops 1879048192 | bytes 4194304 | tf_op jit(solution)/shard_map/pallas_call | solution.py:354
  65.0 0.0 collective-permute-done.4.last
  65.0 2.5 %shard_map.76 = bf16[8,272,128]{2,1,0:T(8,128)(2,1)S(1)} custom-call(s32[4]{0:T(128)S(1)} %copy-done.3, bf16[8,512,128]{2,1,0:T(8,128)(2,1)S(1)} %all-to-all-done.queries, bf16[512,128]{1,0:T(8,128)(2,1)S(1)} %collective-permute-done.4.last, f32[8,144,256]{2,1,0:T(8,128)S(1)} %get-tuple-element.20.sums, f32[8,8,256]{2,1,0:T(8,128)S(1)} %get-tuple-element.21.tops), custom_call_target="tpu_custom_call" | custom-call | flops 268435456 | bytes 4194304 | tf_op jit(solution)/shard_map/pallas_call | solution.py:371
  67.6 20.6 %all_to_all.15.parts = bf16[8,272,128]{2,1,0:T(8,128)(2,1)S(1)} all-to-all(bf16[8,272,128]{2,1,0:T(8,128)(2,1)S(1)} %shard_map.76), channel_id=1, replica_groups=mesh['k'=8,'e'=2,'x'=4,'y'=4,'c'=2] {'e','x'}, dimensions={0} | all-to-all | bytes 1114112 | tf_op jit(solution)/shard_map/all_to_all | solution.py:380
  88.1 0.0 copy-done
  88.1 1.5 %shard_map.77 = (bf16[4,128,512]{2,1,0:T(8,128)(2,1)S(1)}, f32[4,128,512]{2,1,0:T(8,128)S(1)}) custom-call(s32[4]{0:T(128)S(1)} %copy-done.3, bf16[8,272,128]{2,1,0:T(8,128)(2,1)S(1)} %all_to_all.15.parts, bf16[2,128,128]{2,1,0:T(8,128)(2,1)S(1)} %get-tuple-element.22.near, bf16[512,4096]{1,0:T(8,128)(2,1)S(1)} %copy-done), custom_call_target="tpu_custom_call" | custom-call | flops 536870912 | bytes 5242880 | tf_op jit(solution)/shard_map/pallas_call | solution.py:382
  89.6 1.9 %collective-permute-start.7 = (bf16[4,128,512]{2,1,0:T(8,128)(2,1)S(1)}, bf16[4,128,512]{2,1,0:T(8,128)(2,1)S(1)}, u32[]{:S(2)}, u32[]{:S(2)}) collective-permute-start(bf16[4,128,512]{2,1,0:T(8,128)(2,1)S(1)} %get-tuple-element.24), channel_id=1, source_target_pairs={{0,1},{1,0},{2,3},{3,2},{4,5},{5,4},{6,7},{7,6},{8,9},{9,8},{10,11... | collective-permute-start | bytes 1572872 | tf_op jit(solution)/shard_map/ppermute | solution.py:393
  91.5 1.9 %collective-permute-done.7.received = bf16[4,128,512]{2,1,0:T(8,128)(2,1)S(1)} collective-permute-done((bf16[4,128,512]{2,1,0:T(8,128)(2,1)S(1)}, bf16[4,128,512]{2,1,0:T(8,128)(2,1)S(1)}, u32[]{:S(2)}, u32[]{:S(2)}) %collective-permute-start.7) | collective-permute-done | bytes 524320 | tf_op jit(solution)/shard_map/ppermute | solution.py:393
  93.4 0.1 shard_map.78
  93.5 13.1 %all_to_all.16.shares = bf16[4,128,512]{2,1,0:T(8,128)(2,1)S(1)} all-to-all(bf16[4,128,512]{2,1,0:T(8,128)(2,1)S(1)} %shard_map.78), channel_id=1, replica_groups=mesh['k'=8,'e'=2,'x'=4,'y'=4,'c'=2] {'y'}, dimensions={0} | all-to-all | bytes 1048576 | tf_op jit(solution)/shard_map/all_to_all | solution.py:400
  106.7 0.8 shard_map.79
Async XLA Ops:
  1.7 15.1 %collective-permute-start = (bf16[512,128]{1,0:T(8,128)(2,1)}, bf16[512,128]{1,0:T(8,128)(2,1)S(1)}, u32[]{:S(2)}, u32[]{:S(2)}) collective-permute-start(bf16[512,128]{1,0:T(8,128)(2,1)} %get-tuple-element.16.own), channel_id=1, source_target_pairs={{0,64},{1,449},{64,128},{65,1},{128,192},{129,65},{192,256},{193,1... | collective-permute-start | bytes 393224 | tf_op jit(solution)/shard_map/ppermute | solution.py:338
  14.1 8.4 %collective-permute-start.1 = (bf16[512,128]{1,0:T(8,128)(2,1)}, bf16[512,128]{1,0:T(8,128)(2,1)S(1)}, u32[]{:S(2)}, u32[]{:S(2)}) collective-permute-start(bf16[512,128]{1,0:T(8,128)(2,1)} %get-tuple-element.16.own), channel_id=1, source_target_pairs={{0,448},{1,65},{64,0},{65,129},{128,64},{129,193},{192,128},{193,2... | collective-permute-start | bytes 393224 | tf_op jit(solution)/shard_map/ppermute | solution.py:339
  22.5 0.9 copy-start.1
  23.4 0.9 copy-start.2
  25.5 32.9 %all-to-all-start = ((bf16[8,512,128]{2,1,0:T(8,128)(2,1)}), bf16[8,512,128]{2,1,0:T(8,128)(2,1)S(1)}, u32[]{:S(2)}, u32[]{:S(2)}) async-start(bf16[8,512,128]{2,1,0:T(8,128)(2,1)} %get-tuple-element.17), calls=%async_computation | async-start | bytes 2097152 | tf_op jit(solution)/shard_map/all_to_all | solution.py:352
  30.9 6.9 %collective-permute-start.2 = (bf16[512,128]{1,0:T(8,128)(2,1)S(1)}, bf16[512,128]{1,0:T(8,128)(2,1)S(1)}, u32[]{:S(2)}, u32[]{:S(2)}) collective-permute-start(bf16[512,128]{1,0:T(8,128)(2,1)S(1)} %collective-permute-done.one.refs_1_), channel_id=1, source_target_pairs={{0,64},{1,449},{64,128},{65,1},{128,192},{129,65},{192,256},{193,1... | collective-permute-start | bytes 393224 | tf_op jit(solution)/shard_map/ppermute | solution.py:338
  33.7 16.8 %collective-permute-start.5 = (bf16[512,128]{1,0:T(8,128)(2,1)S(1)}, bf16[512,128]{1,0:T(8,128)(2,1)S(1)}, u32[]{:S(2)}, u32[]{:S(2)}) collective-permute-start(bf16[512,128]{1,0:T(8,128)(2,1)S(1)} %collective-permute-done.1.two.refs_2_), channel_id=1, source_target_pairs={{0,448},{1,65},{64,0},{65,129},{128,64},{129,193},{192,128},{193,2... | collective-permute-start | bytes 393224 | tf_op jit(solution)/shard_map/ppermute | solution.py:339
  37.9 14.6 %collective-permute-start.3 = (bf16[512,128]{1,0:T(8,128)(2,1)S(1)}, bf16[512,128]{1,0:T(8,128)(2,1)S(1)}, u32[]{:S(2)}, u32[]{:S(2)}) collective-permute-start(bf16[512,128]{1,0:T(8,128)(2,1)S(1)} %collective-permute-done.2.refs_3_), channel_id=1, source_target_pairs={{0,64},{1,449},{64,128},{65,1},{128,192},{129,65},{192,256},{193,1... | collective-permute-start | bytes 393224 | tf_op jit(solution)/shard_map/ppermute | solution.py:338
  50.5 7.9 %collective-permute-start.6 = (bf16[512,128]{1,0:T(8,128)(2,1)S(1)}, bf16[512,128]{1,0:T(8,128)(2,1)S(1)}, u32[]{:S(2)}, u32[]{:S(2)}) collective-permute-start(bf16[512,128]{1,0:T(8,128)(2,1)S(1)} %collective-permute-done.5.refs_4_), channel_id=1, source_target_pairs={{0,448},{1,65},{64,0},{65,129},{128,64},{129,193},{192,128},{193,2... | collective-permute-start | bytes 393224 | tf_op jit(solution)/shard_map/ppermute | solution.py:339
  52.5 12.6 %collective-permute-start.4 = (bf16[512,128]{1,0:T(8,128)(2,1)S(1)}, bf16[512,128]{1,0:T(8,128)(2,1)S(1)}, u32[]{:S(2)}, u32[]{:S(2)}) collective-permute-start(bf16[512,128]{1,0:T(8,128)(2,1)S(1)} %collective-permute-done.3.refs_5_), channel_id=1, source_target_pairs={{0,64},{1,449},{64,128},{65,1},{128,192},{129,65},{192,256},{193,1... | collective-permute-start | bytes 393224 | tf_op jit(solution)/shard_map/ppermute | solution.py:341
  58.4 0.7 copy-start.3
  59.1 29.1 %copy-start = (bf16[512,4096]{1,0:T(8,128)(2,1)S(1)}, bf16[512,4096]{1,0:T(8,128)(2,1)}, u32[]{:S(2)}) copy-start(bf16[512,4096]{1,0:T(8,128)(2,1)} %weight.1) | copy-start | bytes 12582916
  89.6 3.8 %collective-permute-start.7 = (bf16[4,128,512]{2,1,0:T(8,128)(2,1)S(1)}, bf16[4,128,512]{2,1,0:T(8,128)(2,1)S(1)}, u32[]{:S(2)}, u32[]{:S(2)}) collective-permute-start(bf16[4,128,512]{2,1,0:T(8,128)(2,1)S(1)} %get-tuple-element.24), channel_id=1, source_target_pairs={{0,1},{1,0},{2,3},{3,2},{4,5},{5,4},{6,7},{7,6},{8,9},{9,8},{10,11... | collective-permute-start | bytes 1572872 | tf_op jit(solution)/shard_map/ppermute | solution.py:393

commit v9 on v8

--- a/solution.py
+++ b/solution.py
@@ -44,7 +44,7 @@
 
 
 def prepare_kernel(
-    spans, queries, keys, values, cache_keys, cache_values, own, own_rows, heads, kinds, sems
+    spans, queries, keys, values, cache_keys, cache_values, own, own_rows, handed, heads, kinds, sems
 ):
     copies = [
         pltpu.make_async_copy(spans, kinds, sems.at[0]),
@@ -58,29 +58,33 @@
         copy.start()
     for copy in copies:
         copy.wait()
+    k, e, _ = position()
+    ends = (k == RING - 1) & (e == 1)
+    handed[...] = jnp.where(ends, own[: 2 * HD, :], own[2 * HD :, :])
     order = head_order(kinds)
     for s in range(GROUP):
         rows = heads[:, pl.ds(pl.multiple_of(order[s] * HD, HD), HD)]
         own_rows[s * HD : (s + 1) * HD, :] = rows
 
 
-def hand_kernel(own_rows, own, one, two, sent, held, near_rows):
-    k, e, x = position()
-    me = e * 4 + x
-    below = jnp.where(lax.axis_index("c") == 0, one[...], two[...])
-    prior = jnp.where(k == 0, below[: 2 * HD, :], below[2 * HD :, :])
-    block = own[2 * HD :, :]
-    rows = own_rows[: FAR * HD, :]
+def spread_kernel(own_rows, other_rows, own, prior, after, sent, held, near_rows):
+    del after
+    first = lax.axis_index("e") == 0
+    mine, other = own_rows[: FAR * HD, :], other_rows[: FAR * HD, :]
+    lower = jnp.where(first, mine, other)
+    upper = jnp.where(first, other, mine)
+    for j in range(4):
+        sent[j, : 2 * HD, :] = lower
+        sent[j, 2 * HD : 4 * HD, :] = upper
+        sent[j, 4 * HD : 6 * HD, :] = own[2 * HD :, :]
+        sent[j, 6 * HD :, :] = prior[...]
+    held[...] = own[...]
     near_rows[...] = own_rows[FAR * HD :, :]
-    held[...] = own[...]
-    for j in range(BLOCKS):
-        sent[j, : FAR * HD, :] = rows
-        sent[j, FAR * HD :, :] = jnp.where(j >= me, block, prior)
-
-
-def query_rows(grouped, slot, first):
-    at = slot * HD
-    return grouped[first : first + TILE // HD, at : at + HD, :].reshape(TILE, HD)
+
+
+def query_rows(gathered, slot, first):
+    at = first // 4 * 2 * HD + slot * HD
+    return gathered[first % 4 : first % 4 + TILE // HD, at : at + HD, :].reshape(TILE, HD)
 
 
 def position():
@@ -122,9 +126,8 @@
     return jnp.max(found.reshape(HD // 8, 8, found.shape[1]), axis=0)
 
 
-def near_heads(spans, order, rows, grouped, out):
-    _, e, x = position()
-    me = e * 4 + x
+def near_heads(spans, order, rows, own, gathered, out):
+    x = lax.axis_index("x")
     column, _ = offsets()
     behind = column - lax.broadcasted_iota(jnp.int32, (HD, TILE), 0)
     span = jnp.where(
@@ -132,12 +135,18 @@
     )
     found, values = [], []
     for j in range(5):
-        block = grouped[lax.rem(me - j + BLOCKS, BLOCKS), FAR * HD :, :]
-        far = behind + j * HD
+        if j < 4:
+            distance = jnp.where(j < x, x - j, x - j + 4) * HD
+            block = jnp.where(j < x, gathered[j, 4 * HD : 6 * HD, :], gathered[j, 6 * HD :, :])
+            key_rows, value_rows = block[:HD, :], block[HD:, :]
+        else:
+            distance = 0
+            key_rows, value_rows = own[2 * HD : 3 * HD, :], own[3 * HD :, :]
+        far = behind + distance
         found.append(
-            jnp.where((far >= 0) & (far < span), dot(block[:HD, :], rows[...], NT), MASKED)
+            jnp.where((far >= 0) & (far < span), dot(key_rows, rows[...], NT), MASKED)
         )
-        values.append(block[HD:, :])
+        values.append(value_rows)
     top = highest(found[0])
     for j in range(1, 5):
         top = jnp.maximum(top, highest(found[j]))
@@ -196,7 +205,7 @@
         sums[t] = dot(flipped[...], weights, NN)
         tops[t] = jnp.broadcast_to(top, (8, TILE))
 
-    near_heads(spans, order, near_rows, queries, near)
+    near_heads(spans, order, near_rows, kv[0], queries, near)
     top = score(0)
     for t in range(TILES):
         later = score(t + 1) if t + 1 < TILES else None
@@ -310,11 +319,12 @@
 
 def per_device(queries, keys, values, cache_keys, cache_values, spans, out_weight):
     bf16, f32 = jnp.bfloat16, jnp.float32
-    own, own_rows = call(
+    own, own_rows, handed = call(
         prepare_kernel,
         [
             jax.ShapeDtypeStruct((4 * HD, HD), bf16),
             jax.ShapeDtypeStruct((GROUP * HD, HD), bf16),
+            jax.ShapeDtypeStruct((2 * HD, HD), bf16),
         ],
         [ANY] * 6,
         [
@@ -325,6 +335,10 @@
         vmem=60,
         moved=2**20,
     )(spans, queries, keys, values, cache_keys, cache_values)
+    other_rows = lax.ppermute(own_rows, "e", [(0, 1), (1, 0)])
+    prior = lax.ppermute(
+        handed, ("k", "e"), [(i, (i + 1) % (2 * RING)) for i in range(2 * RING)]
+    )
     routes = [
         [
             (2 * i + c, (i + (1 if c == turn else -1)) % RING * 2 + c)
@@ -333,23 +347,24 @@
         ]
         for turn in range(2)
     ]
-    kv, one, two = [own], own, own
+    kv, one = [own], own
+    two, other_rows, prior = lax.optimization_barrier((own, other_rows, prior))
     for _ in range(RING // 2 - 1):
         one = lax.ppermute(one, ("k", "c"), routes[0])
         two = lax.ppermute(two, ("k", "c"), routes[1])
         kv += [one, two]
     last = lax.ppermute(one, ("k", "c"), routes[0])
     sent, kv[0], near_rows = call(
-        hand_kernel,
-        [
-            jax.ShapeDtypeStruct((BLOCKS, 4 * HD, HD), bf16),
+        spread_kernel,
+        [
+            jax.ShapeDtypeStruct((4, 8 * HD, HD), bf16),
             jax.ShapeDtypeStruct((4 * HD, HD), bf16),
             jax.ShapeDtypeStruct((2 * HD, HD), bf16),
         ],
-        [VMEM] * 4,
+        [VMEM] * 4 + [ANY],
         moved=2**20,
-    )(own_rows, own, kv[1], kv[2])
-    grouped = lax.all_to_all(sent, ("e", "x"), 0, 0, tiled=True)
+    )(own_rows, other_rows, own, prior, kv[1])
+    grouped = lax.all_to_all(sent, "x", 0, 0, tiled=True)
     near_blocks = 2 * (RING - 1)
     sums, tops, near = call(
         first_kernel,

time: 108 us -> 107 us (level)
  starting transfers between devices: 39.2 us -> 52.5 us
  blocking collectives: 33.7 us -> 25.6 us
  waiting for transfers between devices: 18.3 us -> 11.8 us
    ppermute x3, waiting for transfers between devices: 14.8 us -> 2.97 us  [per_device(): two = lax.ppermute(two, ('k', 'c'), routes[1])]
    all_to_all x1, blocking collectives: 20.6 us -> 13 us  [per_device(): parts = lax.all_to_all(partial, ('e', 'x'), 0, 0, tiled=True)]
    ppermute x0 -> x2, starting transfers between devices: none -> 7.01 us  [the longest x1 4.37 us: per_device(): other_rows = lax.ppermute(own_rows, 'e', [(0, 1), (1, 0)])]
    ppermute x1, starting transfers between devices: 1.92 us -> 8.92 us  [per_device(): received = lax.ppermute(product, 'c', [(0, 1), (1, 0)])]
    ppermute x0 -> x2, waiting for transfers between devices: none -> 3.79 us  [the longest x1 3.79 us: per_device(): lax.ppermute(handed, ('k', 'e'), [(i, (i + 1) % (2 * RING)) for i in rang...]
    ppermute x3, starting transfers between devices: 19.1 us -> 22.5 us  [per_device(): one = lax.ppermute(one, ('k', 'c'), routes[0])]
    ppermute x3, waiting for transfers between devices: 1.57 us -> 3.51 us  [per_device(): one = lax.ppermute(one, ('k', 'c'), routes[0])]
    ppermute x3, starting transfers between devices: 7.25 us -> 5.74 us  [per_device(): two = lax.ppermute(two, ('k', 'c'), routes[1])]
  transfers between devices with their start and end apart: 9 -> 11, of which waited for: 6 -> 6; matrix products, arithmetic and copies ran while one was open for 0% -> 0% of each run, Pallas kernels for 6% -> 6%
where the time goes in v9:
time: 107 us; the launch traced here: 106 us
  starting transfers between devices  52.5 us (49%)
  blocking collectives  25.6 us (24%)
  Pallas kernels  13.6 us (13%)
  waiting for transfers between devices  11.8 us (11%)
  local copies, waits for them, and re-layouts  2.47 us (2%)
    ppermute x3, starting transfers between devices, per_device(): one = lax.ppermute(one, ('k', 'c'), routes[0])  22.5 us
    all_to_all x1, blocking collectives, per_device(): parts = lax.all_to_all(partial, ('e', 'x'), 0, 0, tiled=True)  13 us
    all_to_all x1, blocking collectives, per_device(): shares = lax.all_to_all(halves, 'y', 0, 0, tiled=True)  12.6 us
    ppermute x1, starting transfers between devices, per_device(): received = lax.ppermute(product, 'c', [(0, 1), (1, 0)])  8.92 us
    pallas_call x1, Pallas kernels, per_device(): call(first_kernel, [jax.ShapeDtypeStruct((TILES, HD + STATS, TILE), f32),...  5.95 us
    ppermute x3, starting transfers between devices, per_device(): two = lax.ppermute(two, ('k', 'c'), routes[1])  5.74 us
    ppermute x1, starting transfers between devices, per_device(): other_rows = lax.ppermute(own_rows, 'e', [(0, 1), (1, 0)])  4.37 us
    all_to_all x1, starting transfers between devices, per_device(): grouped = lax.all_to_all(sent, 'x', 0, 0, tiled=True)  4.14 us
  transfers between devices with their start and end apart: 11, of which 6 were waited for; matrix products, arithmetic and copies ran while one was open for 0% of the time, Pallas kernels for 6%

profile of v9, /device:TPU:1, one launch (start us, length us, event | category | flops | bytes accessed | tf_op | source)
XLA Modules:
  0.0 106.1 jit_solution(17306072724125838352)
XLA Ops:
  0.0 1.7 %shard_map.73 = (bf16[512,128]{1,0:T(8,128)(2,1)}, bf16[512,128]{1,0:T(8,128)(2,1)}, bf16[256,128]{1,0:T(8,128)(2,1)}) custom-call(s32[4]{0:T(128)} %spans.7, bf16[128,512]{1,0:T(8,128)(2,1)} %queries.1, bf16[128,128]{1,0:T(8,128)(2,1)} %keys.1, bf16[128,128]{1,0:T(8,128)(2,1)} %values.1, bf16[128,128]{1,0:T(8,128)(2,1)} %cache_keys.1, ...), custom_call_target="tpu_custom_call" | custom-call | bytes 1048576 | tf_op jit(solution)/shard_map/pallas_call | solution.py:322
  1.7 4.4 %collective-permute-start = (bf16[512,128]{1,0:T(8,128)(2,1)}, bf16[512,128]{1,0:T(8,128)(2,1)S(1)}, u32[]{:S(2)}, u32[]{:S(2)}) collective-permute-start(bf16[512,128]{1,0:T(8,128)(2,1)} %get-tuple-element.19.own_rows), channel_id=1, source_target_pairs={{0,32},{32,0},{1,33},{33,1},{2,34},{34,2},{3,35},{35,3},{4,36},{36... | collective-permute-start | bytes 393224 | tf_op jit(solution)/shard_map/ppermute | solution.py:338
  6.1 10.7 %collective-permute-start.2 = (bf16[512,128]{1,0:T(8,128)(2,1)}, bf16[512,128]{1,0:T(8,128)(2,1)S(1)}, u32[]{:S(2)}, u32[]{:S(2)}) collective-permute-start(bf16[512,128]{1,0:T(8,128)(2,1)} %get-tuple-element.27.own), channel_id=1, source_target_pairs={{0,64},{1,449},{64,128},{65,1},{128,192},{129,65},{192,256},{193,1... | collective-permute-start | bytes 393224 | tf_op jit(solution)/shard_map/ppermute | solution.py:353
  16.8 2.6 %collective-permute-start.1 = (bf16[256,128]{1,0:T(8,128)(2,1)}, bf16[256,128]{1,0:T(8,128)(2,1)S(1)}, u32[]{:S(2)}, u32[]{:S(2)}) collective-permute-start(bf16[256,128]{1,0:T(8,128)(2,1)} %get-tuple-element.21), channel_id=1, source_target_pairs={{0,32},{32,64},{64,96},{96,128},{128,160},{160,192},{192,224},{224... | collective-permute-start | bytes 196616 | tf_op jit(solution)/shard_map/ppermute | solution.py:339
  19.4 3.8 %collective-permute-done.1.prior = bf16[256,128]{1,0:T(8,128)(2,1)S(1)} collective-permute-done((bf16[256,128]{1,0:T(8,128)(2,1)}, bf16[256,128]{1,0:T(8,128)(2,1)S(1)}, u32[]{:S(2)}, u32[]{:S(2)}) %collective-permute-start.1) | collective-permute-done | bytes 65568 | tf_op jit(solution)/shard_map/ppermute | solution.py:339
  23.2 0.0 collective-permute-done.other_rows
  23.2 0.0 collective-permute-done.2.after.refs_1_
  23.2 0.0 copy-start.1
  23.2 0.9 copy-done.1
  24.1 0.0 copy-start.2
  24.1 0.9 copy-done.2
  25.0 1.2 %shard_map.74 = (bf16[4,1024,128]{2,1,0:T(8,128)(2,1)}, bf16[512,128]{1,0:T(8,128)(2,1)S(1)}, bf16[256,128]{1,0:T(8,128)(2,1)S(1)}) custom-call(bf16[512,128]{1,0:T(8,128)(2,1)S(1)} %copy-done.2, bf16[512,128]{1,0:T(8,128)(2,1)S(1)} %collective-permute-done.other_rows, bf16[512,128]{1,0:T(8,128)(2,1)S(1)} %copy-done.1, ...), custom_call_target="tpu_custom_call" | custom-call | bytes 1048576 | tf_op jit(solution)/shard_map/pallas_call | solution.py:357
  26.2 0.0 copy-start.4
  26.2 4.1 %all-to-all-start = ((bf16[4,1024,128]{2,1,0:T(8,128)(2,1)}), bf16[4,1024,128]{2,1,0:T(8,128)(2,1)S(1)}, u32[]{:S(2)}, u32[]{:S(2)}) async-start(bf16[4,1024,128]{2,1,0:T(8,128)(2,1)} %get-tuple-element.24), calls=%async_computation | async-start | bytes 2097152 | tf_op jit(solution)/shard_map/all_to_all | solution.py:367
  30.3 1.9 %collective-permute-start.6 = (bf16[512,128]{1,0:T(8,128)(2,1)}, bf16[512,128]{1,0:T(8,128)(2,1)S(1)}, u32[]{:S(2)}, u32[]{:S(2)}) collective-permute-start(bf16[512,128]{1,0:T(8,128)(2,1)} %get-tuple-element.27.own), channel_id=1, source_target_pairs={{0,448},{1,65},{64,0},{65,129},{128,64},{129,193},{192,128},{193,2... | collective-permute-start | bytes 393224 | tf_op jit(solution)/shard_map/ppermute | solution.py:354
  32.2 5.5 %collective-permute-start.3 = (bf16[512,128]{1,0:T(8,128)(2,1)S(1)}, bf16[512,128]{1,0:T(8,128)(2,1)S(1)}, u32[]{:S(2)}, u32[]{:S(2)}) collective-permute-start(bf16[512,128]{1,0:T(8,128)(2,1)S(1)} %collective-permute-done.2.after.refs_1_), channel_id=1, source_target_pairs={{0,64},{1,449},{64,128},{65,1},{128,192},{129,65},{192,256},{193,1... | collective-permute-start | bytes 393224 | tf_op jit(solution)/shard_map/ppermute | solution.py:353
  37.7 1.6 %collective-permute-done.6.refs_2_ = bf16[512,128]{1,0:T(8,128)(2,1)S(1)} collective-permute-done((bf16[512,128]{1,0:T(8,128)(2,1)}, bf16[512,128]{1,0:T(8,128)(2,1)S(1)}, u32[]{:S(2)}, u32[]{:S(2)}) %collective-permute-start.6) | collective-permute-done | bytes 131104 | tf_op jit(solution)/shard_map/ppermute | solution.py:354
  39.3 1.9 %collective-permute-start.7 = (bf16[512,128]{1,0:T(8,128)(2,1)S(1)}, bf16[512,128]{1,0:T(8,128)(2,1)S(1)}, u32[]{:S(2)}, u32[]{:S(2)}) collective-permute-start(bf16[512,128]{1,0:T(8,128)(2,1)S(1)} %collective-permute-done.6.refs_2_), channel_id=1, source_target_pairs={{0,448},{1,65},{64,0},{65,129},{128,64},{129,193},{192,128},{193,2... | collective-permute-start | bytes 393224 | tf_op jit(solution)/shard_map/ppermute | solution.py:354
  41.2 0.8 collective-permute-done.3.refs_3_
  42.0 6.4 %collective-permute-start.4 = (bf16[512,128]{1,0:T(8,128)(2,1)S(1)}, bf16[512,128]{1,0:T(8,128)(2,1)S(1)}, u32[]{:S(2)}, u32[]{:S(2)}) collective-permute-start(bf16[512,128]{1,0:T(8,128)(2,1)S(1)} %collective-permute-done.3.refs_3_), channel_id=1, source_target_pairs={{0,64},{1,449},{64,128},{65,1},{128,192},{129,65},{192,256},{193,1... | collective-permute-start | bytes 393224 | tf_op jit(solution)/shard_map/ppermute | solution.py:353
  48.4 0.0 collective-permute-done.7.refs_4_
  48.4 1.9 %collective-permute-start.8 = (bf16[512,128]{1,0:T(8,128)(2,1)S(1)}, bf16[512,128]{1,0:T(8,128)(2,1)S(1)}, u32[]{:S(2)}, u32[]{:S(2)}) collective-permute-start(bf16[512,128]{1,0:T(8,128)(2,1)S(1)} %collective-permute-done.7.refs_4_), channel_id=1, source_target_pairs={{0,448},{1,65},{64,0},{65,129},{128,64},{129,193},{192,128},{193,2... | collective-permute-start | bytes 393224 | tf_op jit(solution)/shard_map/ppermute | solution.py:354
  50.4 2.7 %collective-permute-done.4.refs_5_ = bf16[512,128]{1,0:T(8,128)(2,1)S(1)} collective-permute-done((bf16[512,128]{1,0:T(8,128)(2,1)S(1)}, bf16[512,128]{1,0:T(8,128)(2,1)S(1)}, u32[]{:S(2)}, u32[]{:S(2)}) %collective-permute-start.4) | collective-permute-done | bytes 131104 | tf_op jit(solution)/shard_map/ppermute | solution.py:353
  53.1 4.1 %collective-permute-start.5 = (bf16[512,128]{1,0:T(8,128)(2,1)S(1)}, bf16[512,128]{1,0:T(8,128)(2,1)S(1)}, u32[]{:S(2)}, u32[]{:S(2)}) collective-permute-start(bf16[512,128]{1,0:T(8,128)(2,1)S(1)} %collective-permute-done.4.refs_5_), channel_id=1, source_target_pairs={{0,64},{1,449},{64,128},{65,1},{128,192},{129,65},{192,256},{193,1... | collective-permute-start | bytes 393224 | tf_op jit(solution)/shard_map/ppermute | solution.py:356
  57.2 1.4 %collective-permute-done.8.refs_6_ = bf16[512,128]{1,0:T(8,128)(2,1)S(1)} collective-permute-done((bf16[512,128]{1,0:T(8,128)(2,1)S(1)}, bf16[512,128]{1,0:T(8,128)(2,1)S(1)}, u32[]{:S(2)}, u32[]{:S(2)}) %collective-permute-start.8) | collective-permute-done | bytes 131104 | tf_op jit(solution)/shard_map/ppermute | solution.py:354
  58.6 0.0 all-to-all-done.queries
  58.6 0.0 copy-start.3
  58.6 0.7 copy-done.3
  59.3 0.0 copy-start
  59.3 5.9 %shard_map.75 = (f32[8,144,256]{2,1,0:T(8,128)S(1)}, f32[8,8,256]{2,1,0:T(8,128)S(1)}, bf16[2,128,128]{2,1,0:T(8,128)(2,1)S(1)}) custom-call(s32[4]{0:T(128)S(1)} %copy-done.3, bf16[256,128]{1,0:T(8,128)(2,1)S(1)} %get-tuple-element.25.near_rows, bf16[4,1024,128]{2,1,0:T(8,128)(2,1)S(1)} %all-to-all-done.queries, ...), custom_call_target="tpu_custom_call" | custom-call | flops 1879048192 | bytes 4194304 | tf_op jit(solution)/shard_map/pallas_call | solution.py:369
  65.2 0.0 collective-permute-done.5.last
  65.2 0.0 copy-done.4
  65.2 2.5 %shard_map.76 = bf16[8,272,128]{2,1,0:T(8,128)(2,1)S(1)} custom-call(s32[4]{0:T(128)S(1)} %copy-done.4, bf16[4,1024,128]{2,1,0:T(8,128)(2,1)S(1)} %all-to-all-done.queries, bf16[512,128]{1,0:T(8,128)(2,1)S(1)} %collective-permute-done.5.last, f32[8,144,256]{2,1,0:T(8,128)S(1)} %get-tuple-element.28.sums, f32[8,8,256]{2,1,0:T(8,128)S(1)} %get-tuple-element.29.tops), custom_call_target="tpu_custom_call" | custom-call | flops 268435456 | bytes 4194304 | tf_op jit(solution)/shard_map/pallas_call | solution.py:386
  67.8 13.0 %all_to_all.15.parts = bf16[8,272,128]{2,1,0:T(8,128)(2,1)S(1)} all-to-all(bf16[8,272,128]{2,1,0:T(8,128)(2,1)S(1)} %shard_map.76), channel_id=1, replica_groups=mesh['k'=8,'e'=2,'x'=4,'y'=4,'c'=2] {'e','x'}, dimensions={0} | all-to-all | bytes 1114112 | tf_op jit(solution)/shard_map/all_to_all | solution.py:395
  80.8 0.0 copy-done
  80.8 1.4 %shard_map.77 = (bf16[4,128,512]{2,1,0:T(8,128)(2,1)S(1)}, f32[4,128,512]{2,1,0:T(8,128)S(1)}) custom-call(s32[4]{0:T(128)S(1)} %copy-done.4, bf16[8,272,128]{2,1,0:T(8,128)(2,1)S(1)} %all_to_all.15.parts, bf16[2,128,128]{2,1,0:T(8,128)(2,1)S(1)} %get-tuple-element.30.near, bf16[512,4096]{1,0:T(8,128)(2,1)S(1)} %copy-done), custom_call_target="tpu_custom_call" | custom-call | flops 536870912 | bytes 5242880 | tf_op jit(solution)/shard_map/pallas_call | solution.py:397
  82.2 8.9 %collective-permute-start.9 = (bf16[4,128,512]{2,1,0:T(8,128)(2,1)S(1)}, bf16[4,128,512]{2,1,0:T(8,128)(2,1)S(1)}, u32[]{:S(2)}, u32[]{:S(2)}) collective-permute-start(bf16[4,128,512]{2,1,0:T(8,128)(2,1)S(1)} %get-tuple-element.32), channel_id=1, source_target_pairs={{0,1},{1,0},{2,3},{3,2},{4,5},{5,4},{6,7},{7,6},{8,9},{9,8},{10,11... | collective-permute-start | bytes 1572872 | tf_op jit(solution)/shard_map/ppermute | solution.py:408
  91.1 1.5 %collective-permute-done.9.received = bf16[4,128,512]{2,1,0:T(8,128)(2,1)S(1)} collective-permute-done((bf16[4,128,512]{2,1,0:T(8,128)(2,1)S(1)}, bf16[4,128,512]{2,1,0:T(8,128)(2,1)S(1)}, u32[]{:S(2)}, u32[]{:S(2)}) %collective-permute-start.9) | collective-permute-done | bytes 524320 | tf_op jit(solution)/shard_map/ppermute | solution.py:408
  92.6 0.1 shard_map.78
  92.7 12.6 %all_to_all.16.shares = bf16[4,128,512]{2,1,0:T(8,128)(2,1)S(1)} all-to-all(bf16[4,128,512]{2,1,0:T(8,128)(2,1)S(1)} %shard_map.78), channel_id=1, replica_groups=mesh['k'=8,'e'=2,'x'=4,'y'=4,'c'=2] {'y'}, dimensions={0} | all-to-all | bytes 1048576 | tf_op jit(solution)/shard_map/all_to_all | solution.py:415
  105.3 0.8 shard_map.79
Async XLA Ops:
  1.7 21.5 %collective-permute-start = (bf16[512,128]{1,0:T(8,128)(2,1)}, bf16[512,128]{1,0:T(8,128)(2,1)S(1)}, u32[]{:S(2)}, u32[]{:S(2)}) collective-permute-start(bf16[512,128]{1,0:T(8,128)(2,1)} %get-tuple-element.19.own_rows), channel_id=1, source_target_pairs={{0,32},{32,0},{1,33},{33,1},{2,34},{34,2},{3,35},{35,3},{4,36},{36... | collective-permute-start | bytes 393224 | tf_op jit(solution)/shard_map/ppermute | solution.py:338
  6.1 17.1 %collective-permute-start.2 = (bf16[512,128]{1,0:T(8,128)(2,1)}, bf16[512,128]{1,0:T(8,128)(2,1)S(1)}, u32[]{:S(2)}, u32[]{:S(2)}) collective-permute-start(bf16[512,128]{1,0:T(8,128)(2,1)} %get-tuple-element.27.own), channel_id=1, source_target_pairs={{0,64},{1,449},{64,128},{65,1},{128,192},{129,65},{192,256},{193,1... | collective-permute-start | bytes 393224 | tf_op jit(solution)/shard_map/ppermute | solution.py:353
  16.8 6.4 %collective-permute-start.1 = (bf16[256,128]{1,0:T(8,128)(2,1)}, bf16[256,128]{1,0:T(8,128)(2,1)S(1)}, u32[]{:S(2)}, u32[]{:S(2)}) collective-permute-start(bf16[256,128]{1,0:T(8,128)(2,1)} %get-tuple-element.21), channel_id=1, source_target_pairs={{0,32},{32,64},{64,96},{96,128},{128,160},{160,192},{192,224},{224... | collective-permute-start | bytes 196616 | tf_op jit(solution)/shard_map/ppermute | solution.py:339
  23.2 0.9 copy-start.1
  24.1 0.9 copy-start.2
  26.2 39.0 %copy-start.4 = (s32[4]{0:T(128)S(1)}, s32[4]{0:T(128)}, u32[]{:S(2)}) copy-start(s32[4]{0:T(128)} %spans.7) | copy-start | bytes 52
  26.2 32.4 %all-to-all-start = ((bf16[4,1024,128]{2,1,0:T(8,128)(2,1)}), bf16[4,1024,128]{2,1,0:T(8,128)(2,1)S(1)}, u32[]{:S(2)}, u32[]{:S(2)}) async-start(bf16[4,1024,128]{2,1,0:T(8,128)(2,1)} %get-tuple-element.24), calls=%async_computation | async-start | bytes 2097152 | tf_op jit(solution)/shard_map/all_to_all | solution.py:367
  30.3 9.0 %collective-permute-start.6 = (bf16[512,128]{1,0:T(8,128)(2,1)}, bf16[512,128]{1,0:T(8,128)(2,1)S(1)}, u32[]{:S(2)}, u32[]{:S(2)}) collective-permute-start(bf16[512,128]{1,0:T(8,128)(2,1)} %get-tuple-element.27.own), channel_id=1, source_target_pairs={{0,448},{1,65},{64,0},{65,129},{128,64},{129,193},{192,128},{193,2... | collective-permute-start | bytes 393224 | tf_op jit(solution)/shard_map/ppermute | solution.py:354
  32.2 9.8 %collective-permute-start.3 = (bf16[512,128]{1,0:T(8,128)(2,1)S(1)}, bf16[512,128]{1,0:T(8,128)(2,1)S(1)}, u32[]{:S(2)}, u32[]{:S(2)}) collective-permute-start(bf16[512,128]{1,0:T(8,128)(2,1)S(1)} %collective-permute-done.2.after.refs_1_), channel_id=1, source_target_pairs={{0,64},{1,449},{64,128},{65,1},{128,192},{129,65},{192,256},{193,1... | collective-permute-start | bytes 393224 | tf_op jit(solution)/shard_map/ppermute | solution.py:353
  39.3 9.1 %collective-permute-start.7 = (bf16[512,128]{1,0:T(8,128)(2,1)S(1)}, bf16[512,128]{1,0:T(8,128)(2,1)S(1)}, u32[]{:S(2)}, u32[]{:S(2)}) collective-permute-start(bf16[512,128]{1,0:T(8,128)(2,1)S(1)} %collective-permute-done.6.refs_2_), channel_id=1, source_target_pairs={{0,448},{1,65},{64,0},{65,129},{128,64},{129,193},{192,128},{193,2... | collective-permute-start | bytes 393224 | tf_op jit(solution)/shard_map/ppermute | solution.py:354
  42.0 11.0 %collective-permute-start.4 = (bf16[512,128]{1,0:T(8,128)(2,1)S(1)}, bf16[512,128]{1,0:T(8,128)(2,1)S(1)}, u32[]{:S(2)}, u32[]{:S(2)}) collective-permute-start(bf16[512,128]{1,0:T(8,128)(2,1)S(1)} %collective-permute-done.3.refs_3_), channel_id=1, source_target_pairs={{0,64},{1,449},{64,128},{65,1},{128,192},{129,65},{192,256},{193,1... | collective-permute-start | bytes 393224 | tf_op jit(solution)/shard_map/ppermute | solution.py:353
  48.4 10.2 %collective-permute-start.8 = (bf16[512,128]{1,0:T(8,128)(2,1)S(1)}, bf16[512,128]{1,0:T(8,128)(2,1)S(1)}, u32[]{:S(2)}, u32[]{:S(2)}) collective-permute-start(bf16[512,128]{1,0:T(8,128)(2,1)S(1)} %collective-permute-done.7.refs_4_), channel_id=1, source_target_pairs={{0,448},{1,65},{64,0},{65,129},{128,64},{129,193},{192,128},{193,2... | collective-permute-start | bytes 393224 | tf_op jit(solution)/shard_map/ppermute | solution.py:354
  53.1 12.2 %collective-permute-start.5 = (bf16[512,128]{1,0:T(8,128)(2,1)S(1)}, bf16[512,128]{1,0:T(8,128)(2,1)S(1)}, u32[]{:S(2)}, u32[]{:S(2)}) collective-permute-start(bf16[512,128]{1,0:T(8,128)(2,1)S(1)} %collective-permute-done.4.refs_5_), channel_id=1, source_target_pairs={{0,64},{1,449},{64,128},{65,1},{128,192},{129,65},{192,256},{193,1... | collective-permute-start | bytes 393224 | tf_op jit(solution)/shard_map/ppermute | solution.py:356
  58.6 0.7 copy-start.3
  59.3 21.5 %copy-start = (bf16[512,4096]{1,0:T(8,128)(2,1)S(1)}, bf16[512,4096]{1,0:T(8,128)(2,1)}, u32[]{:S(2)}) copy-start(bf16[512,4096]{1,0:T(8,128)(2,1)} %weight.1) | copy-start | bytes 12582916
  82.2 10.4 %collective-permute-start.9 = (bf16[4,128,512]{2,1,0:T(8,128)(2,1)S(1)}, bf16[4,128,512]{2,1,0:T(8,128)(2,1)S(1)}, u32[]{:S(2)}, u32[]{:S(2)}) collective-permute-start(bf16[4,128,512]{2,1,0:T(8,128)(2,1)S(1)} %get-tuple-element.32), channel_id=1, source_target_pairs={{0,1},{1,0},{2,3},{3,2},{4,5},{5,4},{6,7},{7,6},{8,9},{9,8},{10,11... | collective-permute-start | bytes 1572872 | tf_op jit(solution)/shard_map/ppermute | solution.py:408

commit v10 on v9

--- a/solution.py
+++ b/solution.py
@@ -67,8 +67,8 @@
         own_rows[s * HD : (s + 1) * HD, :] = rows
 
 
-def spread_kernel(own_rows, other_rows, own, prior, after, sent, held, near_rows):
-    del after
+def spread_kernel(own_rows, other_rows, own, prior, after, after_too, sent, held, near_rows):
+    del after, after_too
     first = lax.axis_index("e") == 0
     mine, other = own_rows[: FAR * HD, :], other_rows[: FAR * HD, :]
     lower = jnp.where(first, mine, other)
@@ -347,12 +347,13 @@
         ]
         for turn in range(2)
     ]
-    kv, one = [own], own
-    two, other_rows, prior = lax.optimization_barrier((own, other_rows, prior))
-    for _ in range(RING // 2 - 1):
+    kv, one, two = [own], own, own
+    for step in range(RING // 2 - 1):
         one = lax.ppermute(one, ("k", "c"), routes[0])
         two = lax.ppermute(two, ("k", "c"), routes[1])
         kv += [one, two]
+        if step == 0:
+            one, two, other_rows, prior = lax.optimization_barrier((one, two, other_rows, prior))
     last = lax.ppermute(one, ("k", "c"), routes[0])
     sent, kv[0], near_rows = call(
         spread_kernel,
@@ -361,9 +362,9 @@
             jax.ShapeDtypeStruct((4 * HD, HD), bf16),
             jax.ShapeDtypeStruct((2 * HD, HD), bf16),
         ],
-        [VMEM] * 4 + [ANY],
+        [VMEM] * 4 + [ANY] * 2,
         moved=2**20,
-    )(own_rows, other_rows, own, prior, kv[1])
+    )(own_rows, other_rows, own, prior, kv[1], kv[2])
     grouped = lax.all_to_all(sent, "x", 0, 0, tiled=True)
     near_blocks = 2 * (RING - 1)
     sums, tops, near = call(

time: 107 us -> 103 us (0.963)
  starting transfers between devices: 52.5 us -> 48.5 us
  blocking collectives: 25.6 us -> 24.4 us
    ppermute x1, starting transfers between devices: 8.92 us -> 6.53 us  [per_device(): received = lax.ppermute(product, 'c', [(0, 1), (1, 0)])]
    ppermute x1, starting transfers between devices: 4.37 us -> 2.65 us  [per_device(): other_rows = lax.ppermute(own_rows, 'e', [(0, 1), (1, 0)])]
    ppermute x1, starting transfers between devices: 4.14 us -> 5.84 us  [per_device(): last = lax.ppermute(one, ('k', 'c'), routes[0])]
    ppermute x3, waiting for transfers between devices: 2.97 us -> 4.65 us  [per_device(): two = lax.ppermute(two, ('k', 'c'), routes[1])]
    ppermute x3, starting transfers between devices: 22.5 us -> 21 us  [per_device(): one = lax.ppermute(one, ('k', 'c'), routes[0])]
    ppermute x3, waiting for transfers between devices: 3.51 us -> 2.12 us  [per_device(): one = lax.ppermute(one, ('k', 'c'), routes[0])]
    all_to_all x1, blocking collectives: 13 us -> 11.8 us  [per_device(): parts = lax.all_to_all(partial, ('e', 'x'), 0, 0, tiled=True)]
    unnamed x10 -> x8, local copies, waits for them, and re-layouts: 2.47 us -> 2.46 us
  transfers between devices with their start and end apart: 11 -> 11, of which waited for: 6 -> 5; matrix products, arithmetic and copies ran while one was open for 0% -> 0% of each run, Pallas kernels for 6% -> 6%
where the time goes in v10:
time: 103 us; the launch traced here: 102 us
  starting transfers between devices  48.5 us (47%)
  blocking collectives  24.4 us (24%)
  Pallas kernels  13.7 us (13%)
  waiting for transfers between devices  12.5 us (12%)
  local copies, waits for them, and re-layouts  2.46 us (2%)
    ppermute x3, starting transfers between devices, per_device(): one = lax.ppermute(one, ('k', 'c'), routes[0])  21 us
    all_to_all x1, blocking collectives, per_device(): shares = lax.all_to_all(halves, 'y', 0, 0, tiled=True)  12.6 us
    all_to_all x1, blocking collectives, per_device(): parts = lax.all_to_all(partial, ('e', 'x'), 0, 0, tiled=True)  11.8 us
    ppermute x1, starting transfers between devices, per_device(): received = lax.ppermute(product, 'c', [(0, 1), (1, 0)])  6.53 us
    pallas_call x1, Pallas kernels, per_device(): call(first_kernel, [jax.ShapeDtypeStruct((TILES, HD + STATS, TILE), f32),...  5.93 us
    ppermute x3, starting transfers between devices, per_device(): two = lax.ppermute(two, ('k', 'c'), routes[1])  5.87 us
    ppermute x1, starting transfers between devices, per_device(): last = lax.ppermute(one, ('k', 'c'), routes[0])  5.84 us
    ppermute x3, waiting for transfers between devices, per_device(): two = lax.ppermute(two, ('k', 'c'), routes[1])  4.65 us
  transfers between devices with their start and end apart: 11, of which 5 were waited for; matrix products, arithmetic and copies ran while one was open for 0% of the time, Pallas kernels for 6%

profile of v10, /device:TPU:1, one launch (start us, length us, event | category | flops | bytes accessed | tf_op | source)
XLA Modules:
  0.0 101.7 jit_solution(7881575940368998371)
XLA Ops:
  0.0 1.7 %shard_map.73 = (bf16[512,128]{1,0:T(8,128)(2,1)}, bf16[512,128]{1,0:T(8,128)(2,1)}, bf16[256,128]{1,0:T(8,128)(2,1)}) custom-call(s32[4]{0:T(128)} %spans.7, bf16[128,512]{1,0:T(8,128)(2,1)} %queries.1, bf16[128,128]{1,0:T(8,128)(2,1)} %keys.1, bf16[128,128]{1,0:T(8,128)(2,1)} %values.1, bf16[128,128]{1,0:T(8,128)(2,1)} %cache_keys.1, ...), custom_call_target="tpu_custom_call" | custom-call | bytes 1048576 | tf_op jit(solution)/shard_map/pallas_call | solution.py:322
  1.7 12.4 %collective-permute-start = (bf16[512,128]{1,0:T(8,128)(2,1)}, bf16[512,128]{1,0:T(8,128)(2,1)S(1)}, u32[]{:S(2)}, u32[]{:S(2)}) collective-permute-start(bf16[512,128]{1,0:T(8,128)(2,1)} %get-tuple-element.21.own), channel_id=1, source_target_pairs={{0,64},{1,449},{64,128},{65,1},{128,192},{129,65},{192,256},{193,1... | collective-permute-start | bytes 393224 | tf_op jit(solution)/shard_map/ppermute | solution.py:352
  14.1 1.9 %collective-permute-start.1 = (bf16[512,128]{1,0:T(8,128)(2,1)}, bf16[512,128]{1,0:T(8,128)(2,1)S(1)}, u32[]{:S(2)}, u32[]{:S(2)}) collective-permute-start(bf16[512,128]{1,0:T(8,128)(2,1)} %get-tuple-element.21.own), channel_id=1, source_target_pairs={{0,448},{1,65},{64,0},{65,129},{128,64},{129,193},{192,128},{193,2... | collective-permute-start | bytes 393224 | tf_op jit(solution)/shard_map/ppermute | solution.py:353
  16.0 2.6 %collective-permute-start.2 = (bf16[512,128]{1,0:T(8,128)(2,1)}, bf16[512,128]{1,0:T(8,128)(2,1)S(1)}, u32[]{:S(2)}, u32[]{:S(2)}) collective-permute-start(bf16[512,128]{1,0:T(8,128)(2,1)} %get-tuple-element.20.own_rows), channel_id=1, source_target_pairs={{0,32},{32,0},{1,33},{33,1},{2,34},{34,2},{3,35},{35,3},{4,36},{36... | collective-permute-start | bytes 393224 | tf_op jit(solution)/shard_map/ppermute | solution.py:338
  18.7 2.6 %collective-permute-start.3 = (bf16[256,128]{1,0:T(8,128)(2,1)}, bf16[256,128]{1,0:T(8,128)(2,1)S(1)}, u32[]{:S(2)}, u32[]{:S(2)}) collective-permute-start(bf16[256,128]{1,0:T(8,128)(2,1)} %get-tuple-element.22), channel_id=1, source_target_pairs={{0,32},{32,64},{64,96},{96,128},{128,160},{160,192},{192,224},{224... | collective-permute-start | bytes 196616 | tf_op jit(solution)/shard_map/ppermute | solution.py:339
  21.3 4.2 %collective-permute-done.3.prior = bf16[256,128]{1,0:T(8,128)(2,1)S(1)} collective-permute-done((bf16[256,128]{1,0:T(8,128)(2,1)}, bf16[256,128]{1,0:T(8,128)(2,1)S(1)}, u32[]{:S(2)}, u32[]{:S(2)}) %collective-permute-start.3) | collective-permute-done | bytes 65568 | tf_op jit(solution)/shard_map/ppermute | solution.py:339
  25.6 0.0 collective-permute-done.after.refs_1_
  25.6 0.0 collective-permute-done.1.after_too.refs_2_
  25.6 0.0 collective-permute-done.2.other_rows
  25.6 0.0 copy-start.1
  25.6 0.9 copy-done.1
  26.5 0.0 copy-start.2
  26.5 0.9 copy-done.2
  27.4 1.1 %shard_map.74 = (bf16[4,1024,128]{2,1,0:T(8,128)(2,1)}, bf16[512,128]{1,0:T(8,128)(2,1)S(1)}, bf16[256,128]{1,0:T(8,128)(2,1)S(1)}) custom-call(bf16[512,128]{1,0:T(8,128)(2,1)S(1)} %copy-done.2, bf16[512,128]{1,0:T(8,128)(2,1)S(1)} %collective-permute-done.2.other_rows, bf16[512,128]{1,0:T(8,128)(2,1)S(1)} %copy-done.1, ...), custom_call_target="tpu_custom_call" | custom-call | bytes 1048576 | tf_op jit(solution)/shard_map/pallas_call | solution.py:358
  28.5 4.0 %all-to-all-start = ((bf16[4,1024,128]{2,1,0:T(8,128)(2,1)}), bf16[4,1024,128]{2,1,0:T(8,128)(2,1)S(1)}, u32[]{:S(2)}, u32[]{:S(2)}) async-start(bf16[4,1024,128]{2,1,0:T(8,128)(2,1)} %get-tuple-element.25), calls=%async_computation | async-start | bytes 2097152 | tf_op jit(solution)/shard_map/all_to_all | solution.py:368
  32.5 4.1 %collective-permute-start.4 = (bf16[512,128]{1,0:T(8,128)(2,1)S(1)}, bf16[512,128]{1,0:T(8,128)(2,1)S(1)}, u32[]{:S(2)}, u32[]{:S(2)}) collective-permute-start(bf16[512,128]{1,0:T(8,128)(2,1)S(1)} %collective-permute-done.after.refs_1_), channel_id=1, source_target_pairs={{0,64},{1,449},{64,128},{65,1},{128,192},{129,65},{192,256},{193,1... | collective-permute-start | bytes 393224 | tf_op jit(solution)/shard_map/ppermute | solution.py:352
  36.7 2.0 %collective-permute-start.7 = (bf16[512,128]{1,0:T(8,128)(2,1)S(1)}, bf16[512,128]{1,0:T(8,128)(2,1)S(1)}, u32[]{:S(2)}, u32[]{:S(2)}) collective-permute-start(bf16[512,128]{1,0:T(8,128)(2,1)S(1)} %collective-permute-done.1.after_too.refs_2_), channel_id=1, source_target_pairs={{0,448},{1,65},{64,0},{65,129},{128,64},{129,193},{192,128},{193,2... | collective-permute-start | bytes 393224 | tf_op jit(solution)/shard_map/ppermute | solution.py:353
  38.7 2.1 %collective-permute-done.4.refs_3_ = bf16[512,128]{1,0:T(8,128)(2,1)S(1)} collective-permute-done((bf16[512,128]{1,0:T(8,128)(2,1)S(1)}, bf16[512,128]{1,0:T(8,128)(2,1)S(1)}, u32[]{:S(2)}, u32[]{:S(2)}) %collective-permute-start.4) | collective-permute-done | bytes 131104 | tf_op jit(solution)/shard_map/ppermute | solution.py:352
  40.8 4.5 %collective-permute-start.5 = (bf16[512,128]{1,0:T(8,128)(2,1)S(1)}, bf16[512,128]{1,0:T(8,128)(2,1)S(1)}, u32[]{:S(2)}, u32[]{:S(2)}) collective-permute-start(bf16[512,128]{1,0:T(8,128)(2,1)S(1)} %collective-permute-done.4.refs_3_), channel_id=1, source_target_pairs={{0,64},{1,449},{64,128},{65,1},{128,192},{129,65},{192,256},{193,1... | collective-permute-start | bytes 393224 | tf_op jit(solution)/shard_map/ppermute | solution.py:352
  45.3 1.8 %collective-permute-done.7.refs_4_ = bf16[512,128]{1,0:T(8,128)(2,1)S(1)} collective-permute-done((bf16[512,128]{1,0:T(8,128)(2,1)S(1)}, bf16[512,128]{1,0:T(8,128)(2,1)S(1)}, u32[]{:S(2)}, u32[]{:S(2)}) %collective-permute-start.7) | collective-permute-done | bytes 131104 | tf_op jit(solution)/shard_map/ppermute | solution.py:353
  47.1 1.9 %collective-permute-start.8 = (bf16[512,128]{1,0:T(8,128)(2,1)S(1)}, bf16[512,128]{1,0:T(8,128)(2,1)S(1)}, u32[]{:S(2)}, u32[]{:S(2)}) collective-permute-start(bf16[512,128]{1,0:T(8,128)(2,1)S(1)} %collective-permute-done.7.refs_4_), channel_id=1, source_target_pairs={{0,448},{1,65},{64,0},{65,129},{128,64},{129,193},{192,128},{193,2... | collective-permute-start | bytes 393224 | tf_op jit(solution)/shard_map/ppermute | solution.py:353
  49.0 0.0 collective-permute-done.5.refs_5_
  49.1 5.8 %collective-permute-start.6 = (bf16[512,128]{1,0:T(8,128)(2,1)S(1)}, bf16[512,128]{1,0:T(8,128)(2,1)S(1)}, u32[]{:S(2)}, u32[]{:S(2)}) collective-permute-start(bf16[512,128]{1,0:T(8,128)(2,1)S(1)} %collective-permute-done.5.refs_5_), channel_id=1, source_target_pairs={{0,64},{1,449},{64,128},{65,1},{128,192},{129,65},{192,256},{193,1... | collective-permute-start | bytes 393224 | tf_op jit(solution)/shard_map/ppermute | solution.py:357
  54.9 2.8 %collective-permute-done.8.refs_6_ = bf16[512,128]{1,0:T(8,128)(2,1)S(1)} collective-permute-done((bf16[512,128]{1,0:T(8,128)(2,1)S(1)}, bf16[512,128]{1,0:T(8,128)(2,1)S(1)}, u32[]{:S(2)}, u32[]{:S(2)}) %collective-permute-start.8) | collective-permute-done | bytes 131104 | tf_op jit(solution)/shard_map/ppermute | solution.py:353
  57.8 0.0 all-to-all-done.queries
  57.8 0.0 copy-start.3
  57.8 0.7 copy-done.3
  58.4 0.0 copy-start
  58.4 5.9 %shard_map.75 = (f32[8,144,256]{2,1,0:T(8,128)S(1)}, f32[8,8,256]{2,1,0:T(8,128)S(1)}, bf16[2,128,128]{2,1,0:T(8,128)(2,1)S(1)}) custom-call(s32[4]{0:T(128)S(1)} %copy-done.3, bf16[256,128]{1,0:T(8,128)(2,1)S(1)} %get-tuple-element.27.near_rows, bf16[4,1024,128]{2,1,0:T(8,128)(2,1)S(1)} %all-to-all-done.queries, ...), custom_call_target="tpu_custom_call" | custom-call | flops 1879048192 | bytes 4194304 | tf_op jit(solution)/shard_map/pallas_call | solution.py:370
  64.4 0.0 collective-permute-done.6.last
  64.4 2.5 %shard_map.76 = bf16[8,272,128]{2,1,0:T(8,128)(2,1)S(1)} custom-call(s32[4]{0:T(128)S(1)} %copy-done.3, bf16[4,1024,128]{2,1,0:T(8,128)(2,1)S(1)} %all-to-all-done.queries, bf16[512,128]{1,0:T(8,128)(2,1)S(1)} %collective-permute-done.6.last, f32[8,144,256]{2,1,0:T(8,128)S(1)} %get-tuple-element.30.sums, f32[8,8,256]{2,1,0:T(8,128)S(1)} %get-tuple-element.31.tops), custom_call_target="tpu_custom_call" | custom-call | flops 268435456 | bytes 4194304 | tf_op jit(solution)/shard_map/pallas_call | solution.py:387
  66.9 11.8 %all_to_all.15.parts = bf16[8,272,128]{2,1,0:T(8,128)(2,1)S(1)} all-to-all(bf16[8,272,128]{2,1,0:T(8,128)(2,1)S(1)} %shard_map.76), channel_id=1, replica_groups=mesh['k'=8,'e'=2,'x'=4,'y'=4,'c'=2] {'e','x'}, dimensions={0} | all-to-all | bytes 1114112 | tf_op jit(solution)/shard_map/all_to_all | solution.py:396
  78.7 0.0 copy-done
  78.7 1.5 %shard_map.77 = (bf16[4,128,512]{2,1,0:T(8,128)(2,1)S(1)}, f32[4,128,512]{2,1,0:T(8,128)S(1)}) custom-call(s32[4]{0:T(128)S(1)} %copy-done.3, bf16[8,272,128]{2,1,0:T(8,128)(2,1)S(1)} %all_to_all.15.parts, bf16[2,128,128]{2,1,0:T(8,128)(2,1)S(1)} %get-tuple-element.32.near, bf16[512,4096]{1,0:T(8,128)(2,1)S(1)} %copy-done), custom_call_target="tpu_custom_call" | custom-call | flops 536870912 | bytes 5242880 | tf_op jit(solution)/shard_map/pallas_call | solution.py:398
  80.2 6.5 %collective-permute-start.9 = (bf16[4,128,512]{2,1,0:T(8,128)(2,1)S(1)}, bf16[4,128,512]{2,1,0:T(8,128)(2,1)S(1)}, u32[]{:S(2)}, u32[]{:S(2)}) collective-permute-start(bf16[4,128,512]{2,1,0:T(8,128)(2,1)S(1)} %get-tuple-element.34), channel_id=1, source_target_pairs={{0,1},{1,0},{2,3},{3,2},{4,5},{5,4},{6,7},{7,6},{8,9},{9,8},{10,11... | collective-permute-start | bytes 1572872 | tf_op jit(solution)/shard_map/ppermute | solution.py:409
  86.7 1.5 %collective-permute-done.9.received = bf16[4,128,512]{2,1,0:T(8,128)(2,1)S(1)} collective-permute-done((bf16[4,128,512]{2,1,0:T(8,128)(2,1)S(1)}, bf16[4,128,512]{2,1,0:T(8,128)(2,1)S(1)}, u32[]{:S(2)}, u32[]{:S(2)}) %collective-permute-start.9) | collective-permute-done | bytes 524320 | tf_op jit(solution)/shard_map/ppermute | solution.py:409
  88.2 0.1 shard_map.78
  88.3 12.6 %all_to_all.16.shares = bf16[4,128,512]{2,1,0:T(8,128)(2,1)S(1)} all-to-all(bf16[4,128,512]{2,1,0:T(8,128)(2,1)S(1)} %shard_map.78), channel_id=1, replica_groups=mesh['k'=8,'e'=2,'x'=4,'y'=4,'c'=2] {'y'}, dimensions={0} | all-to-all | bytes 1048576 | tf_op jit(solution)/shard_map/all_to_all | solution.py:416
  100.9 0.8 shard_map.79
Async XLA Ops:
  1.7 23.9 %collective-permute-start = (bf16[512,128]{1,0:T(8,128)(2,1)}, bf16[512,128]{1,0:T(8,128)(2,1)S(1)}, u32[]{:S(2)}, u32[]{:S(2)}) collective-permute-start(bf16[512,128]{1,0:T(8,128)(2,1)} %get-tuple-element.21.own), channel_id=1, source_target_pairs={{0,64},{1,449},{64,128},{65,1},{128,192},{129,65},{192,256},{193,1... | collective-permute-start | bytes 393224 | tf_op jit(solution)/shard_map/ppermute | solution.py:352
  14.1 11.5 %collective-permute-start.1 = (bf16[512,128]{1,0:T(8,128)(2,1)}, bf16[512,128]{1,0:T(8,128)(2,1)S(1)}, u32[]{:S(2)}, u32[]{:S(2)}) collective-permute-start(bf16[512,128]{1,0:T(8,128)(2,1)} %get-tuple-element.21.own), channel_id=1, source_target_pairs={{0,448},{1,65},{64,0},{65,129},{128,64},{129,193},{192,128},{193,2... | collective-permute-start | bytes 393224 | tf_op jit(solution)/shard_map/ppermute | solution.py:353
  16.0 9.5 %collective-permute-start.2 = (bf16[512,128]{1,0:T(8,128)(2,1)}, bf16[512,128]{1,0:T(8,128)(2,1)S(1)}, u32[]{:S(2)}, u32[]{:S(2)}) collective-permute-start(bf16[512,128]{1,0:T(8,128)(2,1)} %get-tuple-element.20.own_rows), channel_id=1, source_target_pairs={{0,32},{32,0},{1,33},{33,1},{2,34},{34,2},{3,35},{35,3},{4,36},{36... | collective-permute-start | bytes 393224 | tf_op jit(solution)/shard_map/ppermute | solution.py:338
  18.7 6.9 %collective-permute-start.3 = (bf16[256,128]{1,0:T(8,128)(2,1)}, bf16[256,128]{1,0:T(8,128)(2,1)S(1)}, u32[]{:S(2)}, u32[]{:S(2)}) collective-permute-start(bf16[256,128]{1,0:T(8,128)(2,1)} %get-tuple-element.22), channel_id=1, source_target_pairs={{0,32},{32,64},{64,96},{96,128},{128,160},{160,192},{192,224},{224... | collective-permute-start | bytes 196616 | tf_op jit(solution)/shard_map/ppermute | solution.py:339
  25.6 0.9 copy-start.1
  26.5 0.9 copy-start.2
  28.5 29.2 %all-to-all-start = ((bf16[4,1024,128]{2,1,0:T(8,128)(2,1)}), bf16[4,1024,128]{2,1,0:T(8,128)(2,1)S(1)}, u32[]{:S(2)}, u32[]{:S(2)}) async-start(bf16[4,1024,128]{2,1,0:T(8,128)(2,1)} %get-tuple-element.25), calls=%async_computation | async-start | bytes 2097152 | tf_op jit(solution)/shard_map/all_to_all | solution.py:368
  32.5 8.3 %collective-permute-start.4 = (bf16[512,128]{1,0:T(8,128)(2,1)S(1)}, bf16[512,128]{1,0:T(8,128)(2,1)S(1)}, u32[]{:S(2)}, u32[]{:S(2)}) collective-permute-start(bf16[512,128]{1,0:T(8,128)(2,1)S(1)} %collective-permute-done.after.refs_1_), channel_id=1, source_target_pairs={{0,64},{1,449},{64,128},{65,1},{128,192},{129,65},{192,256},{193,1... | collective-permute-start | bytes 393224 | tf_op jit(solution)/shard_map/ppermute | solution.py:352
  36.7 10.4 %collective-permute-start.7 = (bf16[512,128]{1,0:T(8,128)(2,1)S(1)}, bf16[512,128]{1,0:T(8,128)(2,1)S(1)}, u32[]{:S(2)}, u32[]{:S(2)}) collective-permute-start(bf16[512,128]{1,0:T(8,128)(2,1)S(1)} %collective-permute-done.1.after_too.refs_2_), channel_id=1, source_target_pairs={{0,448},{1,65},{64,0},{65,129},{128,64},{129,193},{192,128},{193,2... | collective-permute-start | bytes 393224 | tf_op jit(solution)/shard_map/ppermute | solution.py:353
  40.8 8.2 %collective-permute-start.5 = (bf16[512,128]{1,0:T(8,128)(2,1)S(1)}, bf16[512,128]{1,0:T(8,128)(2,1)S(1)}, u32[]{:S(2)}, u32[]{:S(2)}) collective-permute-start(bf16[512,128]{1,0:T(8,128)(2,1)S(1)} %collective-permute-done.4.refs_3_), channel_id=1, source_target_pairs={{0,64},{1,449},{64,128},{65,1},{128,192},{129,65},{192,256},{193,1... | collective-permute-start | bytes 393224 | tf_op jit(solution)/shard_map/ppermute | solution.py:352
  47.1 10.6 %collective-permute-start.8 = (bf16[512,128]{1,0:T(8,128)(2,1)S(1)}, bf16[512,128]{1,0:T(8,128)(2,1)S(1)}, u32[]{:S(2)}, u32[]{:S(2)}) collective-permute-start(bf16[512,128]{1,0:T(8,128)(2,1)S(1)} %collective-permute-done.7.refs_4_), channel_id=1, source_target_pairs={{0,448},{1,65},{64,0},{65,129},{128,64},{129,193},{192,128},{193,2... | collective-permute-start | bytes 393224 | tf_op jit(solution)/shard_map/ppermute | solution.py:353
  49.1 15.3 %collective-permute-start.6 = (bf16[512,128]{1,0:T(8,128)(2,1)S(1)}, bf16[512,128]{1,0:T(8,128)(2,1)S(1)}, u32[]{:S(2)}, u32[]{:S(2)}) collective-permute-start(bf16[512,128]{1,0:T(8,128)(2,1)S(1)} %collective-permute-done.5.refs_5_), channel_id=1, source_target_pairs={{0,64},{1,449},{64,128},{65,1},{128,192},{129,65},{192,256},{193,1... | collective-permute-start | bytes 393224 | tf_op jit(solution)/shard_map/ppermute | solution.py:357
  57.8 0.7 copy-start.3
  58.4 20.3 %copy-start = (bf16[512,4096]{1,0:T(8,128)(2,1)S(1)}, bf16[512,4096]{1,0:T(8,128)(2,1)}, u32[]{:S(2)}) copy-start(bf16[512,4096]{1,0:T(8,128)(2,1)} %weight.1) | copy-start | bytes 12582916
  80.2 8.0 %collective-permute-start.9 = (bf16[4,128,512]{2,1,0:T(8,128)(2,1)S(1)}, bf16[4,128,512]{2,1,0:T(8,128)(2,1)S(1)}, u32[]{:S(2)}, u32[]{:S(2)}) collective-permute-start(bf16[4,128,512]{2,1,0:T(8,128)(2,1)S(1)} %get-tuple-element.34), channel_id=1, source_target_pairs={{0,1},{1,0},{2,3},{3,2},{4,5},{5,4},{6,7},{7,6},{8,9},{9,8},{10,11... | collective-permute-start | bytes 1572872 | tf_op jit(solution)/shard_map/ppermute | solution.py:409

commit v11 on v10

--- a/solution.py
+++ b/solution.py
@@ -44,7 +44,7 @@
 
 
 def prepare_kernel(
-    spans, queries, keys, values, cache_keys, cache_values, own, own_rows, handed, heads, kinds, sems
+    spans, queries, keys, values, cache_keys, cache_values, own, own_rows, handed, joint, heads, kinds, sems
 ):
     copies = [
         pltpu.make_async_copy(spans, kinds, sems.at[0]),
@@ -65,21 +65,23 @@
     for s in range(GROUP):
         rows = heads[:, pl.ds(pl.multiple_of(order[s] * HD, HD), HD)]
         own_rows[s * HD : (s + 1) * HD, :] = rows
-
-
-def spread_kernel(own_rows, other_rows, own, prior, after, after_too, sent, held, near_rows):
+        joint[(GROUP + s) * HD : (GROUP + s + 1) * HD, :] = rows
+    joint[: GROUP * HD, :] = own[...]
+
+
+def spread_kernel(joint, other_rows, prior, after, after_too, sent, held, near_rows):
     del after, after_too
     first = lax.axis_index("e") == 0
-    mine, other = own_rows[: FAR * HD, :], other_rows[: FAR * HD, :]
+    mine, other = joint[4 * HD : (4 + FAR) * HD, :], other_rows[: FAR * HD, :]
     lower = jnp.where(first, mine, other)
     upper = jnp.where(first, other, mine)
     for j in range(4):
         sent[j, : 2 * HD, :] = lower
         sent[j, 2 * HD : 4 * HD, :] = upper
-        sent[j, 4 * HD : 6 * HD, :] = own[2 * HD :, :]
+        sent[j, 4 * HD : 6 * HD, :] = joint[2 * HD : 4 * HD, :]
         sent[j, 6 * HD :, :] = prior[...]
-    held[...] = own[...]
-    near_rows[...] = own_rows[FAR * HD :, :]
+    held[...] = joint[: 4 * HD, :]
+    near_rows[...] = joint[(4 + FAR) * HD :, :]
 
 
 def query_rows(gathered, slot, first):
@@ -319,12 +321,13 @@
 
 def per_device(queries, keys, values, cache_keys, cache_values, spans, out_weight):
     bf16, f32 = jnp.bfloat16, jnp.float32
-    own, own_rows, handed = call(
+    own, own_rows, handed, joint = call(
         prepare_kernel,
         [
             jax.ShapeDtypeStruct((4 * HD, HD), bf16),
             jax.ShapeDtypeStruct((GROUP * HD, HD), bf16),
             jax.ShapeDtypeStruct((2 * HD, HD), bf16),
+            jax.ShapeDtypeStruct((2 * GROUP * HD, HD), bf16),
         ],
         [ANY] * 6,
         [
@@ -362,9 +365,9 @@
             jax.ShapeDtypeStruct((4 * HD, HD), bf16),
             jax.ShapeDtypeStruct((2 * HD, HD), bf16),
         ],
-        [VMEM] * 4 + [ANY] * 2,
+        [VMEM] * 3 + [ANY] * 2,
         moved=2**20,
-    )(own_rows, other_rows, own, prior, kv[1], kv[2])
+    )(joint, other_rows, prior, kv[1], kv[2])
     grouped = lax.all_to_all(sent, "x", 0, 0, tiled=True)
     near_blocks = 2 * (RING - 1)
     sums, tops, near = call(

time: 103 us -> 102 us (level)
    unnamed x8 -> x6, local copies, waits for them, and re-layouts: 2.46 us -> 1.6 us
where the time goes in v11:
time: 102 us; the launch traced here: 101 us
  starting transfers between devices  48.5 us (48%)
  blocking collectives  24.4 us (24%)
  Pallas kernels  13.8 us (14%)
  waiting for transfers between devices  12.5 us (12%)
  local copies, waits for them, and re-layouts  1.6 us (2%)
    ppermute x3, starting transfers between devices, per_device(): one = lax.ppermute(one, ('k', 'c'), routes[0])  21 us
    all_to_all x1, blocking collectives, per_device(): shares = lax.all_to_all(halves, 'y', 0, 0, tiled=True)  12.6 us
    all_to_all x1, blocking collectives, per_device(): parts = lax.all_to_all(partial, ('e', 'x'), 0, 0, tiled=True)  11.8 us
    ppermute x1, starting transfers between devices, per_device(): received = lax.ppermute(product, 'c', [(0, 1), (1, 0)])  6.53 us
    pallas_call x1, Pallas kernels, per_device(): call(first_kernel, [jax.ShapeDtypeStruct((TILES, HD + STATS, TILE), f32),...  5.93 us
    ppermute x3, starting transfers between devices, per_device(): two = lax.ppermute(two, ('k', 'c'), routes[1])  5.87 us
    ppermute x1, starting transfers between devices, per_device(): last = lax.ppermute(one, ('k', 'c'), routes[0])  5.84 us
    ppermute x3, waiting for transfers between devices, per_device(): two = lax.ppermute(two, ('k', 'c'), routes[1])  4.65 us
  transfers between devices with their start and end apart: 11, of which 5 were waited for; matrix products, arithmetic and copies ran while one was open for 0% of the time, Pallas kernels for 6%

profile of v11, /device:TPU:1, one launch (start us, length us, event | category | flops | bytes accessed | tf_op | source)
XLA Modules:
  0.0 101.0 jit_solution(568810833601846044)
XLA Ops:
  0.0 1.8 %shard_map.73 = (bf16[512,128]{1,0:T(8,128)(2,1)}, bf16[512,128]{1,0:T(8,128)(2,1)}, bf16[256,128]{1,0:T(8,128)(2,1)}, bf16[1024,128]{1,0:T(8,128)(2,1)}) custom-call(s32[4]{0:T(128)} %spans.7, bf16[128,512]{1,0:T(8,128)(2,1)} %queries.1, bf16[128,128]{1,0:T(8,128)(2,1)} %keys.1, bf16[128,128]{1,0:T(8,128)(2,1)} %values.1, bf16[128,128]{1,0:T(8,128)(2,1)} %cache_keys.1, ...), custom_call_target="tpu_custom_call" | custom-call | bytes 1048576 | tf_op jit(solution)/shard_map/pallas_call | solution.py:324
  1.8 12.4 %collective-permute-start = (bf16[512,128]{1,0:T(8,128)(2,1)}, bf16[512,128]{1,0:T(8,128)(2,1)S(1)}, u32[]{:S(2)}, u32[]{:S(2)}) collective-permute-start(bf16[512,128]{1,0:T(8,128)(2,1)} %get-tuple-element.22), channel_id=1, source_target_pairs={{0,64},{1,449},{64,128},{65,1},{128,192},{129,65},{192,256},{193,1... | collective-permute-start | bytes 393224 | tf_op jit(solution)/shard_map/ppermute | solution.py:355
  14.2 1.9 %collective-permute-start.1 = (bf16[512,128]{1,0:T(8,128)(2,1)}, bf16[512,128]{1,0:T(8,128)(2,1)S(1)}, u32[]{:S(2)}, u32[]{:S(2)}) collective-permute-start(bf16[512,128]{1,0:T(8,128)(2,1)} %get-tuple-element.22), channel_id=1, source_target_pairs={{0,448},{1,65},{64,0},{65,129},{128,64},{129,193},{192,128},{193,2... | collective-permute-start | bytes 393224 | tf_op jit(solution)/shard_map/ppermute | solution.py:356
  16.2 2.6 %collective-permute-start.2 = (bf16[512,128]{1,0:T(8,128)(2,1)}, bf16[512,128]{1,0:T(8,128)(2,1)S(1)}, u32[]{:S(2)}, u32[]{:S(2)}) collective-permute-start(bf16[512,128]{1,0:T(8,128)(2,1)} %get-tuple-element.23), channel_id=1, source_target_pairs={{0,32},{32,0},{1,33},{33,1},{2,34},{34,2},{3,35},{35,3},{4,36},{36... | collective-permute-start | bytes 393224 | tf_op jit(solution)/shard_map/ppermute | solution.py:341
  18.8 2.6 %collective-permute-start.3 = (bf16[256,128]{1,0:T(8,128)(2,1)}, bf16[256,128]{1,0:T(8,128)(2,1)S(1)}, u32[]{:S(2)}, u32[]{:S(2)}) collective-permute-start(bf16[256,128]{1,0:T(8,128)(2,1)} %get-tuple-element.24), channel_id=1, source_target_pairs={{0,32},{32,64},{64,96},{96,128},{128,160},{160,192},{192,224},{224... | collective-permute-start | bytes 196616 | tf_op jit(solution)/shard_map/ppermute | solution.py:342
  21.5 4.2 %collective-permute-done.3.prior = bf16[256,128]{1,0:T(8,128)(2,1)S(1)} collective-permute-done((bf16[256,128]{1,0:T(8,128)(2,1)}, bf16[256,128]{1,0:T(8,128)(2,1)S(1)}, u32[]{:S(2)}, u32[]{:S(2)}) %collective-permute-start.3) | collective-permute-done | bytes 65568 | tf_op jit(solution)/shard_map/ppermute | solution.py:342
  25.7 0.0 collective-permute-done.after.refs_1_
  25.7 0.0 collective-permute-done.1.after_too.refs_2_
  25.7 0.0 collective-permute-done.2.other_rows
  25.7 0.0 copy-start.1
  25.7 0.9 copy-done.1
  26.7 1.1 %shard_map.74 = (bf16[4,1024,128]{2,1,0:T(8,128)(2,1)}, bf16[512,128]{1,0:T(8,128)(2,1)S(1)}, bf16[256,128]{1,0:T(8,128)(2,1)S(1)}) custom-call(bf16[1024,128]{1,0:T(8,128)(2,1)S(1)} %copy-done.1, bf16[512,128]{1,0:T(8,128)(2,1)S(1)} %collective-permute-done.2.other_rows, bf16[256,128]{1,0:T(8,128)(2,1)S(1)} %collective-permute-done.3.prior, ...), custom_call_target="tpu_custom_call" | custom-call | bytes 1048576 | tf_op jit(solution)/shard_map/pallas_call | solution.py:361
  27.8 4.0 %all-to-all-start = ((bf16[4,1024,128]{2,1,0:T(8,128)(2,1)}), bf16[4,1024,128]{2,1,0:T(8,128)(2,1)S(1)}, u32[]{:S(2)}, u32[]{:S(2)}) async-start(bf16[4,1024,128]{2,1,0:T(8,128)(2,1)} %get-tuple-element.27), calls=%async_computation | async-start | bytes 2097152 | tf_op jit(solution)/shard_map/all_to_all | solution.py:371
  31.8 4.1 %collective-permute-start.4 = (bf16[512,128]{1,0:T(8,128)(2,1)S(1)}, bf16[512,128]{1,0:T(8,128)(2,1)S(1)}, u32[]{:S(2)}, u32[]{:S(2)}) collective-permute-start(bf16[512,128]{1,0:T(8,128)(2,1)S(1)} %collective-permute-done.after.refs_1_), channel_id=1, source_target_pairs={{0,64},{1,449},{64,128},{65,1},{128,192},{129,65},{192,256},{193,1... | collective-permute-start | bytes 393224 | tf_op jit(solution)/shard_map/ppermute | solution.py:355
  36.0 2.0 %collective-permute-start.7 = (bf16[512,128]{1,0:T(8,128)(2,1)S(1)}, bf16[512,128]{1,0:T(8,128)(2,1)S(1)}, u32[]{:S(2)}, u32[]{:S(2)}) collective-permute-start(bf16[512,128]{1,0:T(8,128)(2,1)S(1)} %collective-permute-done.1.after_too.refs_2_), channel_id=1, source_target_pairs={{0,448},{1,65},{64,0},{65,129},{128,64},{129,193},{192,128},{193,2... | collective-permute-start | bytes 393224 | tf_op jit(solution)/shard_map/ppermute | solution.py:356
  38.0 2.1 %collective-permute-done.4.refs_3_ = bf16[512,128]{1,0:T(8,128)(2,1)S(1)} collective-permute-done((bf16[512,128]{1,0:T(8,128)(2,1)S(1)}, bf16[512,128]{1,0:T(8,128)(2,1)S(1)}, u32[]{:S(2)}, u32[]{:S(2)}) %collective-permute-start.4) | collective-permute-done | bytes 131104 | tf_op jit(solution)/shard_map/ppermute | solution.py:355
  40.1 4.5 %collective-permute-start.5 = (bf16[512,128]{1,0:T(8,128)(2,1)S(1)}, bf16[512,128]{1,0:T(8,128)(2,1)S(1)}, u32[]{:S(2)}, u32[]{:S(2)}) collective-permute-start(bf16[512,128]{1,0:T(8,128)(2,1)S(1)} %collective-permute-done.4.refs_3_), channel_id=1, source_target_pairs={{0,64},{1,449},{64,128},{65,1},{128,192},{129,65},{192,256},{193,1... | collective-permute-start | bytes 393224 | tf_op jit(solution)/shard_map/ppermute | solution.py:355
  44.6 1.8 %collective-permute-done.7.refs_4_ = bf16[512,128]{1,0:T(8,128)(2,1)S(1)} collective-permute-done((bf16[512,128]{1,0:T(8,128)(2,1)S(1)}, bf16[512,128]{1,0:T(8,128)(2,1)S(1)}, u32[]{:S(2)}, u32[]{:S(2)}) %collective-permute-start.7) | collective-permute-done | bytes 131104 | tf_op jit(solution)/shard_map/ppermute | solution.py:356
  46.4 1.9 %collective-permute-start.8 = (bf16[512,128]{1,0:T(8,128)(2,1)S(1)}, bf16[512,128]{1,0:T(8,128)(2,1)S(1)}, u32[]{:S(2)}, u32[]{:S(2)}) collective-permute-start(bf16[512,128]{1,0:T(8,128)(2,1)S(1)} %collective-permute-done.7.refs_4_), channel_id=1, source_target_pairs={{0,448},{1,65},{64,0},{65,129},{128,64},{129,193},{192,128},{193,2... | collective-permute-start | bytes 393224 | tf_op jit(solution)/shard_map/ppermute | solution.py:356
  48.3 0.0 collective-permute-done.5.refs_5_
  48.3 5.8 %collective-permute-start.6 = (bf16[512,128]{1,0:T(8,128)(2,1)S(1)}, bf16[512,128]{1,0:T(8,128)(2,1)S(1)}, u32[]{:S(2)}, u32[]{:S(2)}) collective-permute-start(bf16[512,128]{1,0:T(8,128)(2,1)S(1)} %collective-permute-done.5.refs_5_), channel_id=1, source_target_pairs={{0,64},{1,449},{64,128},{65,1},{128,192},{129,65},{192,256},{193,1... | collective-permute-start | bytes 393224 | tf_op jit(solution)/shard_map/ppermute | solution.py:360
  54.2 2.8 %collective-permute-done.8.refs_6_ = bf16[512,128]{1,0:T(8,128)(2,1)S(1)} collective-permute-done((bf16[512,128]{1,0:T(8,128)(2,1)S(1)}, bf16[512,128]{1,0:T(8,128)(2,1)S(1)}, u32[]{:S(2)}, u32[]{:S(2)}) %collective-permute-start.8) | collective-permute-done | bytes 131104 | tf_op jit(solution)/shard_map/ppermute | solution.py:356
  57.0 0.0 all-to-all-done.queries
  57.0 0.0 copy-start.2
  57.0 0.7 copy-done.2
  57.7 0.0 copy-start
  57.7 5.9 %shard_map.75 = (f32[8,144,256]{2,1,0:T(8,128)S(1)}, f32[8,8,256]{2,1,0:T(8,128)S(1)}, bf16[2,128,128]{2,1,0:T(8,128)(2,1)S(1)}) custom-call(s32[4]{0:T(128)S(1)} %copy-done.2, bf16[256,128]{1,0:T(8,128)(2,1)S(1)} %get-tuple-element.29.near_rows, bf16[4,1024,128]{2,1,0:T(8,128)(2,1)S(1)} %all-to-all-done.queries, ...), custom_call_target="tpu_custom_call" | custom-call | flops 1879048192 | bytes 4194304 | tf_op jit(solution)/shard_map/pallas_call | solution.py:373
  63.6 0.0 collective-permute-done.6.last
  63.6 2.5 %shard_map.76 = bf16[8,272,128]{2,1,0:T(8,128)(2,1)S(1)} custom-call(s32[4]{0:T(128)S(1)} %copy-done.2, bf16[4,1024,128]{2,1,0:T(8,128)(2,1)S(1)} %all-to-all-done.queries, bf16[512,128]{1,0:T(8,128)(2,1)S(1)} %collective-permute-done.6.last, f32[8,144,256]{2,1,0:T(8,128)S(1)} %get-tuple-element.32.sums, f32[8,8,256]{2,1,0:T(8,128)S(1)} %get-tuple-element.33.tops), custom_call_target="tpu_custom_call" | custom-call | flops 268435456 | bytes 4194304 | tf_op jit(solution)/shard_map/pallas_call | solution.py:390
  66.2 11.8 %all_to_all.15.parts = bf16[8,272,128]{2,1,0:T(8,128)(2,1)S(1)} all-to-all(bf16[8,272,128]{2,1,0:T(8,128)(2,1)S(1)} %shard_map.76), channel_id=1, replica_groups=mesh['k'=8,'e'=2,'x'=4,'y'=4,'c'=2] {'e','x'}, dimensions={0} | all-to-all | bytes 1114112 | tf_op jit(solution)/shard_map/all_to_all | solution.py:399
  78.0 0.0 copy-done
  78.0 1.5 %shard_map.77 = (bf16[4,128,512]{2,1,0:T(8,128)(2,1)S(1)}, f32[4,128,512]{2,1,0:T(8,128)S(1)}) custom-call(s32[4]{0:T(128)S(1)} %copy-done.2, bf16[8,272,128]{2,1,0:T(8,128)(2,1)S(1)} %all_to_all.15.parts, bf16[2,128,128]{2,1,0:T(8,128)(2,1)S(1)} %get-tuple-element.34.near, bf16[512,4096]{1,0:T(8,128)(2,1)S(1)} %copy-done), custom_call_target="tpu_custom_call" | custom-call | flops 536870912 | bytes 5242880 | tf_op jit(solution)/shard_map/pallas_call | solution.py:401
  79.4 6.5 %collective-permute-start.9 = (bf16[4,128,512]{2,1,0:T(8,128)(2,1)S(1)}, bf16[4,128,512]{2,1,0:T(8,128)(2,1)S(1)}, u32[]{:S(2)}, u32[]{:S(2)}) collective-permute-start(bf16[4,128,512]{2,1,0:T(8,128)(2,1)S(1)} %get-tuple-element.36), channel_id=1, source_target_pairs={{0,1},{1,0},{2,3},{3,2},{4,5},{5,4},{6,7},{7,6},{8,9},{9,8},{10,11... | collective-permute-start | bytes 1572872 | tf_op jit(solution)/shard_map/ppermute | solution.py:412
  86.0 1.5 %collective-permute-done.9.received = bf16[4,128,512]{2,1,0:T(8,128)(2,1)S(1)} collective-permute-done((bf16[4,128,512]{2,1,0:T(8,128)(2,1)S(1)}, bf16[4,128,512]{2,1,0:T(8,128)(2,1)S(1)}, u32[]{:S(2)}, u32[]{:S(2)}) %collective-permute-start.9) | collective-permute-done | bytes 524320 | tf_op jit(solution)/shard_map/ppermute | solution.py:412
  87.5 0.1 shard_map.78
  87.6 12.6 %all_to_all.16.shares = bf16[4,128,512]{2,1,0:T(8,128)(2,1)S(1)} all-to-all(bf16[4,128,512]{2,1,0:T(8,128)(2,1)S(1)} %shard_map.78), channel_id=1, replica_groups=mesh['k'=8,'e'=2,'x'=4,'y'=4,'c'=2] {'y'}, dimensions={0} | all-to-all | bytes 1048576 | tf_op jit(solution)/shard_map/all_to_all | solution.py:419
  100.2 0.8 shard_map.79
Async XLA Ops:
  1.8 23.9 %collective-permute-start = (bf16[512,128]{1,0:T(8,128)(2,1)}, bf16[512,128]{1,0:T(8,128)(2,1)S(1)}, u32[]{:S(2)}, u32[]{:S(2)}) collective-permute-start(bf16[512,128]{1,0:T(8,128)(2,1)} %get-tuple-element.22), channel_id=1, source_target_pairs={{0,64},{1,449},{64,128},{65,1},{128,192},{129,65},{192,256},{193,1... | collective-permute-start | bytes 393224 | tf_op jit(solution)/shard_map/ppermute | solution.py:355
  14.2 11.5 %collective-permute-start.1 = (bf16[512,128]{1,0:T(8,128)(2,1)}, bf16[512,128]{1,0:T(8,128)(2,1)S(1)}, u32[]{:S(2)}, u32[]{:S(2)}) collective-permute-start(bf16[512,128]{1,0:T(8,128)(2,1)} %get-tuple-element.22), channel_id=1, source_target_pairs={{0,448},{1,65},{64,0},{65,129},{128,64},{129,193},{192,128},{193,2... | collective-permute-start | bytes 393224 | tf_op jit(solution)/shard_map/ppermute | solution.py:356
  16.2 9.5 %collective-permute-start.2 = (bf16[512,128]{1,0:T(8,128)(2,1)}, bf16[512,128]{1,0:T(8,128)(2,1)S(1)}, u32[]{:S(2)}, u32[]{:S(2)}) collective-permute-start(bf16[512,128]{1,0:T(8,128)(2,1)} %get-tuple-element.23), channel_id=1, source_target_pairs={{0,32},{32,0},{1,33},{33,1},{2,34},{34,2},{3,35},{35,3},{4,36},{36... | collective-permute-start | bytes 393224 | tf_op jit(solution)/shard_map/ppermute | solution.py:341
  18.8 6.9 %collective-permute-start.3 = (bf16[256,128]{1,0:T(8,128)(2,1)}, bf16[256,128]{1,0:T(8,128)(2,1)S(1)}, u32[]{:S(2)}, u32[]{:S(2)}) collective-permute-start(bf16[256,128]{1,0:T(8,128)(2,1)} %get-tuple-element.24), channel_id=1, source_target_pairs={{0,32},{32,64},{64,96},{96,128},{128,160},{160,192},{192,224},{224... | collective-permute-start | bytes 196616 | tf_op jit(solution)/shard_map/ppermute | solution.py:342
  25.7 1.0 copy-start.1
  27.8 29.2 %all-to-all-start = ((bf16[4,1024,128]{2,1,0:T(8,128)(2,1)}), bf16[4,1024,128]{2,1,0:T(8,128)(2,1)S(1)}, u32[]{:S(2)}, u32[]{:S(2)}) async-start(bf16[4,1024,128]{2,1,0:T(8,128)(2,1)} %get-tuple-element.27), calls=%async_computation | async-start | bytes 2097152 | tf_op jit(solution)/shard_map/all_to_all | solution.py:371
  31.8 8.3 %collective-permute-start.4 = (bf16[512,128]{1,0:T(8,128)(2,1)S(1)}, bf16[512,128]{1,0:T(8,128)(2,1)S(1)}, u32[]{:S(2)}, u32[]{:S(2)}) collective-permute-start(bf16[512,128]{1,0:T(8,128)(2,1)S(1)} %collective-permute-done.after.refs_1_), channel_id=1, source_target_pairs={{0,64},{1,449},{64,128},{65,1},{128,192},{129,65},{192,256},{193,1... | collective-permute-start | bytes 393224 | tf_op jit(solution)/shard_map/ppermute | solution.py:355
  36.0 10.4 %collective-permute-start.7 = (bf16[512,128]{1,0:T(8,128)(2,1)S(1)}, bf16[512,128]{1,0:T(8,128)(2,1)S(1)}, u32[]{:S(2)}, u32[]{:S(2)}) collective-permute-start(bf16[512,128]{1,0:T(8,128)(2,1)S(1)} %collective-permute-done.1.after_too.refs_2_), channel_id=1, source_target_pairs={{0,448},{1,65},{64,0},{65,129},{128,64},{129,193},{192,128},{193,2... | collective-permute-start | bytes 393224 | tf_op jit(solution)/shard_map/ppermute | solution.py:356
  40.1 8.2 %collective-permute-start.5 = (bf16[512,128]{1,0:T(8,128)(2,1)S(1)}, bf16[512,128]{1,0:T(8,128)(2,1)S(1)}, u32[]{:S(2)}, u32[]{:S(2)}) collective-permute-start(bf16[512,128]{1,0:T(8,128)(2,1)S(1)} %collective-permute-done.4.refs_3_), channel_id=1, source_target_pairs={{0,64},{1,449},{64,128},{65,1},{128,192},{129,65},{192,256},{193,1... | collective-permute-start | bytes 393224 | tf_op jit(solution)/shard_map/ppermute | solution.py:355
  46.4 10.6 %collective-permute-start.8 = (bf16[512,128]{1,0:T(8,128)(2,1)S(1)}, bf16[512,128]{1,0:T(8,128)(2,1)S(1)}, u32[]{:S(2)}, u32[]{:S(2)}) collective-permute-start(bf16[512,128]{1,0:T(8,128)(2,1)S(1)} %collective-permute-done.7.refs_4_), channel_id=1, source_target_pairs={{0,448},{1,65},{64,0},{65,129},{128,64},{129,193},{192,128},{193,2... | collective-permute-start | bytes 393224 | tf_op jit(solution)/shard_map/ppermute | solution.py:356
  48.3 15.3 %collective-permute-start.6 = (bf16[512,128]{1,0:T(8,128)(2,1)S(1)}, bf16[512,128]{1,0:T(8,128)(2,1)S(1)}, u32[]{:S(2)}, u32[]{:S(2)}) collective-permute-start(bf16[512,128]{1,0:T(8,128)(2,1)S(1)} %collective-permute-done.5.refs_5_), channel_id=1, source_target_pairs={{0,64},{1,449},{64,128},{65,1},{128,192},{129,65},{192,256},{193,1... | collective-permute-start | bytes 393224 | tf_op jit(solution)/shard_map/ppermute | solution.py:360
  57.0 0.7 copy-start.2
  57.7 20.3 %copy-start = (bf16[512,4096]{1,0:T(8,128)(2,1)S(1)}, bf16[512,4096]{1,0:T(8,128)(2,1)}, u32[]{:S(2)}) copy-start(bf16[512,4096]{1,0:T(8,128)(2,1)} %weight.1) | copy-start | bytes 12582916
  79.4 8.1 %collective-permute-start.9 = (bf16[4,128,512]{2,1,0:T(8,128)(2,1)S(1)}, bf16[4,128,512]{2,1,0:T(8,128)(2,1)S(1)}, u32[]{:S(2)}, u32[]{:S(2)}) collective-permute-start(bf16[4,128,512]{2,1,0:T(8,128)(2,1)S(1)} %get-tuple-element.36), channel_id=1, source_target_pairs={{0,1},{1,0},{2,3},{3,2},{4,5},{5,4},{6,7},{7,6},{8,9},{9,8},{10,11... | collective-permute-start | bytes 1572872 | tf_op jit(solution)/shard_map/ppermute | solution.py:412
